TPU v7x, 32 devices: a whole 2x2x4 slice. The times are simulated.
32 devices in a mesh: frames: 8 (over z, x), tokens: 4 (over y, core).
Axes of the slice: x: 2, y: 2, z: 4, core: 2. Of those that a mesh axis runs over, the one named last changes fastest.
Arguments:
- encoder_out: bfloat16 [8, 512, 512], P('tokens', 'frames'), may hold values from -6 to 6
- encoder_weight: bfloat16 [512, 512], replicated, may hold values from -0.1875 to 0.1875
- encoder_bias: float32 [512], replicated, may hold values from -2 to 2
- predictor_out: bfloat16 [8, 24, 512], P('frames', 'tokens'), may hold values from -6 to 6
- predictor_weight: bfloat16 [512, 512], replicated, may hold values from -0.1875 to 0.1875
- predictor_bias: float32 [512], replicated, may hold values from -2 to 2
- output_weight: bfloat16 [512, 1024], replicated, may hold values from -0.5 to 0.5
- output_bias: float32 [1024], replicated, may hold values from -3 to 3
- labels: int32 [8, 24], P(None, 'tokens'), may hold values from 1 to 1023
- frame_lens: int32 [8], replicated, may hold values from 85 to 512, as said below
- token_lens: int32 [8], replicated, may hold values from 1 to 23, as said below
- loss_scale: float32 [8], replicated, may hold values from 0.5 to 1.5
Outputs:
- losses: float32 [8], P('frames')
- encoder_gradient: float32 [8, 512, 512], P('tokens', 'frames')
- predictor_gradient: float32 [8, 24, 512], P('frames', 'tokens')
- encoder_weight_gradient: float32 [512, 512], replicated
- encoder_bias_gradient: float32 [512], replicated
- predictor_weight_gradient: float32 [512, 512], replicated
- predictor_bias_gradient: float32 [512], replicated
- output_weight_gradient: float32 [512, 1024], replicated
- output_bias_gradient: float32 [1024], replicated
Inputs may be any that keep to these rules, and one draw needn't show every extreme that they name: `frame_lens`: some sequence, drawn from the seed, has all 512 frames. `token_lens`: the sequence with all 512 frames has 23 labels.
All inputs are finite; a program needn't handle non-finite values.
Results may differ from a plain program's by a relative error of at most 0.0087.
Values may be sent and summed in bfloat16 or wider, within the bound.
No kernel may reach another device: no remote copies, remote signals or barrier semaphores. Data moves between devices by JAX's collectives and lax.ppermute only.
A program may use at most 256 MiB of HBM per device.

v0:
```python
import functools

import jax
import jax.numpy as jnp
from jax import lax
from jax.experimental import pallas as pl
from jax.experimental.pallas import tpu as pltpu
from jax.sharding import PartitionSpec as P

NEG = -1e30
LOG2E = 1.4426950408889634
LN2 = 0.6931471805599453
BF16 = jnp.bfloat16
F32 = jnp.float32
GROUP = 32
SUB_UNITS = 4
ORDERS = ((0, 1), (2, 1))
SENT_TYPES = (jnp.bfloat16, jnp.bfloat16, jnp.float32)
EXACT = 16
AXES = ("frames", "tokens")


def lane_ids(rows):
    return lax.broadcasted_iota(jnp.int32, (rows, 128), 1)


def log2_add(a, b):
    return jnp.maximum(a, b) + jnp.log2(1.0 + jnp.exp2(-jnp.abs(a - b)))


def both_ways(blank_ref, label_ref, units, steps, ahead, behind, keep=None):
    def one_step(i, state):
        ahead, behind = state
        back = steps - 1 - i
        here = pl.ds(pl.multiple_of(i * units, 8), units)
        there = pl.ds(pl.multiple_of(back * units, 8), units)
        if keep is not None:
            keep[0][here, :] = ahead
            keep[1][there, :] = behind
        from_left = pltpu.roll(ahead + label_ref[here, :], 1, 0)
        to_right = pltpu.roll(behind, units - 1, 0) + label_ref[there, :]
        ahead = log2_add(ahead + blank_ref[here, :], from_left)
        behind = log2_add(behind + blank_ref[there, :], to_right)
        return ahead, behind

    return lax.fori_loop(0, steps, one_step, (ahead, behind))


def in_two_stages(count, first, second, even, odd, between=None):
    def two_blocks(n, _):
        first(2 * n + 1, odd)
        second(2 * n, even)
        first(2 * n + 2, even)
        second(2 * n + 1, odd)
        return 0

    @pl.when(count > 0)
    def _():
        first(0, even)

    if between is not None:
        between()

    @pl.when(count > 0)
    def _():
        lax.fori_loop(0, (count - 1) // 2, two_blocks, 0)

        @pl.when(count % 2 == 1)
        def _():
            second(count - 1, even)

        @pl.when(count % 2 == 0)
        def _():
            first(count - 1, odd)
            second(count - 2, even)
            second(count - 1, odd)


def packet_kernel(predictor_hbm, packets_ref, predictor_ref, packet_ref, sem):
    load = pltpu.make_async_copy(predictor_hbm, predictor_ref, sem)
    load.start()
    load.wait()
    rows, width = predictor_ref.shape
    for v in range(width // 128):
        packet_ref[v * rows : (v + 1) * rows, :] = predictor_ref[
            :, v * 128 : (v + 1) * 128
        ].astype(F32)
    packet = packet_ref[...].astype(BF16)
    for d in range(packets_ref.shape[0]):
        packets_ref[d] = packet


def unpack_rows(packet, rows_ref, place):
    blocks = rows_ref.shape[1] // 128
    count = packet.shape[0] // blocks
    packet = packet.astype(F32)
    for v in range(blocks):
        rows_ref[place : place + count, v * 128 : (v + 1) * 128] = packet[
            v * count : (v + 1) * count
        ]


def table_kernel(places, seqs_here, offset_ref, *refs):
    *label_refs, table_ref = refs
    first_seq = first_of(seqs_here, offset_ref)
    shard_units = label_refs[0].shape[2]
    units = shard_units * len(places)
    lanes = lane_ids(1)
    table = jnp.zeros((1, 128), F32)
    received = [(ref, n) for ref in label_refs for n in range(ref.shape[0])]
    for place, (ref, n) in zip(places, received):
        shard = lax.axis_index("tokens") ^ place
        for s in range(2):
            row = ref[n, pl.ds(first_seq + s, 1), :].astype(F32)
            row = jnp.concatenate([row, jnp.zeros((1, 128 - shard_units), F32)], axis=1)
            start = s * units + shard * shard_units
            table = jnp.where(
                (lanes >= start) & (lanes < start + shard_units), pltpu.roll(row, start, 1), table
            )
    table_ref[...] = table.astype(jnp.int32)


def load_kernel(*refs):
    count = (len(refs) - 2) // 2
    *loaded_refs, frame_ref, sems = refs[count:]
    loads = [
        pltpu.make_async_copy(source, target, sems.at[n])
        for n, (source, target) in enumerate(zip(refs[:count], loaded_refs))
    ]
    for load in loads:
        load.start()
    for load in loads:
        load.wait()
    encoder_ref, weight_ref, bias_ref = loaded_refs[:3]
    frame_ref[...] = (
        (
            jnp.dot(
                encoder_ref[...].reshape(-1, encoder_ref.shape[-1]),
                weight_ref[...],
                preferred_element_type=F32,
            )
            + bias_ref[...]
        )
        .astype(BF16)
        .astype(F32)
        .reshape(frame_ref.shape)
    )


def entry(row_ref, place):
    row = row_ref[...].astype(F32)
    ids = lax.broadcasted_iota(jnp.int32, row.shape, 1)
    return jnp.sum(jnp.where(ids == place, row, 0.0), axis=1, keepdims=True)


def whole_number(row_ref, place):
    return entry(row_ref, place).astype(jnp.int32)[0, 0]


def first_of(seqs_here, offset_ref):
    first_seq = lax.axis_index("tokens") * seqs_here
    return first_seq if offset_ref is None else first_seq + whole_number(offset_ref, 0)


def block_counts(lens_ref, tokens_ref, first_seq, first_frame):
    counts = []
    for s in range(2):
        inside = first_frame < whole_number(lens_ref, first_seq + s)
        units = whole_number(tokens_ref, first_seq + s)
        counts.append(jnp.where(inside, units // SUB_UNITS + 1, 0))
    return counts


def score_kernel(
    seqs_here,
    offset_ref,
    packets_ref,
    lens_ref,
    tokens_ref,
    frame_ref,
    predictor_weight_ref,
    predictor_bias_ref,
    weight_ref,
    bias_ref,
    label_table_ref,
    softmax_ref,
    token_ref,
    blank_ref,
    label_ref,
    hidden_ref,
    inverse_ref,
    parts_ref,
    matrix_ref,
    even_ref,
    odd_ref,
    labels_smem,
    label_sem,
):
    label_copy = pltpu.make_async_copy(label_table_ref, labels_smem, label_sem)
    label_copy.start()
    seqs, frame_count, width = frame_ref.shape
    units = token_ref.shape[0] // seqs
    shards = lax.axis_size("tokens")
    shard_units = units // shards
    part = frame_count // 2
    steps = part + units - 1
    first_frame = lax.axis_index("frames") * frame_count
    first_seq = first_of(seqs_here, offset_ref)
    vocab = weight_ref.shape[1]
    blank_ref[...] = jnp.zeros_like(blank_ref)
    label_ref[...] = jnp.full(label_ref.shape, NEG, F32)
    for s in range(seqs):
        for k in range(shards):
            packet = packets_ref[(first_seq + s) * shards + k]
            unpack_rows(packet, token_ref, s * units + k * shard_units)
    token_ref[...] = (
        jnp.dot(token_ref[...].astype(BF16), predictor_weight_ref[...], preferred_element_type=F32)
        + predictor_bias_ref[...]
    ).astype(BF16).astype(F32)

    counts = block_counts(lens_ref, tokens_ref, first_seq, first_frame)
    blocks = counts[0] + counts[1]
    lens = [whole_number(lens_ref, first_seq + s) for s in range(2)]
    last_units = [whole_number(tokens_ref, first_seq + s) for s in range(2)]
    lanes = lane_ids(frame_count)
    part_lanes = lane_ids(part)
    times = first_frame + lax.broadcasted_iota(jnp.int32, (frame_count, 1), 0)

    def place_of(i):
        seq = jnp.where(i >= counts[0], 1, 0)
        sub = i - seq * counts[0]
        return seq, sub, seq * (units // SUB_UNITS) + sub

    def multiply(i, logits_ref):
        seq, sub, block = place_of(i)
        frames = frame_ref[seq]
        hidden = jnp.concatenate(
            [
                jnp.tanh(frames + token_ref[pl.ds(seq * units + sub * SUB_UNITS + j, 1), :])
                for j in range(SUB_UNITS)
            ],
            axis=0,
        )
        hidden_ref[block] = hidden
        low = hidden.astype(BF16)
        logits_ref[...] = (
            jnp.dot(low, weight_ref[...], preferred_element_type=F32) + bias_ref[...]
        )

    def score(i, logits_ref):
        seq, sub, block = place_of(i)
        first_unit = sub * SUB_UNITS
        seq_len = jnp.where(seq == 0, lens[0], lens[1])
        last_unit = jnp.where(seq == 0, last_units[0], last_units[1])
        own_lanes = (part_lanes // GROUP) % 2 == seq
        logits = logits_ref[...]
        top = jnp.max(logits, axis=1, keepdims=True)
        weights = jnp.exp(logits - top)
        total = jnp.sum(weights, axis=1, keepdims=True)
        softmax_ref[block] = weights
        inverse_ref[block] = jnp.broadcast_to(1.0 / total, (weights.shape[0], 128))
        log_total = top + jnp.log(total)
        blanks = (logits[:, :1] - log_total) * LOG2E
        for j in range(SUB_UNITS):
            unit = first_unit + j
            rows = slice(j * frame_count, (j + 1) * frame_count)
            label = labels_smem[0, seq * units + unit]
            tile = logits_ref[rows, pl.ds(pl.multiple_of(label // 128 * 128, 128), 128)]
            picked = jnp.sum(
                jnp.where(lanes == label % 128, tile, 0.0), axis=1, keepdims=True
            )
            blank = blanks[rows]
            blank = jnp.where((times == seq_len - 1) & (unit < last_unit), NEG, blank)
            blank = jnp.where((times >= seq_len) | (unit > last_unit), 0.0, blank)
            step = jnp.where(
                (times >= seq_len) | (unit >= last_unit),
                NEG,
                (picked - log_total[rows]) * LOG2E,
            )
            at = (pl.ds(unit * (units + 1), part, stride=units), slice(None))
            blank = jnp.where(part_lanes < 64, blank[:part], blank[part:])
            step = jnp.where(part_lanes < 64, step[:part], step[part:])
            blank_ref[at] = jnp.where(own_lanes, blank, blank_ref[at])
            label_ref[at] = jnp.where(own_lanes, step, label_ref[at])

    in_two_stages(blocks, multiply, score, even_ref, odd_ref, label_copy.wait)
    eye = jnp.where(
        lane_ids(units) % GROUP == lax.broadcasted_iota(jnp.int32, (units, 128), 0), 0.0, NEG
    ).astype(F32)
    ahead, behind = both_ways(blank_ref, label_ref, units, steps, eye, eye)
    lanes = lane_ids(units)
    early = lanes < 64
    columns = jnp.where(early, behind, ahead)
    parts_ref[...] = columns
    others = pltpu.roll(jnp.where(early, ahead, behind), 64, 1)
    ways = [
        jnp.take_along_axis(
            columns, lanes // GROUP * GROUP + k, axis=1, mode="promise_in_bounds"
        )
        + others[k : k + 1, :]
        for k in range(units)
    ]
    top = functools.reduce(jnp.maximum, ways)
    total = functools.reduce(jnp.add, [jnp.exp2(way - top) for way in ways])
    matrix_ref[0, 0] = top + jnp.log2(total)


def turn_kernel(layout, offset_ref, lens_ref, tokens_ref, hidden_ref, turned_ref):
    width = hidden_ref.shape[2]
    first_frame = lax.axis_index("frames") * layout["frame_count"]
    first_seq = first_of(layout["seqs_here"], offset_ref)
    counts = block_counts(lens_ref, tokens_ref, first_seq, first_frame)

    def one_block(i, _):
        seq = jnp.where(i >= counts[0], 1, 0)
        block = i + seq * (layout["units"] // SUB_UNITS - counts[0])
        turned_ref[block, :width, :] = hidden_ref[block].astype(BF16).T
        turned_ref[block, width:, :] = jnp.ones((16, turned_ref.shape[2]), BF16)
        return 0

    lax.fori_loop(0, counts[0] + counts[1], one_block, 0)


def tangent_kernel(
    layout,
    offset_ref,
    lens_ref,
    tokens_ref,
    scale_ref,
    softmax_ref,
    label_table_ref,
    blank_ref,
    label_ref,
    turned_ref,
    inverse_ref,
    parts_ref,
    *refs,
):
    hops = layout["hops"]
    matrix_refs, refs = refs[: hops + 1], refs[hops + 1 :]
    (
        tangents_ref,
        output_bias_ref,
        loss_ref,
        *kept_refs,
        sums_ref,
        matrices_ref,
        ahead_ref,
        behind_ref,
        blank_part_ref,
        label_part_ref,
        even_ref,
        odd_ref,
        labels_smem,
        label_sem,
        sems,
    ) = refs
    label_copy = pltpu.make_async_copy(label_table_ref, labels_smem, label_sem)
    label_copy.start()
    frame_count = layout["frame_count"]
    width = turned_ref.shape[1] - 16
    units = layout["units"]
    part = frame_count // 2
    steps = part + units - 1
    here = lax.axis_index("frames")
    first_frame = here * frame_count
    first_seq = first_of(layout["seqs_here"], offset_ref)
    chunks = matrices_ref.shape[0]
    vocab = softmax_ref.shape[2]
    received = [(ref, n) for ref in matrix_refs for n in range(ref.shape[0])]
    for place, (matrix_ref, n) in zip(layout["matrix_places"], received):
        matrices_ref[place] = matrix_ref[n, 0]
    starts = lax.broadcasted_iota(jnp.int32, (units, 128), 0)
    lanes = lane_ids(units)
    early = lanes < 64
    gather_ids = lanes // GROUP * GROUP + starts
    own_first = (lane_ids(1) // GROUP) % 2 == 0

    def through(column, matrix):
        ways = column + matrix
        top = jnp.max(ways, axis=0, keepdims=True)
        row = top + jnp.log2(jnp.sum(jnp.exp2(ways - top), axis=0, keepdims=True))
        row = jnp.broadcast_to(row, (units, 128))
        return jnp.take_along_axis(row, gather_ids, axis=1, mode="promise_in_bounds")

    def one_chunk(i, carry):
        column, kept = carry
        other = chunks - 1 - i
        kept = jnp.where(jnp.where(early, i, other) == here, column, kept)
        matrix = jnp.where(early, matrices_ref[here ^ i], matrices_ref[here ^ other])
        return through(column, matrix), kept

    start = jnp.where(early & (starts > 0), NEG, 0.0).astype(F32)
    last, kept = lax.fori_loop(0, chunks, one_chunk, (start, start))
    middle = pltpu.roll(through(kept, parts_ref[...]), 64, 1)
    both_ways(
        blank_ref,
        label_ref,
        units,
        steps,
        jnp.where(early, kept, middle),
        jnp.where(early, middle, kept),
        (ahead_ref, behind_ref),
    )
    log_norm = jnp.max(jnp.where(early, last, pltpu.roll(last, 64, 1)), axis=0, keepdims=True)
    scale, length, bound = (
        jnp.where(own_first, entry(ref, first_seq), entry(ref, first_seq + 1))
        for ref in (scale_ref, lens_ref, tokens_ref)
    )
    length, bound = length.astype(jnp.int32), bound.astype(jnp.int32)
    part_start = first_frame + jnp.where(lane_ids(1) < 64, 0, part)
    last_diagonal = starts + jnp.minimum(length - part_start, part)
    first_blank = jnp.where(starts <= bound, starts, steps)
    first_label = jnp.where(starts < bound, starts, steps)
    norm = log_norm - jnp.log2(scale)

    def one_diagonal(e, _):
        rows = pl.ds(pl.multiple_of(e * units, 8), units)
        behind = behind_ref[rows, :]
        base = ahead_ref[rows, :] - norm
        before_end = last_diagonal > e
        blank_part_ref[rows, :] = jnp.where(
            before_end & (first_blank <= e), jnp.exp2(base + blank_ref[rows, :] + behind), 0.0
        )
        label_part_ref[rows, :] = jnp.where(
            before_end & (first_label <= e),
            jnp.exp2(base + label_ref[rows, :] + pltpu.roll(behind, units - 1, 0)),
            0.0,
        )
        return 0

    lax.fori_loop(0, steps, one_diagonal, 0, unroll=5)

    counts = block_counts(lens_ref, tokens_ref, first_seq, first_frame)
    block_lanes = lane_ids(frame_count)
    part_lanes = lane_ids(part)

    def place_of(i):
        seq = jnp.where(i >= counts[0], 1, 0)
        sub = i - seq * counts[0]
        return seq, sub, seq * (units // SUB_UNITS) + sub

    wide = lane_ids(1)
    loss = jnp.where(here == 0, -log_norm * LN2, 0.0)
    spread = jnp.where(wide == first_seq, loss[:, :1], 0.0)
    loss_ref[...] = spread + jnp.where(wide == first_seq + 1, loss[:, GROUP : GROUP + 1], 0.0)
    label_copy.wait()

    counts_all = counts[0] + counts[1]
    sums_ref[...] = jnp.zeros_like(sums_ref)
    output_bias_ref[...] = jnp.zeros_like(output_bias_ref)

    def prepare(i, tangent_ref):
        seq, sub, block = place_of(i)
        own_lanes = [part_lanes % GROUP + GROUP * (seq + 2 * half) for half in (0, 1)]
        for j in range(SUB_UNITS):
            unit = sub * SUB_UNITS + j
            rows = slice(j * frame_count, (j + 1) * frame_count)
            at = (pl.ds(unit * (units + 1), part, stride=units), slice(None))
            blank, step = (
                jnp.concatenate(
                    [
                        jnp.take_along_axis(ref[at], ids, axis=1, mode="promise_in_bounds")
                        for ids in own_lanes
                    ],
                    axis=0,
                )
                for ref in (blank_part_ref, label_part_ref)
            )
            both = (blank + step) * inverse_ref[block, rows, :]
            for v in range(vocab // 128):
                cut = slice(v * 128, (v + 1) * 128)
                piece = softmax_ref[block, rows, cut] * both
                if v == 0:
                    piece = piece - jnp.where(block_lanes == 0, blank, 0.0)
                piece = piece.astype(BF16)
                tangent_ref[rows, cut] = piece
                tangents_ref[block, rows, cut] = piece
            label = labels_smem[0, seq * units + unit]
            cut = pl.ds(pl.multiple_of(label // 128 * 128, 128), 128)
            piece = softmax_ref[block, rows, cut] * both
            piece = piece - jnp.where((block_lanes == 0) & (label < 128), blank, 0.0)
            piece = (piece - jnp.where(block_lanes == label % 128, step, 0.0)).astype(BF16)
            tangent_ref[rows, cut] = piece
            tangents_ref[block, rows, cut] = piece

    def multiply(i, tangent_ref):
        _, _, block = place_of(i)
        product = jnp.dot(turned_ref[block], tangent_ref[...], preferred_element_type=F32)
        for v in range(vocab // 128):
            sums_ref[v * width : (v + 1) * width, :] += product[:width, v * 128 : (v + 1) * 128]
        output_bias_ref[...] += product[width : width + 1, :]

    in_two_stages(counts_all, prepare, multiply, even_ref, odd_ref)
    part_halves(sums_ref, kept_refs, sems)


def part_halves(sums_ref, piece_refs, sems):
    place = lax.axis_index("tokens") & 1
    copies, start = [], 0
    for kept_ref, sent_ref in zip(piece_refs[::2], piece_refs[1::2]):
        half = kept_ref.shape[0]
        for part, target in ((1 - place, sent_ref.at[:half, :]), (place, kept_ref)):
            source = sums_ref.at[pl.ds(pl.multiple_of(start + part * half, 8), half), :]
            copies.append(pltpu.make_async_copy(source, target, sems.at[len(copies)]))
        start += 2 * half
    for copy in copies:
        copy.start()
    for copy in copies:
        copy.wait()


def inner_kernel(
    layout,
    offset_ref,
    lens_ref,
    tokens_ref,
    tangents_ref,
    hidden_ref,
    weight_ref,
    encoder_ref,
    output_bias_ref,
    loss_ref,
    frame_tangent_ref,
    exact_ref,
    kept_ref,
    sent_ref,
    sums_ref,
    frame_sum_ref,
    token_sum_ref,
    even_ref,
    odd_ref,
    sems,
):
    seqs, frame_count, width = encoder_ref.shape
    units = token_sum_ref.shape[0] // seqs
    vocab = weight_ref.shape[1]
    first_frame = lax.axis_index("frames") * frame_count
    first_seq = first_of(layout["seqs_here"], offset_ref)
    frame_sum_ref[...] = jnp.zeros_like(frame_sum_ref)
    token_sum_ref[...] = jnp.zeros_like(token_sum_ref)
    half = layout["half"]
    for side in (0, 1):
        unset = slice(side * half + layout["token"], (side + 1) * half)
        sums_ref[unset, :] = jnp.zeros_like(sums_ref[unset, :])
    counts = block_counts(lens_ref, tokens_ref, first_seq, first_frame)

    def place_of(i):
        seq = jnp.where(i >= counts[0], 1, 0)
        sub = i - seq * counts[0]
        return seq, sub, seq * (units // SUB_UNITS) + sub

    def product_of(tangents):
        return lax.dot_general(
            tangents, weight_ref[...], (((1,), (1,)), ((), ())), preferred_element_type=F32
        )

    def add_up(i, product):
        seq, sub, block = place_of(i)
        hidden = hidden_ref[block]
        inner = product * (1.0 - hidden * hidden)
        total = frame_sum_ref[seq]
        for j in range(SUB_UNITS):
            rows = slice(j * frame_count, (j + 1) * frame_count)
            total = total + inner[rows]
            token_sum_ref[pl.ds(seq * units + sub * SUB_UNITS + j, 1), :] = jnp.sum(
                inner[rows], axis=0, keepdims=True
            )
        frame_sum_ref[seq] = total

    def multiply_two(n, product_ref):
        both = [tangents_ref[place_of(2 * n + m)[2]] for m in (0, 1)]
        product_ref[...] = product_of(jnp.concatenate(both, axis=0))

    def add_up_two(n, product_ref):
        half = product_ref.shape[0] // 2
        add_up(2 * n, product_ref[:half])
        add_up(2 * n + 1, product_ref[half:])

    blocks = counts[0] + counts[1]
    in_two_stages(blocks // 2, multiply_two, add_up_two, even_ref, odd_ref)

    @pl.when(blocks % 2 == 1)
    def _():
        add_up(blocks - 1, product_of(tangents_ref[place_of(blocks - 1)[2]]))

    low = frame_sum_ref[...].reshape(seqs * frame_count, width).astype(BF16)
    frame_tangent_ref[...] = low
    product = lax.dot_general(
        encoder_ref[...].reshape(seqs * frame_count, width),
        low,
        (((0,), (0,)), ((), ())),
        preferred_element_type=F32,
    )
    encoder_bias = jnp.sum(low.astype(F32), axis=0, keepdims=True)
    blocks_each = width // 128 // 2
    exact_ref[...] = jnp.zeros_like(exact_ref)
    for v in range(width // 128):
        cut = slice(v * 128, (v + 1) * 128)
        start, n = v // blocks_each * half, v % blocks_each
        sums_ref[start + n * width : start + (n + 1) * width, :] = product[:, cut]
        at = start + layout["token"] + n * layout["token_rows"] + first_seq * units
        sums_ref[pl.ds(pl.multiple_of(at, 8), seqs * units), :] = token_sum_ref[:, cut]
        at = vocab // 128 + v
        exact_ref[at : at + 1, :] = encoder_bias[:, cut]
    for v in range(vocab // 128):
        exact_ref[v : v + 1, :] = output_bias_ref[:, v * 128 : (v + 1) * 128]
    at = vocab // 128 + width // 128
    exact_ref[at : at + 1, :] = loss_ref[...]
    part_halves(sums_ref, (kept_ref, sent_ref), sems)
    write_exact(sent_ref, kept_ref.shape[0], exact_ref[...])


def encoder_kernel(frame_tangent_ref, encoder_weight_ref, encoder_gradient_ref):
    encoder_gradient_ref[...] = lax.dot_general(
        frame_tangent_ref[...],
        encoder_weight_ref[...],
        (((1,), (1,)), ((), ())),
        preferred_element_type=F32,
    ).reshape(encoder_gradient_ref.shape)


def two_halves(stage, half):
    upper = upper_of(stage)
    own = pl.ds(pl.multiple_of(jnp.where(upper != 0, half, 0), 16), half)
    other = pl.ds(pl.multiple_of(jnp.where(upper != 0, 0, half), 16), half)
    return own, other


def exact_rows(kind):
    return EXACT if kind == F32 else 3 * EXACT


def write_exact(sent_ref, at, values):
    if sent_ref.dtype == F32:
        sent_ref[at : at + EXACT, :] = values
        return
    for n in range(3):
        part = values.astype(BF16)
        sent_ref[at + n * EXACT : at + (n + 1) * EXACT, :] = part
        values = values - part.astype(F32)


def read_exact(received_ref, at):
    parts = [
        received_ref[at + n * EXACT : at + (n + 1) * EXACT, :].astype(F32)
        for n in range(exact_rows(received_ref.dtype) // EXACT)
    ]
    return sum(parts[1:], parts[0])


def halve_kernel(stages, merge, has_exact, *refs):
    count, at = len(stages), 0
    outs = refs[2 * count + has_exact :]
    for n, stage in enumerate(stages):
        kept_ref, received_ref = refs[2 * n : 2 * n + 2]
        half = kept_ref.shape[0] // 2
        own, other = two_halves(stage, half)
        if merge:
            next_ref, sent_ref = (ref.at[at : at + half, :] for ref in outs[:2])
            at += half
        else:
            next_ref, sent_ref = outs[2 * n : 2 * n + 2]
        sent = kept_ref[other, :] + received_ref[other, :].astype(F32)
        sent_ref[:half, :] = sent.astype(sent_ref.dtype)
        next_ref[...] = kept_ref[own, :] + received_ref[own, :].astype(F32)
    if has_exact:
        exact = refs[2 * count][...] + read_exact(received_ref, kept_ref.shape[0])
        outs[-1][...] = exact
        write_exact(outs[-2], outs[-3].shape[0], exact)


def add_kernel(count, *refs):
    sum_ref, exact_sum_ref = refs[2 * count + 1 :]
    at = 0
    for n in range(count):
        kept_ref, received_ref = refs[2 * n : 2 * n + 2]
        rows = kept_ref.shape[0]
        total = kept_ref[...] + received_ref[:rows, :].astype(F32)
        high = total.astype(BF16)
        sum_ref[at : at + rows, :] = high
        at += rows
    sum_ref[at : at + rows, :] = (total - high.astype(F32)).astype(BF16)
    exact = refs[2 * count][...] + read_exact(received_ref, rows)
    exact_sum_ref[...] = exact
    write_exact(sum_ref, at + rows, exact)


def last_kernel(own_ref, other_ref, exact_ref, beside_ref, *sum_refs):
    *sum_refs, exact_sum_ref = sum_refs
    at = 0
    for n, sum_ref in enumerate(sum_refs):
        rows = sum_ref.shape[0]
        totals = []
        for ref in (own_ref, other_ref):
            total = ref[at : at + rows, :].astype(F32)
            if n == len(sum_refs) - 1:
                total = total + ref[at + rows : at + 2 * rows, :].astype(F32)
            totals.append(total)
        sum_ref[...] = (totals[0] + totals[1]).astype(BF16)
        at += rows
    exact_sum_ref[...] = exact_ref[...] + read_exact(other_ref, at + rows)


def join_kernel(stages, merged, *refs):
    count, at = len(stages), 0
    joined_refs = refs[2:] if merged else refs[2 * count :]
    for n, (stage, joined_ref) in enumerate(zip(stages, joined_refs)):
        half = joined_ref.shape[0] // 2
        own, other = two_halves(stage, half)
        if merged:
            own_ref, other_ref = (ref.at[at : at + half, :] for ref in refs[:2])
            at += half
        else:
            own_ref, other_ref = refs[2 * n : 2 * n + 2]
        joined_ref[own, :] = own_ref[...]
        joined_ref[other, :] = other_ref[...]


def copy_out(output_ref, rest_ref, side, output_hbm, encoder_hbm, output_buffer, encoder_buffer, sems):
    copies = []
    for source, buffer, target in (
        (output_ref, output_buffer, output_hbm),
        (rest_ref, encoder_buffer, encoder_hbm),
    ):
        rows, columns = buffer.shape
        for v in range(columns // 128):
            buffer[:, v * 128 : (v + 1) * 128] = source[v * rows : (v + 1) * rows, :].astype(F32)
        start = pl.multiple_of(side * columns, 128)
        copy = pltpu.make_async_copy(
            buffer, target.at[:, pl.ds(start, columns)], sems.at[len(copies)]
        )
        copy.start()
        copies.append(copy)
    return copies


def finish_own_kernel(output_ref, rest_ref, output_hbm, encoder_hbm, *scratch):
    place = lax.axis_index("tokens") & 1
    for copy in copy_out(output_ref, rest_ref, place, output_hbm, encoder_hbm, *scratch):
        copy.wait()


def finish_kernel(
    layout,
    output_other_ref,
    rest_own_ref,
    rest_other_ref,
    packets_ref,
    predictor_weight_ref,
    exact_ref,
    output_weight_begun,
    encoder_weight_begun,
    output_weight_hbm,
    encoder_weight_hbm,
    weight_gradient_hbm,
    output_bias_ref,
    encoder_bias_ref,
    bias_gradient_ref,
    predictor_gradient_ref,
    losses_ref,
    output_buffer,
    encoder_buffer,
    weight_gradient_ref,
    tokens_ref,
    predictor_ref,
    sems,
    gradient_sem,
):
    width, vocab = encoder_buffer.shape[0], output_bias_ref.shape[1]
    place = lax.axis_index("tokens") & 1
    copies = copy_out(
        output_other_ref,
        rest_other_ref,
        1 - place,
        output_weight_hbm,
        encoder_weight_hbm,
        output_buffer,
        encoder_buffer,
        sems,
    )
    count = layout["token_rows"]
    blocks_each = width // 128 // 2

    def gather_tokens(*halves):
        for v in range(width // 128):
            at = layout["token"] + v % blocks_each * count
            tokens_ref[:, v * 128 : (v + 1) * 128] = halves[v // blocks_each][
                at : at + count, :
            ].astype(F32)

    pl.when(place == 0)(lambda: gather_tokens(rest_own_ref, rest_other_ref))
    pl.when(place == 1)(lambda: gather_tokens(rest_other_ref, rest_own_ref))
    tokens = tokens_ref[...]
    held_rows = packets_ref.shape[1] // (width // 128)
    for d in range(packets_ref.shape[0]):
        unpack_rows(packets_ref[d], predictor_ref, d * held_rows)
    weight_gradient_ref[...] = lax.dot_general(
        predictor_ref[...].astype(BF16),
        tokens.astype(BF16),
        (((0,), (0,)), ((), ())),
        preferred_element_type=F32,
    )
    gradient_copy = pltpu.make_async_copy(weight_gradient_ref, weight_gradient_hbm, gradient_sem)
    gradient_copy.start()

    def row(n):
        return exact_ref[n : n + 1, :]

    output_bias_ref[...] = jnp.concatenate([row(v) for v in range(vocab // 128)], axis=1)
    encoder_bias_ref[...] = jnp.concatenate(
        [row(vocab // 128 + v) for v in range(width // 128)], axis=1
    )
    bias_gradient_ref[...] = jnp.sum(tokens, axis=0, keepdims=True)
    device = lax.axis_index("frames") * lax.axis_size("tokens") + lax.axis_index("tokens")
    mine = jnp.concatenate(
        [tokens_ref[pl.ds(device * held_rows + r, 1), :] for r in range(held_rows)], axis=0
    )
    predictor_gradient_ref[:, 0, :] = lax.dot_general(
        mine.astype(BF16),
        predictor_weight_ref[...],
        (((1,), (1,)), ((), ())),
        preferred_element_type=F32,
    )
    loss = row(vocab // 128 + width // 128)
    losses_ref[...] = jnp.sum(
        jnp.where(lane_ids(1) == lax.axis_index("frames"), loss, 0.0), axis=1, keepdims=True
    )
    for copy in copies:
        copy.wait()
    gradient_copy.wait()


def in_hbm(array):
    return pltpu.with_memory_space_constraint(array, pltpu.HBM)


def in_vmem(array):
    return pltpu.with_memory_space_constraint(array, pltpu.VMEM)


def permuted(array, partner):
    frames, tokens = lax.axis_size("frames"), lax.axis_size("tokens")
    pairs = []
    for f in range(frames):
        for k in range(tokens):
            g, h = partner(f, k)
            pairs.append((f * tokens + k, g * tokens + h))
    return lax.ppermute(array, AXES, pairs)


def doubled(array, axis):
    blocks, places = [array], [[0]]
    bit = lax.axis_size(axis) // 2
    while bit:
        joined = jnp.concatenate(blocks, axis=0) if len(blocks) > 1 else blocks[0]
        flip = ((bit, 0), (bit, 0)) if axis == "frames" else ((0, bit), (0, bit))
        blocks.append(permuted(joined, across(flip)))
        places.append([place ^ bit for held in places for place in held])
        bit //= 2
    return blocks, [place for held in places for place in held]


def stages(even, odd):
    frame_bits = [(1 << i, 0) for i in range(lax.axis_size("frames").bit_length() - 1)]
    token_bits = [(0, 1 << i) for i in range(1, lax.axis_size("tokens").bit_length() - 1)]
    first = frame_bits[:1] + token_bits + frame_bits[1:2]
    orders = [first[shift:] + first[:shift] + frame_bits[2:] for shift in (even, odd)]
    return list(zip(*orders))


def upper_of(stage):
    f, k = lax.axis_index("frames"), lax.axis_index("tokens")
    even, odd = ((f & frame_bit) | (k & token_bit) for frame_bit, token_bit in stage)
    return jnp.where((k & 1) == 0, even, odd)


def across(stage):
    return lambda f, k: (f ^ stage[k & 1][0], k ^ stage[k & 1][1])


def neighbour(f, k):
    return f, k ^ 1


def call(body, ins, outs, scratch=(), limit=4):
    vmem = pl.BlockSpec(memory_space=pltpu.VMEM)
    there = [array is not None for array in ins]

    def kernel(*refs):
        given = iter(refs)
        body(*(next(given) if here else None for here in there), *given)

    return pl.pallas_call(
        kernel,
        in_specs=[vmem] * sum(there),
        out_specs=[
            pl.BlockSpec(memory_space=pl.ANY) if inside is None else vmem for _, _, inside in outs
        ],
        out_shape=[
            pltpu.VMEM(shape, kind) if inside else jax.ShapeDtypeStruct(shape, kind)
            for shape, kind, inside in outs
        ],
        scratch_shapes=list(scratch),
        compiler_params=pltpu.CompilerParams(vmem_limit_bytes=limit * 2**20),
    )(*(in_vmem(array) for array in ins if array is not None))


def reduced_and_gathered(pieces, exact, beside):
    plans = list(zip(*(stages(*shifts) for shifts in ORDERS)))
    flat = [a for kept, sent in pieces for a in (kept, permuted(sent, neighbour))]
    way_back = []
    *plans, last_plan = plans
    for number, plan in enumerate(plans):
        plan = plan[: len(flat) // 2]
        merge = len(plan) > 1 and len(set(plan)) == 1
        halves = [kept.shape[0] // 2 for kept in flat[::2]]
        way_back.append((plan, merge, [2 * half for half in halves]))
        if merge:
            halves = [sum(halves)]
        sent_type = SENT_TYPES[min(number, len(SENT_TYPES) - 1)]
        outs = []
        for n, half in enumerate(halves):
            sent_rows = half + (exact_rows(sent_type) if n == len(halves) - 1 else 0)
            outs += [((half, 128), F32, True), ((sent_rows, 128), sent_type, True)]
        exact_out = ((EXACT, 128), F32, True)
        if number < 2:
            given, flat = flat, []
            for n, stage in enumerate(plan):
                last = n == len(plan) - 1
                made = call(
                    functools.partial(halve_kernel, [stage], False, last),
                    given[2 * n : 2 * n + 2] + [exact] * last,
                    outs[2 * n : 2 * n + 2] + [exact_out] * last,
                )
                flat += made[:2]
                if last:
                    exact = made[2]
        else:
            *flat, exact = call(
                functools.partial(halve_kernel, plan, merge, True),
                [*flat, exact],
                [*outs, exact_out],
            )
        flat = [
            permuted(a, across(plan[n // 2])) if n % 2 else a for n, a in enumerate(flat)
        ]
    shapes = [kept.shape for kept in flat[::2]]
    rows = sum(shape[0] for shape in shapes) + shapes[-1][0] + exact_rows(BF16)
    own, exact = call(
        functools.partial(add_kernel, len(shapes)),
        [*flat, exact],
        [((rows, 128), BF16, True), ((EXACT, 128), F32, True)],
    )
    other = permuted(own, across(last_plan[0]))
    vmem = pl.BlockSpec(memory_space=pltpu.VMEM)
    *arrays, exact = pl.pallas_call(
        last_kernel,
        in_specs=[vmem, vmem, vmem, pl.BlockSpec(memory_space=pl.ANY)],
        out_specs=[vmem] * (len(shapes) + 1),
        out_shape=[pltpu.VMEM(shape, BF16) for shape in shapes] + [pltpu.VMEM((EXACT, 128), F32)],
        compiler_params=pltpu.CompilerParams(vmem_limit_bytes=4 * 2**20),
    )(in_vmem(own), in_vmem(other), in_vmem(exact), in_hbm(beside))
    for number, (plan, merged, sizes) in reversed(list(enumerate(way_back))):
        flat = [a for array, stage in zip(arrays, plan) for a in (array, permuted(array, across(stage)))]
        outs = [((size, 128), BF16, True) for size in sizes]
        if number in (0,):
            arrays = [
                call(
                    functools.partial(join_kernel, [stage], False),
                    flat[2 * n : 2 * n + 2],
                    outs[n : n + 1],
                )[0]
                for n, stage in enumerate(plan)
            ]
        else:
            arrays = call(functools.partial(join_kernel, plan, merged), flat, outs)
    return [(array, permuted(array, neighbour)) for array in arrays], exact


def per_device(
    encoder_out,
    encoder_weight,
    encoder_bias,
    predictor_out,
    predictor_weight,
    predictor_bias,
    output_weight,
    output_bias,
    labels,
    frame_lens,
    token_lens,
    loss_scale,
):
    seq_count, frame_count, width = encoder_out.shape
    vocab = output_weight.shape[1]
    all_seqs = labels.shape[0]
    held_seqs, held_units = predictor_out.shape[:2]
    assert held_seqs == 1
    frame_axis, token_axis = lax.axis_size("frames"), lax.axis_size("tokens")
    device_count = frame_axis * token_axis
    units = held_units * token_axis
    calls = seq_count // 2
    diagonals = (frame_count // 2 + units) * units
    vmem = pl.BlockSpec(memory_space=pltpu.VMEM)
    anywhere = pl.BlockSpec(memory_space=pl.ANY)

    weights = (
        encoder_out,
        encoder_weight,
        encoder_bias.reshape(1, width),
        predictor_weight,
        predictor_bias.reshape(1, width),
        output_weight,
        output_bias.reshape(1, vocab),
        frame_lens.reshape(1, all_seqs),
        token_lens.reshape(1, all_seqs),
        loss_scale.reshape(1, all_seqs),
    )
    packet_rows = held_units * width // 128
    packets = pl.pallas_call(
        packet_kernel,
        in_specs=[anywhere],
        out_specs=vmem,
        out_shape=jax.ShapeDtypeStruct((device_count, packet_rows, 128), BF16),
        scratch_shapes=[
            pltpu.VMEM((held_units, width), BF16),
            pltpu.VMEM((packet_rows, 128), F32),
            pltpu.SemaphoreType.DMA,
        ],
        compiler_params=pltpu.CompilerParams(vmem_limit_bytes=4 * 2**20),
    )(in_hbm(predictor_out.reshape(held_units, width)))
    label_blocks, label_places = doubled(labels[None], "tokens")
    *weights, frames = pl.pallas_call(
        load_kernel,
        in_specs=[anywhere] * len(weights),
        out_specs=[vmem] * (1 + len(weights)),
        out_shape=[pltpu.VMEM(w.shape, w.dtype) for w in weights]
        + [pltpu.VMEM(encoder_out.shape, F32)],
        scratch_shapes=[pltpu.SemaphoreType.DMA((len(weights),))],
        compiler_params=pltpu.CompilerParams(vmem_limit_bytes=4 * 2**20),
    )(*map(in_hbm, weights))
    *weights, frame_lens, token_lens, loss_scale = weights
    lens = frame_lens, token_lens
    packets = lax.all_to_all(packets, AXES, 0, 0, tiled=True)

    score_shapes = [
        ((2 * units // SUB_UNITS, SUB_UNITS * frame_count, vocab), F32),
        ((2 * units, width), F32),
        ((diagonals, 128), F32),
        ((diagonals, 128), F32),
        ((2 * units // SUB_UNITS, SUB_UNITS * frame_count, width), F32),
        ((2 * units // SUB_UNITS, SUB_UNITS * frame_count, 128), F32),
        ((units, 128), F32),
        ((1, 1, units, 128), F32),
    ]

    def scores(offset, frames):
        (table,) = call(
            functools.partial(table_kernel, label_places, seq_count),
            (offset, *label_blocks),
            [((1, 128), jnp.int32, True)],
        )
        scored = call(
            functools.partial(score_kernel, seq_count),
            (offset, packets, *lens, frames, *weights[3:], table),
            [(shape, kind, True) for shape, kind in score_shapes],
            scratch=[
                pltpu.VMEM((SUB_UNITS * frame_count, vocab), F32),
                pltpu.VMEM((SUB_UNITS * frame_count, vocab), F32),
                pltpu.SMEM((1, 128), jnp.int32),
                pltpu.SemaphoreType.DMA,
            ],
            limit=8,
        )
        return [table, *scored]

    offsets = 2 * jnp.arange(calls, dtype=jnp.int32).reshape(calls, 1, 1)
    encoders = weights[0].reshape(calls, 2, frame_count, width)
    if calls == 1:
        scored = scores(None, frames)
        matrix = scored[-1]
    else:
        scored = lax.map(
            lambda given: scores(*given),
            (offsets, frames.reshape(calls, 2, frame_count, width)),
        )
        matrix = scored[-1].reshape(1, calls, units, 128)

    matrices, matrix_places = doubled(matrix, "frames")
    layout = {"matrix_places": matrix_places, "seqs_here": seq_count, "frame_count": frame_count, "units": units}
    align = 16 * device_count // 4
    blocks_each = width // 128 // 2
    layout["token"], layout["token_rows"] = blocks_each * width, all_seqs * units
    half = layout["token"] + blocks_each * all_seqs * units
    layout["half"] = half + (-half % align)
    rest_rows = 2 * layout["half"]
    output_rows = vocab // 128 * width
    assert output_rows % (2 * align) == 0 and vocab // 128 + width // 128 < EXACT

    blocks = 2 * units // SUB_UNITS
    block_rows = SUB_UNITS * frame_count

    def turns(offset, scored):
        hidden = scored[5]
        (turned,) = call(
            functools.partial(turn_kernel, layout),
            (offset, *lens, hidden),
            [((hidden.shape[0], width + 16, hidden.shape[1]), BF16, True)],
        )
        return turned

    def tangents(offset, scored, turned, matrices):
        table, softmax, _, blank, label, _, inverse, parts = scored
        return call(
            functools.partial(tangent_kernel, dict(layout, hops=len(matrices) - 1)),
            (
                *(offset, *lens, loss_scale, softmax, table, blank, label),
                *(turned, inverse, parts, *matrices),
            ),
            [
                ((blocks, block_rows, vocab), BF16, True),
                ((1, vocab), F32, True),
                ((1, 128), F32, True),
                ((output_rows // 2, 128), F32, True),
                ((output_rows // 2, 128), F32, True),
            ],
            scratch=[
                pltpu.VMEM((output_rows, 128), F32),
                pltpu.VMEM((frame_axis, units, 128), F32),
                pltpu.VMEM((diagonals, 128), F32),
                pltpu.VMEM((diagonals, 128), F32),
                pltpu.VMEM((diagonals, 128), F32),
                pltpu.VMEM((diagonals, 128), F32),
                pltpu.VMEM((block_rows, vocab), BF16),
                pltpu.VMEM((block_rows, vocab), BF16),
                pltpu.SMEM((1, 128), jnp.int32),
                pltpu.SemaphoreType.DMA,
                pltpu.SemaphoreType.DMA((4,)),
            ],
            limit=12,
        )

    def inners(offset, encoder, scored, tangent, output_bias_sum, loss):
        return call(
            functools.partial(inner_kernel, layout),
            (offset, *lens, tangent, scored[5], weights[5], encoder, output_bias_sum, loss),
            [
                ((2 * frame_count, width), BF16, True),
                ((EXACT, 128), F32, True),
                ((rest_rows // 2, 128), F32, True),
                ((rest_rows // 2 + EXACT, 128), F32, True),
            ],
            scratch=[
                pltpu.VMEM((rest_rows, 128), F32),
                pltpu.VMEM((2, frame_count, width), F32),
                pltpu.VMEM((2 * units, width), F32),
                pltpu.VMEM((2 * block_rows, width), F32),
                pltpu.VMEM((2 * block_rows, width), F32),
                pltpu.SemaphoreType.DMA((2,)),
            ],
            limit=10,
        )

    def encoder_gradient_of(frame_tangent):
        return call(
            encoder_kernel,
            (frame_tangent, weights[1]),
            [((2, frame_count, width), F32, False)],
        )[0]

    if calls == 1:
        scored = scored[:-1]
        turned = turns(None, scored)
        tangent, output_bias_sum, loss, *output_sums = tangents(None, scored, turned, matrices)

        frame_tangent, exact, *rest = inners(
            None, weights[0], scored, tangent, output_bias_sum, loss
        )
        sums = [*output_sums, *rest, exact]
        encoder_gradient = encoder_gradient_of(frame_tangent)
    else:

        def add_call(sums, given):
            offset, encoder, scored, call = given
            own = [lax.dynamic_slice_in_dim(m, call, 1, 1) for m in matrices]
            turned = turns(offset, scored)
            tangent, output_bias_sum, loss, *more = tangents(offset, scored, turned, own)
            frame_tangent, exact, *rest = inners(
                offset, encoder, scored, tangent, output_bias_sum, loss
            )
            sums = [a + b for a, b in zip(sums, [*more, *rest, exact])]
            return sums, encoder_gradient_of(frame_tangent)

        sizes = (output_rows // 2,) * 2 + (rest_rows // 2, rest_rows // 2 + EXACT, EXACT)
        sums, encoder_gradient = lax.scan(
            add_call,
            [jnp.zeros((size, 128), F32) for size in sizes],
            (offsets, encoders, scored[:-1], jnp.arange(calls)),
        )
        encoder_gradient = encoder_gradient.reshape(encoder_out.shape)

    halves, exact = reduced_and_gathered(
        [sums[:2], sums[2:4]], sums[4], encoder_gradient
    )
    (output_own, output_other), (rest_own, rest_other) = halves
    buffers = [
        pltpu.VMEM((width, vocab // 2), F32),
        pltpu.VMEM((width, width // 2), F32),
    ]
    begun = call(
        finish_own_kernel,
        (output_own, rest_own),
        [((width, vocab), F32, None), ((width, width), F32, None)],
        scratch=[*buffers, pltpu.SemaphoreType.DMA((2,))],
        limit=8,
    )
    finished = pl.pallas_call(
        functools.partial(finish_kernel, layout),
        in_specs=[vmem] * 6 + [anywhere] * 2,
        out_specs=[anywhere] * 3 + [vmem] * 5,
        out_shape=[
            jax.ShapeDtypeStruct((width, vocab), F32),
            jax.ShapeDtypeStruct((width, width), F32),
            jax.ShapeDtypeStruct((width, width), F32),
            jax.ShapeDtypeStruct((1, vocab), F32),
            jax.ShapeDtypeStruct((1, width), F32),
            jax.ShapeDtypeStruct((1, width), F32),
            jax.ShapeDtypeStruct((held_units, 1, width), F32),
            jax.ShapeDtypeStruct((1, 1), F32),
        ],
        input_output_aliases={6: 0, 7: 1},
        scratch_shapes=[
            *buffers,
            pltpu.VMEM((width, width), F32),
            pltpu.VMEM((all_seqs * units, width), F32),
            pltpu.VMEM((all_seqs * units, width), F32),
            pltpu.SemaphoreType.DMA((2,)),
            pltpu.SemaphoreType.DMA,
        ],
        compiler_params=pltpu.CompilerParams(vmem_limit_bytes=20 * 2**20),
    )(
        *map(in_vmem, (output_other, rest_own, rest_other, packets, weights[3], exact)),
        *map(in_hbm, begun),
    )
    return (
        finished[7].reshape(1),
        encoder_gradient,
        finished[6].transpose(1, 0, 2),
        finished[1],
        finished[4].reshape(width),
        finished[2],
        finished[5].reshape(width),
        finished[0],
        finished[3].reshape(vocab),
    )


def solution(mesh):
    placed = (
        P("tokens", "frames", None),
        P(),
        P(),
        P("frames", "tokens", None),
        P(),
        P(),
        P(),
        P(),
        P(None, "tokens"),
        P(),
        P(),
        P(),
    )
    return jax.shard_map(
        per_device,
        mesh=mesh,
        in_specs=placed,
        out_specs=(
            P("frames"),
            P("tokens", "frames", None),
            P("frames", "tokens", None),
            P(),
            P(),
            P(),
            P(),
            P(),
            P(),
        ),
        check_vma=False,
    )
```

profile of v0, /device:TPU:0, one launch (start us, length us, event | category | flops | bytes accessed | tf_op | source)
XLA Modules:
  0.0 100.4 jit_solution(11397269091283969986)
XLA Ops:
  0.6 1.4 %shard_map.188 = bf16[32,24,128]{2,1,0:T(8,128)(2,1)} custom-call(bf16[6,512]{1,0:T(8,128)(2,1)} %bitcast.16), custom_call_target="tpu_custom_call" | custom-call | tf_op jit(solution)/shard_map/pallas_call | solution.py:1021
  2.1 7.3 %all-to-all-start = ((bf16[32,24,128]{2,1,0:T(8,128)(2,1)}), bf16[32,24,128]{2,1,0:T(8,128)(2,1)S(1)}, u32[]{:S(2)}, u32[]{:S(2)}) async-start(bf16[32,24,128]{2,1,0:T(8,128)(2,1)} %shard_map.188), calls=%async_computation | async-start | bytes 393216 | tf_op jit(solution)/shard_map/all_to_all | solution.py:1045
  9.4 1.8 %collective-permute-start = (s32[1,8,6]{2,1,0:T(8,128)}, s32[1,8,6]{2,1,0:T(8,128)S(1)}, u32[]{:S(2)}, u32[]{:S(2)}) collective-permute-start(s32[1,8,6]{2,1,0:T(8,128)} %bitcast.13), channel_id=1, source_target_pairs={{0,2},{1,3},{2,0},{3,1},{4,6},{5,7},{6,4},{7,5},{8,10},{9,11},{10,... | collective-permute-start | bytes 584 | tf_op jit(solution)/shard_map/ppermute | solution.py:849
  11.2 2.2 %collective-permute-done.refs_1_ = s32[1,8,6]{2,1,0:T(8,128)S(1)} collective-permute-done((s32[1,8,6]{2,1,0:T(8,128)}, s32[1,8,6]{2,1,0:T(8,128)S(1)}, u32[]{:S(2)}, u32[]{:S(2)}) %collective-permute-start) | collective-permute-done | bytes 224 | tf_op jit(solution)/shard_map/ppermute | solution.py:849
  14.1 2.3 %shard_map.187 = (bf16[2,64,512]{2,1,0:T(8,128)(2,1)S(1)}, bf16[512,512]{1,0:T(8,128)(2,1)S(1)}, f32[1,512]{1,0:T(1,128)}, bf16[512,512]{1,0:T(8,128)(2,1)S(1)},...) custom-call(bf16[2,64,512]{2,1,0:T(8,128)(2,1)} %refs_0_.1, ...), custom_call_target="tpu_custom_call" | custom-call | tf_op jit(solution)/shard_map/pallas_call | solution.py:1034
  18.2 7.4 %shard_map.190 = (f32[12,256,1024]{2,1,0:T(8,128)S(1)}, f32[48,512]{1,0:T(8,128)}, f32[1344,128]{1,0:T(8,128)S(1)}, f32[1344,128]{1,0:T(8,128)S(1)}, f32[12,256,...) custom-call(bf16[32,24,128]{2,1,0:T(8,128)(2,1)S(1)} %all-to-all-done.ref, ...), custom_call_target="tpu_custom_call" | custom-call | tf_op jit(solution)/shard_map/pallas_call | solution.py:894
  25.8 4.6 %collective-permute-done.2.refs_11_ = f32[1,1,24,128]{3,2,1,0:T(8,128)S(1)} collective-permute-done((f32[1,1,24,128]{3,2,1,0:T(8,128)S(1)}, f32[1,1,24,128]{3,2,1,0:T(8,128)S(1)}, u32[]{:S(2)}, u32[]{:S(2)}) %collective-permute-start.2) | collective-permute-done | bytes 12320 | tf_op jit(solution)/shard_map/ppermute | solution.py:849
  31.4 2.8 %collective-permute-done.3.refs_12_ = f32[2,1,24,128]{3,2,1,0:T(8,128)S(1)} collective-permute-done((f32[2,1,24,128]{3,2,1,0:T(8,128)S(1)}, f32[2,1,24,128]{3,2,1,0:T(8,128)S(1)}, u32[]{:S(2)}, u32[]{:S(2)}) %collective-permute-start.3) | collective-permute-done | bytes 24608 | tf_op jit(solution)/shard_map/ppermute | solution.py:849
  35.1 1.2 %shard_map.191.refs_7_ = bf16[12,528,256]{2,1,0:T(8,128)(2,1)S(1)} custom-call(s32[1,8]{1,0:T(1,128)S(1)} %get-tuple-element.69.refs_1_.refs_0_, s32[1,8]{1,0:T(1,128)S(1)} %get-tuple-element.70.refs_2_.refs_1_, f32[12,256,512]{2,1,0:T(8,128)S(1)} %get-tuple-element.80.refs_2_.refs_3_), custom_call_target="tpu_custom_call" | custom-call | tf_op jit(solution)/shard_map/pallas_call | solution.py:894
  36.4 1.9 %collective-permute-done.4.refs_13_ = f32[4,1,24,128]{3,2,1,0:T(8,128)S(1)} collective-permute-done((f32[4,1,24,128]{3,2,1,0:T(8,128)S(1)}, f32[4,1,24,128]{3,2,1,0:T(8,128)S(1)}, u32[]{:S(2)}, u32[]{:S(2)}) %collective-permute-start.4) | collective-permute-done | bytes 49184 | tf_op jit(solution)/shard_map/ppermute | solution.py:849
  38.3 7.9 %shard_map.192 = (bf16[12,256,1024]{2,1,0:T(8,128)(2,1)S(1)}, f32[1,1024]{1,0:T(1,128)S(1)}, f32[1,128]{1,0:T(1,128)S(1)}, f32[2048,128]{1,0:T(8,128)S(1)}, f32[2048,128]{1,0:T(8,128)S(1)}) custom-call(s32[1,8]{1,0:T(1,128)S(1)} %get-tuple-element.69.refs_1_.refs_0_, s32[1,8]{1,0:T(1,128)S(1)} %get-tuple-element.70.refs_2_.refs_1_, ...), custom_call_target="tpu_custom_call" | custom-call | tf_op jit(solution)/shard_map/pallas_call | solution.py:894
  46.2 5.0 %shard_map.195 = (bf16[128,512]{1,0:T(8,128)(2,1)S(1)}, f32[16,128]{1,0:T(8,128)S(1)}, f32[1408,128]{1,0:T(8,128)S(1)}, f32[1424,128]{1,0:T(8,128)S(1)}) custom-call(s32[1,8]{1,0:T(1,128)S(1)} %get-tuple-element.69.refs_1_.refs_0_, s32[1,8]{1,0:T(1,128)S(1)} %get-tuple-element.70.refs_2_.refs_1_, bf16[12,256,1024]{2,1,0:T(8,128)(2,1)S(1)} %get-tuple-element.90.refs_2_, ...), custom_call_target="tpu_custom_call" | custom-call | tf_op jit(solution)/shard_map/pallas_call | solution.py:894
  53.7 1.1 %collective-permute-start.9 = (bf16[752,128]{1,0:T(8,128)(2,1)S(1)}, bf16[752,128]{1,0:T(8,128)(2,1)S(1)}, u32[]{:S(2)}, u32[]{:S(2)}) collective-permute-start(bf16[752,128]{1,0:T(8,128)(2,1)S(1)} %get-tuple-element.98), channel_id=1, source_target_pairs={{0,8},{1,3},{2,10},{3,1},{4,12},{5,7},{6,14},{7,5},{8,0},{9,11},{1... | collective-permute-start | bytes 577544 | tf_op jit(solution)/shard_map/ppermute | solution.py:849
  54.8 3.2 %collective-permute-done.6.refs_1_ = bf16[1024,128]{1,0:T(8,128)(2,1)S(1)} collective-permute-done((bf16[1024,128]{1,0:T(8,128)(2,1)S(1)}, bf16[1024,128]{1,0:T(8,128)(2,1)S(1)}, u32[]{:S(2)}, u32[]{:S(2)}) %collective-permute-start.6) | collective-permute-done | bytes 262176 | tf_op jit(solution)/shard_map/ppermute | solution.py:849
  58.1 1.3 %collective-permute-done.9.refs_1_ = bf16[752,128]{1,0:T(8,128)(2,1)S(1)} collective-permute-done((bf16[752,128]{1,0:T(8,128)(2,1)S(1)}, bf16[752,128]{1,0:T(8,128)(2,1)S(1)}, u32[]{:S(2)}, u32[]{:S(2)}) %collective-permute-start.9) | collective-permute-done | bytes 192544 | tf_op jit(solution)/shard_map/ppermute | solution.py:849
  60.4 3.7 %collective-permute-done.10.refs_3_ = bf16[400,128]{1,0:T(8,128)(2,1)S(1)} collective-permute-done((bf16[400,128]{1,0:T(8,128)(2,1)S(1)}, bf16[400,128]{1,0:T(8,128)(2,1)S(1)}, u32[]{:S(2)}, u32[]{:S(2)}) %collective-permute-start.10) | collective-permute-done | bytes 102432 | tf_op jit(solution)/shard_map/ppermute | solution.py:849
  66.0 3.9 %collective-permute-done.12.refs_3_ = f32[192,128]{1,0:T(8,128)S(1)} collective-permute-done((f32[192,128]{1,0:T(8,128)S(1)}, f32[192,128]{1,0:T(8,128)S(1)}, u32[]{:S(2)}, u32[]{:S(2)}) %collective-permute-start.12) | collective-permute-done | bytes 98336 | tf_op jit(solution)/shard_map/ppermute | solution.py:849
  71.0 8.5 %collective-permute-done.13.other_ref = bf16[656,128]{1,0:T(8,128)(2,1)S(1)} collective-permute-done((bf16[656,128]{1,0:T(8,128)(2,1)S(1)}, bf16[656,128]{1,0:T(8,128)(2,1)S(1)}, u32[]{:S(2)}, u32[]{:S(2)}) %collective-permute-start.13) | collective-permute-done | bytes 167968 | tf_op jit(solution)/shard_map/ppermute | solution.py:849
  79.7 4.0 %collective-permute-done.15.refs_3_ = bf16[176,128]{1,0:T(8,128)(2,1)S(1)} collective-permute-done((bf16[176,128]{1,0:T(8,128)(2,1)S(1)}, bf16[176,128]{1,0:T(8,128)(2,1)S(1)}, u32[]{:S(2)}, u32[]{:S(2)}) %collective-permute-start.15) | collective-permute-done | bytes 45088 | tf_op jit(solution)/shard_map/ppermute | solution.py:849
  84.9 3.7 %collective-permute-done.17.refs_3_ = bf16[352,128]{1,0:T(8,128)(2,1)S(1)} collective-permute-done((bf16[352,128]{1,0:T(8,128)(2,1)S(1)}, bf16[352,128]{1,0:T(8,128)(2,1)S(1)}, u32[]{:S(2)}, u32[]{:S(2)}) %collective-permute-start.17) | collective-permute-done | bytes 90144 | tf_op jit(solution)/shard_map/ppermute | solution.py:849
  89.9 1.8 %collective-permute-start.20 = (bf16[704,128]{1,0:T(8,128)(2,1)S(1)}, bf16[704,128]{1,0:T(8,128)(2,1)S(1)}, u32[]{:S(2)}, u32[]{:S(2)}) collective-permute-start(bf16[704,128]{1,0:T(8,128)(2,1)S(1)} %get-tuple-element.117.refs_0_), channel_id=1, source_target_pairs={{0,8},{1,3},{2,10},{3,1},{4,12},{5,7},{6,14},{7,5},{8,0},{9,11},{1... | collective-permute-start | bytes 540680 | tf_op jit(solution)/shard_map/ppermute | solution.py:849
  91.7 3.8 %collective-permute-done.18.refs_1_ = bf16[1024,128]{1,0:T(8,128)(2,1)S(1)} collective-permute-done((bf16[1024,128]{1,0:T(8,128)(2,1)S(1)}, bf16[1024,128]{1,0:T(8,128)(2,1)S(1)}, u32[]{:S(2)}, u32[]{:S(2)}) %collective-permute-start.18) | collective-permute-done | bytes 262176 | tf_op jit(solution)/shard_map/ppermute | solution.py:849
  96.2 1.3 %shard_map.206 = (f32[512,1024]{1,0:T(8,128)}, f32[512,512]{1,0:T(8,128)}) custom-call(bf16[2048,128]{1,0:T(8,128)(2,1)S(1)} %shard_map.204.refs_0_, bf16[1408,128]{1,0:T(8,128)(2,1)S(1)} %shard_map.205.refs_1_.rest_own_ref), custom_call_target="tpu_custom_call" | custom-call | tf_op jit(solution)/shard_map/pallas_call | solution.py:894
  98.0 2.3 %shard_map.207 = (f32[512,1024]{1,0:T(8,128)}, f32[512,512]{1,0:T(8,128)}, f32[512,512]{1,0:T(8,128)}, f32[1,1024]{1,0:T(1,128)}, f32[1,512]{1,0:T(1,128)}, /*in...) custom-call(bf16[2048,128]{1,0:T(8,128)(2,1)S(1)} %collective-permute-don, ...), custom_call_target="tpu_custom_call", output_to_operand_aliasing={{0}: (6, {}), {1}: (7, {})} | custom-call | tf_op jit(solution)/shard_map/pallas_call | solution.py:1218
  (48 shorter events, 14.9 us)
Async XLA Ops:
  2.1 16.2 %all-to-all-start = ((bf16[32,24,128]{2,1,0:T(8,128)(2,1)}), bf16[32,24,128]{2,1,0:T(8,128)(2,1)S(1)}, u32[]{:S(2)}, u32[]{:S(2)}) async-start(bf16[32,24,128]{2,1,0:T(8,128)(2,1)} %shard_map.188), calls=%async_computation | async-start | bytes 393216 | tf_op jit(solution)/shard_map/all_to_all | solution.py:1045
  9.4 4.1 %collective-permute-start = (s32[1,8,6]{2,1,0:T(8,128)}, s32[1,8,6]{2,1,0:T(8,128)S(1)}, u32[]{:S(2)}, u32[]{:S(2)}) collective-permute-start(s32[1,8,6]{2,1,0:T(8,128)} %bitcast.13), channel_id=1, source_target_pairs={{0,2},{1,3},{2,0},{3,1},{4,6},{5,7},{6,4},{7,5},{8,10},{9,11},{10,... | collective-permute-start | bytes 584 | tf_op jit(solution)/shard_map/ppermute | solution.py:849
  14.1 2.3 %collective-permute-start.1 = (s32[2,8,6]{2,1,0:T(8,128)S(1)}, s32[2,8,6]{2,1,0:T(8,128)S(1)}, u32[]{:S(2)}, u32[]{:S(2)}) collective-permute-start(s32[2,8,6]{2,1,0:T(8,128)S(1)} %pad_add_fusion), channel_id=1, source_target_pairs={{0,1},{1,0},{2,3},{3,2},{4,5},{5,4},{6,7},{7,6},{8,9},{9,8},{10,11... | collective-permute-start | bytes 1160 | tf_op jit(solution)/shard_map/ppermute | solution.py:849
  16.5 0.7 copy-start
  25.7 4.7 %collective-permute-start.2 = (f32[1,1,24,128]{3,2,1,0:T(8,128)S(1)}, f32[1,1,24,128]{3,2,1,0:T(8,128)S(1)}, u32[]{:S(2)}, u32[]{:S(2)}) collective-permute-start(f32[1,1,24,128]{3,2,1,0:T(8,128)S(1)} %get-tuple-element.83.refs_10_), channel_id=1, source_target_pairs={{0,16},{1,17},{2,18},{3,19},{4,20},{5,21},{6,22},{7,23},{8,24},{9,... | collective-permute-start | bytes 36872 | tf_op jit(solution)/shard_map/ppermute | solution.py:849
  30.4 3.8 %collective-permute-start.3 = (f32[2,1,24,128]{3,2,1,0:T(8,128)S(1)}, f32[2,1,24,128]{3,2,1,0:T(8,128)S(1)}, u32[]{:S(2)}, u32[]{:S(2)}) collective-permute-start(f32[2,1,24,128]{3,2,1,0:T(8,128)S(1)} %pad_maximum_fusion.1), channel_id=1, source_target_pairs={{0,8},{1,9},{2,10},{3,11},{4,12},{5,13},{6,14},{7,15},{8,0},{9,1},... | collective-permute-start | bytes 73736 | tf_op jit(solution)/shard_map/ppermute | solution.py:849
  34.2 4.1 %collective-permute-start.4 = (f32[4,1,24,128]{3,2,1,0:T(8,128)S(1)}, f32[4,1,24,128]{3,2,1,0:T(8,128)S(1)}, u32[]{:S(2)}, u32[]{:S(2)}) collective-permute-start(f32[4,1,24,128]{3,2,1,0:T(8,128)S(1)} %pad_maximum_fusion), channel_id=1, source_target_pairs={{0,4},{1,5},{2,6},{3,7},{4,0},{5,1},{6,2},{7,3},{8,12},{9,13},{10,... | collective-permute-start | bytes 147464 | tf_op jit(solution)/shard_map/ppermute | solution.py:849
  46.2 5.2 %collective-permute-start.5 = (f32[2048,128]{1,0:T(8,128)S(1)}, f32[2048,128]{1,0:T(8,128)S(1)}, u32[]{:S(2)}, u32[]{:S(2)}) collective-permute-start(f32[2048,128]{1,0:T(8,128)S(1)} %get-tuple-element.85), channel_id=1, source_target_pairs={{0,1},{1,0},{2,3},{3,2},{4,5},{5,4},{6,7},{7,6},{8,9},{9,8},{10,11... | collective-permute-start | bytes 3145736 | tf_op jit(solution)/shard_map/ppermute | solution.py:849
  51.3 2.3 %collective-permute-start.8 = (f32[1424,128]{1,0:T(8,128)S(1)}, f32[1424,128]{1,0:T(8,128)S(1)}, u32[]{:S(2)}, u32[]{:S(2)}) collective-permute-start(f32[1424,128]{1,0:T(8,128)S(1)} %get-tuple-element.95), channel_id=1, source_target_pairs={{0,1},{1,0},{2,3},{3,2},{4,5},{5,4},{6,7},{7,6},{8,9},{9,8},{10,11... | collective-permute-start | bytes 2187272 | tf_op jit(solution)/shard_map/ppermute | solution.py:849
  51.5 6.4 %collective-permute-start.6 = (bf16[1024,128]{1,0:T(8,128)(2,1)S(1)}, bf16[1024,128]{1,0:T(8,128)(2,1)S(1)}, u32[]{:S(2)}, u32[]{:S(2)}) collective-permute-start(bf16[1024,128]{1,0:T(8,128)(2,1)S(1)} %get-tuple-element.87), channel_id=1, source_target_pairs={{0,4},{1,3},{2,6},{3,1},{4,0},{5,7},{6,2},{7,5},{8,12},{9,11},{10,... | collective-permute-start | bytes 786440 | tf_op jit(solution)/shard_map/ppermute | solution.py:849
  53.7 5.7 %collective-permute-start.9 = (bf16[752,128]{1,0:T(8,128)(2,1)S(1)}, bf16[752,128]{1,0:T(8,128)(2,1)S(1)}, u32[]{:S(2)}, u32[]{:S(2)}) collective-permute-start(bf16[752,128]{1,0:T(8,128)(2,1)S(1)} %get-tuple-element.98), channel_id=1, source_target_pairs={{0,8},{1,3},{2,10},{3,1},{4,12},{5,7},{6,14},{7,5},{8,0},{9,11},{1... | collective-permute-start | bytes 577544 | tf_op jit(solution)/shard_map/ppermute | solution.py:849
  58.0 6.2 %collective-permute-start.7 = (bf16[512,128]{1,0:T(8,128)(2,1)S(1)}, bf16[512,128]{1,0:T(8,128)(2,1)S(1)}, u32[]{:S(2)}, u32[]{:S(2)}) collective-permute-start(bf16[512,128]{1,0:T(8,128)(2,1)S(1)} %get-tuple-element.89), channel_id=1, source_target_pairs={{0,2},{1,9},{2,0},{3,11},{4,6},{5,13},{6,4},{7,15},{8,10},{9,1},{1... | collective-permute-start | bytes 393224 | tf_op jit(solution)/shard_map/ppermute | solution.py:849
  59.4 4.7 %collective-permute-start.10 = (bf16[400,128]{1,0:T(8,128)(2,1)S(1)}, bf16[400,128]{1,0:T(8,128)(2,1)S(1)}, u32[]{:S(2)}, u32[]{:S(2)}) collective-permute-start(bf16[400,128]{1,0:T(8,128)(2,1)S(1)} %get-tuple-element.101), channel_id=1, source_target_pairs={{0,4},{1,9},{2,6},{3,11},{4,0},{5,13},{6,2},{7,15},{8,12},{9,1},{1... | collective-permute-start | bytes 307208 | tf_op jit(solution)/shard_map/ppermute | solution.py:849
  64.2 5.7 %collective-permute-start.11 = (f32[256,128]{1,0:T(8,128)S(1)}, f32[256,128]{1,0:T(8,128)S(1)}, u32[]{:S(2)}, u32[]{:S(2)}) collective-permute-start(f32[256,128]{1,0:T(8,128)S(1)} %get-tuple-element.104), channel_id=1, source_target_pairs={{0,8},{1,5},{2,10},{3,7},{4,12},{5,1},{6,14},{7,3},{8,0},{9,13},{1... | collective-permute-start | bytes 393224 | tf_op jit(solution)/shard_map/ppermute | solution.py:849
  65.3 4.6 %collective-permute-start.12 = (f32[192,128]{1,0:T(8,128)S(1)}, f32[192,128]{1,0:T(8,128)S(1)}, u32[]{:S(2)}, u32[]{:S(2)}) collective-permute-start(f32[192,128]{1,0:T(8,128)S(1)} %get-tuple-element.106), channel_id=1, source_target_pairs={{0,2},{1,5},{2,0},{3,7},{4,6},{5,1},{6,4},{7,3},{8,10},{9,13},{10,... | collective-permute-start | bytes 294920 | tf_op jit(solution)/shard_map/ppermute | solution.py:849
  70.0 9.6 %collective-permute-start.13 = (bf16[656,128]{1,0:T(8,128)(2,1)S(1)}, bf16[656,128]{1,0:T(8,128)(2,1)S(1)}, u32[]{:S(2)}, u32[]{:S(2)}) collective-permute-start(bf16[656,128]{1,0:T(8,128)(2,1)S(1)} %get-tuple-element.108.own_ref), channel_id=1, source_target_pairs={{0,16},{1,17},{2,18},{3,19},{4,20},{5,21},{6,22},{7,23},{8,24},{9,... | collective-permute-start | bytes 503816 | tf_op jit(solution)/shard_map/ppermute | solution.py:849
  79.6 4.3 %collective-permute-start.14 = (bf16[256,128]{1,0:T(8,128)(2,1)S(1)}, bf16[256,128]{1,0:T(8,128)(2,1)S(1)}, u32[]{:S(2)}, u32[]{:S(2)}) collective-permute-start(bf16[256,128]{1,0:T(8,128)(2,1)S(1)} %get-tuple-element.112.refs_0_), channel_id=1, source_target_pairs={{0,8},{1,5},{2,10},{3,7},{4,12},{5,1},{6,14},{7,3},{8,0},{9,13},{1... | collective-permute-start | bytes 196616 | tf_op jit(solution)/shard_map/ppermute | solution.py:849
  79.6 4.1 %collective-permute-start.15 = (bf16[176,128]{1,0:T(8,128)(2,1)S(1)}, bf16[176,128]{1,0:T(8,128)(2,1)S(1)}, u32[]{:S(2)}, u32[]{:S(2)}) collective-permute-start(bf16[176,128]{1,0:T(8,128)(2,1)S(1)} %get-tuple-element.113.refs_2_), channel_id=1, source_target_pairs={{0,2},{1,5},{2,0},{3,7},{4,6},{5,1},{6,4},{7,3},{8,10},{9,13},{10,... | collective-permute-start | bytes 135176 | tf_op jit(solution)/shard_map/ppermute | solution.py:849
  83.9 5.0 %collective-permute-start.16 = (bf16[512,128]{1,0:T(8,128)(2,1)S(1)}, bf16[512,128]{1,0:T(8,128)(2,1)S(1)}, u32[]{:S(2)}, u32[]{:S(2)}) collective-permute-start(bf16[512,128]{1,0:T(8,128)(2,1)S(1)} %get-tuple-element.114.refs_0_), channel_id=1, source_target_pairs={{0,2},{1,9},{2,0},{3,11},{4,6},{5,13},{6,4},{7,15},{8,10},{9,1},{1... | collective-permute-start | bytes 393224 | tf_op jit(solution)/shard_map/ppermute | solution.py:849
  84.0 4.6 %collective-permute-start.17 = (bf16[352,128]{1,0:T(8,128)(2,1)S(1)}, bf16[352,128]{1,0:T(8,128)(2,1)S(1)}, u32[]{:S(2)}, u32[]{:S(2)}) collective-permute-start(bf16[352,128]{1,0:T(8,128)(2,1)S(1)} %get-tuple-element.115.refs_2_), channel_id=1, source_target_pairs={{0,4},{1,9},{2,6},{3,11},{4,0},{5,13},{6,2},{7,15},{8,12},{9,1},{1... | collective-permute-start | bytes 270344 | tf_op jit(solution)/shard_map/ppermute | solution.py:849
  89.0 6.4 %collective-permute-start.18 = (bf16[1024,128]{1,0:T(8,128)(2,1)S(1)}, bf16[1024,128]{1,0:T(8,128)(2,1)S(1)}, u32[]{:S(2)}, u32[]{:S(2)}) collective-permute-start(bf16[1024,128]{1,0:T(8,128)(2,1)S(1)} %get-tuple-element.116.refs_0_), channel_id=1, source_target_pairs={{0,4},{1,3},{2,6},{3,1},{4,0},{5,7},{6,2},{7,5},{8,12},{9,11},{10,... | collective-permute-start | bytes 786440 | tf_op jit(solution)/shard_map/ppermute | solution.py:849
  89.9 5.7 %collective-permute-start.20 = (bf16[704,128]{1,0:T(8,128)(2,1)S(1)}, bf16[704,128]{1,0:T(8,128)(2,1)S(1)}, u32[]{:S(2)}, u32[]{:S(2)}) collective-permute-start(bf16[704,128]{1,0:T(8,128)(2,1)S(1)} %get-tuple-element.117.refs_0_), channel_id=1, source_target_pairs={{0,8},{1,3},{2,10},{3,1},{4,12},{5,7},{6,14},{7,5},{8,0},{9,11},{1... | collective-permute-start | bytes 540680 | tf_op jit(solution)/shard_map/ppermute | solution.py:849
  95.5 2.5 %collective-permute-start.19 = (bf16[2048,128]{1,0:T(8,128)(2,1)S(1)}, bf16[2048,128]{1,0:T(8,128)(2,1)S(1)}, u32[]{:S(2)}, u32[]{:S(2)}) collective-permute-start(bf16[2048,128]{1,0:T(8,128)(2,1)S(1)} %shard_map.204.refs_0_), channel_id=1, source_target_pairs={{0,1},{1,0},{2,3},{3,2},{4,5},{5,4},{6,7},{7,6},{8,9},{9,8},{10,11... | collective-permute-start | bytes 1572872 | tf_op jit(solution)/shard_map/ppermute | solution.py:849
  95.6 2.4 %collective-permute-start.21 = (bf16[1408,128]{1,0:T(8,128)(2,1)S(1)}, bf16[1408,128]{1,0:T(8,128)(2,1)S(1)}, u32[]{:S(2)}, u32[]{:S(2)}) collective-permute-start(bf16[1408,128]{1,0:T(8,128)(2,1)S(1)} %shard_map.205.refs_1_.rest_own_ref), channel_id=1, source_target_pairs={{0,1},{1,0},{2,3},{3,2},{4,5},{5,4},{6,7},{7,6},{8,9},{9,8},{10,11... | collective-permute-start | bytes 1081352 | tf_op jit(solution)/shard_map/ppermute | solution.py:849
where the time goes:
time: 101 us; the launch traced here: 100 us
  waiting for transfers between devices  46.7 us (46%)
  Pallas kernels  30.6 us (30%)
  starting transfers between devices  20.7 us (20%)
  between operations  1.04 us (1%)
    ppermute x22, waiting for transfers between devices, permuted(): return lax.ppermute(array, AXES, pairs)  45.7 us
    pallas_call x17, Pallas kernels, call(): pl.pallas_call(kernel, in_specs=[vmem] * sum(there), out_specs=[pl.BlockS...  24.6 us
    ppermute x22, starting transfers between devices, permuted(): return lax.ppermute(array, AXES, pairs)  13.4 us
    all_to_all x1, starting transfers between devices, per_device(): packets = lax.all_to_all(packets, AXES, 0, 0, tiled=True)  7.3 us
    pallas_call x1, Pallas kernels, per_device(): pl.pallas_call(load_kernel, in_specs=[anywhere] * len(weights), out_specs...  2.32 us
    pallas_call x1, Pallas kernels, per_device(): pl.pallas_call(functools.partial(finish_kernel, layout), in_specs=[vmem]...  2.25 us
  transfers between devices with their start and end apart: 23, of which 17 were waited for; matrix products, arithmetic and copies ran while one was open for 1% of the time, Pallas kernels for 11%

commit v1 on v0

--- a/solution.py
+++ b/solution.py
@@ -28,15 +28,14 @@
     return jnp.maximum(a, b) + jnp.log2(1.0 + jnp.exp2(-jnp.abs(a - b)))
 
 
-def both_ways(blank_ref, label_ref, units, steps, ahead, behind, keep=None):
+def both_ways(blank_ref, label_ref, units, steps, ahead, behind, keep):
     def one_step(i, state):
         ahead, behind = state
         back = steps - 1 - i
         here = pl.ds(pl.multiple_of(i * units, 8), units)
         there = pl.ds(pl.multiple_of(back * units, 8), units)
-        if keep is not None:
-            keep[0][here, :] = ahead
-            keep[1][there, :] = behind
+        keep[0][here, :] = ahead
+        keep[1][there, :] = behind
         from_left = pltpu.roll(ahead + label_ref[here, :], 1, 0)
         to_right = pltpu.roll(behind, units - 1, 0) + label_ref[there, :]
         ahead = log2_add(ahead + blank_ref[here, :], from_left)
@@ -44,6 +43,49 @@
         return ahead, behind
 
     return lax.fori_loop(0, steps, one_step, (ahead, behind))
+
+
+def log2_add_three(a, b, c):
+    top = jnp.maximum(jnp.maximum(a, b), c)
+    return top + jnp.log2(jnp.exp2(a - top) + jnp.exp2(b - top) + jnp.exp2(c - top))
+
+
+def both_ways_in_pairs(blank_ref, label_ref, units, steps, ahead, behind):
+    pairs = -(-steps // 2)
+
+    def rows_of(ref, diagonal):
+        return ref[pl.ds(pl.multiple_of(diagonal * units, 8), units), :]
+
+    def up(array, by=1):
+        return pltpu.roll(array, by, 0)
+
+    def down(array, by=1):
+        return pltpu.roll(array, units - by, 0)
+
+    def scores_of(first):
+        return [rows_of(ref, first + n) for ref in (blank_ref, label_ref) for n in (0, 1)]
+
+    def ways_ahead(i):
+        blank, blank_next, label, label_next = scores_of(2 * i)
+        one = log2_add(up(blank + label_next), up(label) + blank_next)
+        return blank + blank_next, one, up(up(label) + label_next)
+
+    def ways_behind(i):
+        blank, blank_next, label, label_next = scores_of(2 * (pairs - 1 - i))
+        one = log2_add(blank + label_next, label + down(blank_next))
+        return blank + blank_next, one, label + down(label_next)
+
+    def one_pair(i, state):
+        ahead, behind, (none, one, two), (none_back, one_back, two_back) = state
+        following = jnp.minimum(i + 1, pairs - 1)
+        ahead = log2_add_three(ahead + none, up(ahead) + one, up(ahead, 2) + two)
+        behind = log2_add_three(
+            behind + none_back, down(behind) + one_back, down(behind, 2) + two_back
+        )
+        return ahead, behind, ways_ahead(following), ways_behind(following)
+
+    start = ahead, behind, ways_ahead(0), ways_behind(0)
+    return lax.fori_loop(0, pairs, one_pair, start)[:2]
 
 
 def in_two_stages(count, first, second, even, odd, between=None):
@@ -287,7 +329,7 @@
     eye = jnp.where(
         lane_ids(units) % GROUP == lax.broadcasted_iota(jnp.int32, (units, 128), 0), 0.0, NEG
     ).astype(F32)
-    ahead, behind = both_ways(blank_ref, label_ref, units, steps, eye, eye)
+    ahead, behind = both_ways_in_pairs(blank_ref, label_ref, units, steps, eye, eye)
     lanes = lane_ids(units)
     early = lanes < 64
     columns = jnp.where(early, behind, ahead)
@@ -342,7 +384,8 @@
         tangents_ref,
         output_bias_ref,
         loss_ref,
-        *kept_refs,
+        kept_ref,
+        sent_ref,
         sums_ref,
         matrices_ref,
         ahead_ref,
@@ -353,7 +396,6 @@
         odd_ref,
         labels_smem,
         label_sem,
-        sems,
     ) = refs
     label_copy = pltpu.make_async_copy(label_table_ref, labels_smem, label_sem)
     label_copy.start()
@@ -492,22 +534,14 @@
         output_bias_ref[...] += product[width : width + 1, :]
 
     in_two_stages(counts_all, prepare, multiply, even_ref, odd_ref)
-    part_halves(sums_ref, kept_refs, sems)
-
-
-def part_halves(sums_ref, piece_refs, sems):
+    part_halves(sums_ref, kept_ref, sent_ref)
+
+
+def part_halves(sums_ref, kept_ref, sent_ref):
+    half = kept_ref.shape[0]
     place = lax.axis_index("tokens") & 1
-    copies, start = [], 0
-    for kept_ref, sent_ref in zip(piece_refs[::2], piece_refs[1::2]):
-        half = kept_ref.shape[0]
-        for part, target in ((1 - place, sent_ref.at[:half, :]), (place, kept_ref)):
-            source = sums_ref.at[pl.ds(pl.multiple_of(start + part * half, 8), half), :]
-            copies.append(pltpu.make_async_copy(source, target, sems.at[len(copies)]))
-        start += 2 * half
-    for copy in copies:
-        copy.start()
-    for copy in copies:
-        copy.wait()
+    sent_ref[:half, :] = sums_ref[pl.ds(pl.multiple_of((1 - place) * half, 8), half), :]
+    kept_ref[...] = sums_ref[pl.ds(pl.multiple_of(place * half, 8), half), :]
 
 
 def inner_kernel(
@@ -530,7 +564,6 @@
     token_sum_ref,
     even_ref,
     odd_ref,
-    sems,
 ):
     seqs, frame_count, width = encoder_ref.shape
     units = token_sum_ref.shape[0] // seqs
@@ -607,7 +640,7 @@
         exact_ref[v : v + 1, :] = output_bias_ref[:, v * 128 : (v + 1) * 128]
     at = vocab // 128 + width // 128
     exact_ref[at : at + 1, :] = loss_ref[...]
-    part_halves(sums_ref, (kept_ref, sent_ref), sems)
+    part_halves(sums_ref, kept_ref, sent_ref)
     write_exact(sent_ref, kept_ref.shape[0], exact_ref[...])
 
 
@@ -735,9 +768,53 @@
     return copies
 
 
-def finish_own_kernel(output_ref, rest_ref, output_hbm, encoder_hbm, *scratch):
+def finish_own_kernel(
+    output_ref,
+    rest_ref,
+    exact_ref,
+    output_hbm,
+    encoder_hbm,
+    output_bias_hbm,
+    encoder_bias_hbm,
+    losses_hbm,
+    output_buffer,
+    encoder_buffer,
+    output_bias_ref,
+    encoder_bias_ref,
+    losses_ref,
+    sems,
+):
     place = lax.axis_index("tokens") & 1
-    for copy in copy_out(output_ref, rest_ref, place, output_hbm, encoder_hbm, *scratch):
+    copies = copy_out(
+        output_ref,
+        rest_ref,
+        place,
+        output_hbm,
+        encoder_hbm,
+        output_buffer,
+        encoder_buffer,
+        sems,
+    )
+
+    def rows(start, count):
+        return jnp.concatenate([exact_ref[start + n : start + n + 1, :] for n in range(count)], axis=1)
+
+    output_blocks, encoder_blocks = output_bias_ref.shape[1] // 128, encoder_bias_ref.shape[1] // 128
+    output_bias_ref[...] = rows(0, output_blocks)
+    encoder_bias_ref[...] = rows(output_blocks, encoder_blocks)
+    loss = rows(output_blocks + encoder_blocks, 1)
+    losses_ref[...] = jnp.sum(
+        jnp.where(lane_ids(1) == lax.axis_index("frames"), loss, 0.0), axis=1, keepdims=True
+    )
+    for source, target in (
+        (output_bias_ref, output_bias_hbm),
+        (encoder_bias_ref, encoder_bias_hbm),
+        (losses_ref, losses_hbm),
+    ):
+        copy = pltpu.make_async_copy(source, target, sems.at[len(copies)])
+        copy.start()
+        copies.append(copy)
+    for copy in copies:
         copy.wait()
 
 
@@ -748,26 +825,23 @@
     rest_other_ref,
     packets_ref,
     predictor_weight_ref,
-    exact_ref,
     output_weight_begun,
     encoder_weight_begun,
     output_weight_hbm,
     encoder_weight_hbm,
     weight_gradient_hbm,
-    output_bias_ref,
-    encoder_bias_ref,
-    bias_gradient_ref,
-    predictor_gradient_ref,
-    losses_ref,
+    bias_gradient_hbm,
+    predictor_gradient_hbm,
     output_buffer,
     encoder_buffer,
     weight_gradient_ref,
+    bias_gradient_ref,
+    predictor_gradient_ref,
     tokens_ref,
     predictor_ref,
     sems,
-    gradient_sem,
 ):
-    width, vocab = encoder_buffer.shape[0], output_bias_ref.shape[1]
+    width = encoder_buffer.shape[0]
     place = lax.axis_index("tokens") & 1
     copies = copy_out(
         output_other_ref,
@@ -795,23 +869,20 @@
     held_rows = packets_ref.shape[1] // (width // 128)
     for d in range(packets_ref.shape[0]):
         unpack_rows(packets_ref[d], predictor_ref, d * held_rows)
+    def send(source, target):
+        copy = pltpu.make_async_copy(source, target, sems.at[len(copies)])
+        copy.start()
+        copies.append(copy)
+
     weight_gradient_ref[...] = lax.dot_general(
         predictor_ref[...].astype(BF16),
         tokens.astype(BF16),
         (((0,), (0,)), ((), ())),
         preferred_element_type=F32,
     )
-    gradient_copy = pltpu.make_async_copy(weight_gradient_ref, weight_gradient_hbm, gradient_sem)
-    gradient_copy.start()
-
-    def row(n):
-        return exact_ref[n : n + 1, :]
-
-    output_bias_ref[...] = jnp.concatenate([row(v) for v in range(vocab // 128)], axis=1)
-    encoder_bias_ref[...] = jnp.concatenate(
-        [row(vocab // 128 + v) for v in range(width // 128)], axis=1
-    )
+    send(weight_gradient_ref, weight_gradient_hbm)
     bias_gradient_ref[...] = jnp.sum(tokens, axis=0, keepdims=True)
+    send(bias_gradient_ref, bias_gradient_hbm)
     device = lax.axis_index("frames") * lax.axis_size("tokens") + lax.axis_index("tokens")
     mine = jnp.concatenate(
         [tokens_ref[pl.ds(device * held_rows + r, 1), :] for r in range(held_rows)], axis=0
@@ -822,13 +893,9 @@
         (((1,), (1,)), ((), ())),
         preferred_element_type=F32,
     )
-    loss = row(vocab // 128 + width // 128)
-    losses_ref[...] = jnp.sum(
-        jnp.where(lane_ids(1) == lax.axis_index("frames"), loss, 0.0), axis=1, keepdims=True
-    )
+    send(predictor_gradient_ref, predictor_gradient_hbm)
     for copy in copies:
         copy.wait()
-    gradient_copy.wait()
 
 
 def in_hbm(array):
@@ -1136,7 +1203,6 @@
                 pltpu.VMEM((block_rows, vocab), BF16),
                 pltpu.SMEM((1, 128), jnp.int32),
                 pltpu.SemaphoreType.DMA,
-                pltpu.SemaphoreType.DMA((4,)),
             ],
             limit=12,
         )
@@ -1157,7 +1223,6 @@
                 pltpu.VMEM((2 * units, width), F32),
                 pltpu.VMEM((2 * block_rows, width), F32),
                 pltpu.VMEM((2 * block_rows, width), F32),
-                pltpu.SemaphoreType.DMA((2,)),
             ],
             limit=10,
         )
@@ -1208,51 +1273,54 @@
         pltpu.VMEM((width, vocab // 2), F32),
         pltpu.VMEM((width, width // 2), F32),
     ]
-    begun = call(
+    *begun, output_bias_gradient, encoder_bias_gradient, losses = call(
         finish_own_kernel,
-        (output_own, rest_own),
-        [((width, vocab), F32, None), ((width, width), F32, None)],
-        scratch=[*buffers, pltpu.SemaphoreType.DMA((2,))],
+        (output_own, rest_own, exact),
+        [
+            ((width, vocab), F32, None),
+            ((width, width), F32, None),
+            ((1, vocab), F32, None),
+            ((1, width), F32, None),
+            ((1, 1), F32, None),
+        ],
+        scratch=[
+            *buffers,
+            pltpu.VMEM((1, vocab), F32),
+            pltpu.VMEM((1, width), F32),
+            pltpu.VMEM((1, 1), F32),
+            pltpu.SemaphoreType.DMA((5,)),
+        ],
         limit=8,
     )
+    shapes = [(width, vocab), (width, width), (width, width), (1, width), (held_units, 1, width)]
     finished = pl.pallas_call(
         functools.partial(finish_kernel, layout),
-        in_specs=[vmem] * 6 + [anywhere] * 2,
-        out_specs=[anywhere] * 3 + [vmem] * 5,
-        out_shape=[
-            jax.ShapeDtypeStruct((width, vocab), F32),
-            jax.ShapeDtypeStruct((width, width), F32),
-            jax.ShapeDtypeStruct((width, width), F32),
-            jax.ShapeDtypeStruct((1, vocab), F32),
-            jax.ShapeDtypeStruct((1, width), F32),
-            jax.ShapeDtypeStruct((1, width), F32),
-            jax.ShapeDtypeStruct((held_units, 1, width), F32),
-            jax.ShapeDtypeStruct((1, 1), F32),
-        ],
-        input_output_aliases={6: 0, 7: 1},
+        in_specs=[vmem] * 5 + [anywhere] * 2,
+        out_specs=[anywhere] * len(shapes),
+        out_shape=[jax.ShapeDtypeStruct(shape, F32) for shape in shapes],
+        input_output_aliases={5: 0, 6: 1},
         scratch_shapes=[
             *buffers,
-            pltpu.VMEM((width, width), F32),
+            *(pltpu.VMEM(shape, F32) for shape in shapes[2:]),
             pltpu.VMEM((all_seqs * units, width), F32),
             pltpu.VMEM((all_seqs * units, width), F32),
-            pltpu.SemaphoreType.DMA((2,)),
-            pltpu.SemaphoreType.DMA,
+            pltpu.SemaphoreType.DMA((5,)),
         ],
         compiler_params=pltpu.CompilerParams(vmem_limit_bytes=20 * 2**20),
     )(
-        *map(in_vmem, (output_other, rest_own, rest_other, packets, weights[3], exact)),
+        *map(in_vmem, (output_other, rest_own, rest_other, packets, weights[3])),
         *map(in_hbm, begun),
     )
     return (
-        finished[7].reshape(1),
+        losses.reshape(1),
         encoder_gradient,
-        finished[6].transpose(1, 0, 2),
+        finished[4].transpose(1, 0, 2),
         finished[1],
-        finished[4].reshape(width),
+        encoder_bias_gradient.reshape(width),
         finished[2],
-        finished[5].reshape(width),
+        finished[3].reshape(width),
         finished[0],
-        finished[3].reshape(vocab),
+        output_bias_gradient.reshape(vocab),
     )
 
 

time: 101 us -> 97.8 us (0.968)
  starting transfers between devices: 20.7 us -> 30.3 us
  Pallas kernels: 30.6 us -> 21.6 us
  waiting for transfers between devices: 46.7 us -> 43.6 us
    ppermute x22, starting transfers between devices: 13.4 us -> 23 us  [permuted(): return lax.ppermute(array, AXES, pairs)]
    pallas_call x17, Pallas kernels: 24.6 us -> 16.1 us  [call(): pl.pallas_call(kernel, in_specs=[vmem] * sum(there), out_specs=[pl.BlockS...]
    ppermute x22, waiting for transfers between devices: 45.7 us -> 42.6 us  [permuted(): return lax.ppermute(array, AXES, pairs)]
  transfers between devices with their start and end apart: 23 -> 23, of which waited for: 17 -> 15; matrix products, arithmetic and copies ran while one was open for 1% -> 1% of each run, Pallas kernels for 11% -> 9%
where the time goes in v1:
time: 97.8 us
  waiting for transfers between devices  43.6 us (45%)
  starting transfers between devices  30.3 us (31%)
  Pallas kernels  21.6 us (22%)
  between operations  0.98 us (1%)
    ppermute x22, waiting for transfers between devices, permuted(): return lax.ppermute(array, AXES, pairs)  42.6 us
    ppermute x22, starting transfers between devices, permuted(): return lax.ppermute(array, AXES, pairs)  23 us
    pallas_call x17, Pallas kernels, call(): pl.pallas_call(kernel, in_specs=[vmem] * sum(there), out_specs=[pl.BlockS...  16.1 us
    all_to_all x1, starting transfers between devices, per_device(): packets = lax.all_to_all(packets, AXES, 0, 0, tiled=True)  7.3 us
    pallas_call x1, Pallas kernels, per_device(): pl.pallas_call(load_kernel, in_specs=[anywhere] * len(weights), out_specs...  2.32 us
  transfers between devices with their start and end apart: 23, of which 15 were waited for; matrix products, arithmetic and copies ran while one was open for 1% of the time, Pallas kernels for 9%

profile of v1, /device:TPU:0, one launch (start us, length us, event | category | flops | bytes accessed | tf_op | source)
XLA Modules:
  0.0 97.8 jit_solution(2485887042111838653)
XLA Ops:
  0.6 1.4 %shard_map.188 = bf16[32,24,128]{2,1,0:T(8,128)(2,1)} custom-call(bf16[6,512]{1,0:T(8,128)(2,1)} %bitcast.16), custom_call_target="tpu_custom_call" | custom-call | tf_op jit(solution)/shard_map/pallas_call | solution.py:1088
  2.1 7.3 %all-to-all-start = ((bf16[32,24,128]{2,1,0:T(8,128)(2,1)}), bf16[32,24,128]{2,1,0:T(8,128)(2,1)S(1)}, u32[]{:S(2)}, u32[]{:S(2)}) async-start(bf16[32,24,128]{2,1,0:T(8,128)(2,1)} %shard_map.188), calls=%async_computation | async-start | bytes 393216 | tf_op jit(solution)/shard_map/all_to_all | solution.py:1112
  9.4 1.8 %collective-permute-start = (s32[1,8,6]{2,1,0:T(8,128)}, s32[1,8,6]{2,1,0:T(8,128)S(1)}, u32[]{:S(2)}, u32[]{:S(2)}) collective-permute-start(s32[1,8,6]{2,1,0:T(8,128)} %bitcast.13), channel_id=1, source_target_pairs={{0,2},{1,3},{2,0},{3,1},{4,6},{5,7},{6,4},{7,5},{8,10},{9,11},{10,... | collective-permute-start | bytes 584 | tf_op jit(solution)/shard_map/ppermute | solution.py:916
  11.2 2.2 %collective-permute-done.refs_1_ = s32[1,8,6]{2,1,0:T(8,128)S(1)} collective-permute-done((s32[1,8,6]{2,1,0:T(8,128)}, s32[1,8,6]{2,1,0:T(8,128)S(1)}, u32[]{:S(2)}, u32[]{:S(2)}) %collective-permute-start) | collective-permute-done | bytes 224 | tf_op jit(solution)/shard_map/ppermute | solution.py:916
  14.1 2.3 %shard_map.187 = (bf16[2,64,512]{2,1,0:T(8,128)(2,1)S(1)}, bf16[512,512]{1,0:T(8,128)(2,1)S(1)}, f32[1,512]{1,0:T(1,128)}, bf16[512,512]{1,0:T(8,128)(2,1)S(1)},...) custom-call(bf16[2,64,512]{2,1,0:T(8,128)(2,1)} %refs_0_.1, ...), custom_call_target="tpu_custom_call" | custom-call | tf_op jit(solution)/shard_map/pallas_call | solution.py:1101
  18.2 4.5 %shard_map.190 = (f32[12,256,1024]{2,1,0:T(8,128)S(1)}, f32[48,512]{1,0:T(8,128)}, f32[1344,128]{1,0:T(8,128)S(1)}, f32[1344,128]{1,0:T(8,128)S(1)}, f32[12,256,...) custom-call(bf16[32,24,128]{2,1,0:T(8,128)(2,1)S(1)} %all-to-all-done.ref, ...), custom_call_target="tpu_custom_call" | custom-call | tf_op jit(solution)/shard_map/pallas_call | solution.py:961
  22.8 4.6 %collective-permute-done.2.refs_11_ = f32[1,1,24,128]{3,2,1,0:T(8,128)S(1)} collective-permute-done((f32[1,1,24,128]{3,2,1,0:T(8,128)S(1)}, f32[1,1,24,128]{3,2,1,0:T(8,128)S(1)}, u32[]{:S(2)}, u32[]{:S(2)}) %collective-permute-start.2) | collective-permute-done | bytes 12320 | tf_op jit(solution)/shard_map/ppermute | solution.py:916
  27.4 4.0 %collective-permute-done.3.refs_12_ = f32[2,1,24,128]{3,2,1,0:T(8,128)S(1)} collective-permute-done((f32[2,1,24,128]{3,2,1,0:T(8,128)S(1)}, f32[2,1,24,128]{3,2,1,0:T(8,128)S(1)}, u32[]{:S(2)}, u32[]{:S(2)}) %collective-permute-start.3) | collective-permute-done | bytes 24608 | tf_op jit(solution)/shard_map/ppermute | solution.py:916
  32.8 2.7 %collective-permute-done.4.refs_13_ = f32[4,1,24,128]{3,2,1,0:T(8,128)S(1)} collective-permute-done((f32[4,1,24,128]{3,2,1,0:T(8,128)S(1)}, f32[4,1,24,128]{3,2,1,0:T(8,128)S(1)}, u32[]{:S(2)}, u32[]{:S(2)}) %collective-permute-start.4) | collective-permute-done | bytes 49184 | tf_op jit(solution)/shard_map/ppermute | solution.py:916
  35.5 5.4 %shard_map.192 = (bf16[12,256,1024]{2,1,0:T(8,128)(2,1)S(1)}, f32[1,1024]{1,0:T(1,128)S(1)}, f32[1,128]{1,0:T(1,128)S(1)}, f32[2048,128]{1,0:T(8,128)S(1)}, f32[2048,128]{1,0:T(8,128)S(1)}) custom-call(s32[1,8]{1,0:T(1,128)S(1)} %get-tuple-element.69.refs_1_.refs_0_, s32[1,8]{1,0:T(1,128)S(1)} %get-tuple-element.70.refs_2_.refs_1_, ...), custom_call_target="tpu_custom_call" | custom-call | tf_op jit(solution)/shard_map/pallas_call | solution.py:961
  41.4 2.6 %shard_map.195 = (bf16[128,512]{1,0:T(8,128)(2,1)S(1)}, f32[16,128]{1,0:T(8,128)S(1)}, f32[1408,128]{1,0:T(8,128)S(1)}, f32[1424,128]{1,0:T(8,128)S(1)}) custom-call(s32[1,8]{1,0:T(1,128)S(1)} %get-tuple-element.69.refs_1_.refs_0_, s32[1,8]{1,0:T(1,128)S(1)} %get-tuple-element.70.refs_2_.refs_1_, bf16[12,256,1024]{2,1,0:T(8,128)(2,1)S(1)} %get-tuple-element.90.refs_2_, ...), custom_call_target="tpu_custom_call" | custom-call | tf_op jit(solution)/shard_map/pallas_call | solution.py:961
  47.5 4.4 %collective-permute-done.6.refs_1_ = bf16[1024,128]{1,0:T(8,128)(2,1)S(1)} collective-permute-done((bf16[1024,128]{1,0:T(8,128)(2,1)S(1)}, bf16[1024,128]{1,0:T(8,128)(2,1)S(1)}, u32[]{:S(2)}, u32[]{:S(2)}) %collective-permute-start.6) | collective-permute-done | bytes 262176 | tf_op jit(solution)/shard_map/ppermute | solution.py:916
  51.9 4.9 %collective-permute-start.7 = (bf16[512,128]{1,0:T(8,128)(2,1)S(1)}, bf16[512,128]{1,0:T(8,128)(2,1)S(1)}, u32[]{:S(2)}, u32[]{:S(2)}) collective-permute-start(bf16[512,128]{1,0:T(8,128)(2,1)S(1)} %get-tuple-element.89), channel_id=1, source_target_pairs={{0,2},{1,9},{2,0},{3,11},{4,6},{5,13},{6,4},{7,15},{8,10},{9,1},{1... | collective-permute-start | bytes 393224 | tf_op jit(solution)/shard_map/ppermute | solution.py:916
  56.9 1.4 %collective-permute-start.10 = (bf16[400,128]{1,0:T(8,128)(2,1)S(1)}, bf16[400,128]{1,0:T(8,128)(2,1)S(1)}, u32[]{:S(2)}, u32[]{:S(2)}) collective-permute-start(bf16[400,128]{1,0:T(8,128)(2,1)S(1)} %get-tuple-element.101), channel_id=1, source_target_pairs={{0,4},{1,9},{2,6},{3,11},{4,0},{5,13},{6,2},{7,15},{8,12},{9,1},{1... | collective-permute-start | bytes 307208 | tf_op jit(solution)/shard_map/ppermute | solution.py:916
  58.3 3.4 %collective-permute-done.10.refs_3_ = bf16[400,128]{1,0:T(8,128)(2,1)S(1)} collective-permute-done((bf16[400,128]{1,0:T(8,128)(2,1)S(1)}, bf16[400,128]{1,0:T(8,128)(2,1)S(1)}, u32[]{:S(2)}, u32[]{:S(2)}) %collective-permute-start.10) | collective-permute-done | bytes 102432 | tf_op jit(solution)/shard_map/ppermute | solution.py:916
  63.9 3.3 %collective-permute-done.12.refs_3_ = f32[192,128]{1,0:T(8,128)S(1)} collective-permute-done((f32[192,128]{1,0:T(8,128)S(1)}, f32[192,128]{1,0:T(8,128)S(1)}, u32[]{:S(2)}, u32[]{:S(2)}) %collective-permute-start.12) | collective-permute-done | bytes 98336 | tf_op jit(solution)/shard_map/ppermute | solution.py:916
  68.6 7.1 %collective-permute-done.13.other_ref = bf16[656,128]{1,0:T(8,128)(2,1)S(1)} collective-permute-done((bf16[656,128]{1,0:T(8,128)(2,1)S(1)}, bf16[656,128]{1,0:T(8,128)(2,1)S(1)}, u32[]{:S(2)}, u32[]{:S(2)}) %collective-permute-start.13) | collective-permute-done | bytes 167968 | tf_op jit(solution)/shard_map/ppermute | solution.py:916
  75.8 2.4 %collective-permute-start.15 = (bf16[176,128]{1,0:T(8,128)(2,1)S(1)}, bf16[176,128]{1,0:T(8,128)(2,1)S(1)}, u32[]{:S(2)}, u32[]{:S(2)}) collective-permute-start(bf16[176,128]{1,0:T(8,128)(2,1)S(1)} %get-tuple-element.113.refs_2_), channel_id=1, source_target_pairs={{0,2},{1,5},{2,0},{3,7},{4,6},{5,1},{6,4},{7,3},{8,10},{9,13},{10,... | collective-permute-start | bytes 135176 | tf_op jit(solution)/shard_map/ppermute | solution.py:916
  78.2 2.0 %collective-permute-done.15.refs_3_ = bf16[176,128]{1,0:T(8,128)(2,1)S(1)} collective-permute-done((bf16[176,128]{1,0:T(8,128)(2,1)S(1)}, bf16[176,128]{1,0:T(8,128)(2,1)S(1)}, u32[]{:S(2)}, u32[]{:S(2)}) %collective-permute-start.15) | collective-permute-done | bytes 45088 | tf_op jit(solution)/shard_map/ppermute | solution.py:916
  80.7 1.7 %collective-permute-start.16 = (bf16[512,128]{1,0:T(8,128)(2,1)S(1)}, bf16[512,128]{1,0:T(8,128)(2,1)S(1)}, u32[]{:S(2)}, u32[]{:S(2)}) collective-permute-start(bf16[512,128]{1,0:T(8,128)(2,1)S(1)} %get-tuple-element.114.refs_0_), channel_id=1, source_target_pairs={{0,2},{1,9},{2,0},{3,11},{4,6},{5,13},{6,4},{7,15},{8,10},{9,1},{1... | collective-permute-start | bytes 393224 | tf_op jit(solution)/shard_map/ppermute | solution.py:916
  83.5 3.5 %collective-permute-done.17.refs_3_ = bf16[352,128]{1,0:T(8,128)(2,1)S(1)} collective-permute-done((bf16[352,128]{1,0:T(8,128)(2,1)S(1)}, bf16[352,128]{1,0:T(8,128)(2,1)S(1)}, u32[]{:S(2)}, u32[]{:S(2)}) %collective-permute-start.17) | collective-permute-done | bytes 90144 | tf_op jit(solution)/shard_map/ppermute | solution.py:916
  88.1 1.8 %collective-permute-start.19 = (bf16[704,128]{1,0:T(8,128)(2,1)S(1)}, bf16[704,128]{1,0:T(8,128)(2,1)S(1)}, u32[]{:S(2)}, u32[]{:S(2)}) collective-permute-start(bf16[704,128]{1,0:T(8,128)(2,1)S(1)} %get-tuple-element.117.refs_0_), channel_id=1, source_target_pairs={{0,8},{1,3},{2,10},{3,1},{4,12},{5,7},{6,14},{7,5},{8,0},{9,11},{1... | collective-permute-start | bytes 540680 | tf_op jit(solution)/shard_map/ppermute | solution.py:916
  89.9 3.5 %collective-permute-done.18.refs_1_ = bf16[1024,128]{1,0:T(8,128)(2,1)S(1)} collective-permute-done((bf16[1024,128]{1,0:T(8,128)(2,1)S(1)}, bf16[1024,128]{1,0:T(8,128)(2,1)S(1)}, u32[]{:S(2)}, u32[]{:S(2)}) %collective-permute-start.18) | collective-permute-done | bytes 262176 | tf_op jit(solution)/shard_map/ppermute | solution.py:916
  96.0 1.7 %shard_map.207 = (f32[512,1024]{1,0:T(8,128)}, f32[512,512]{1,0:T(8,128)}, f32[512,512]{1,0:T(8,128)}, f32[1,512]{1,0:T(1,128)}, f32[6,1,512]{2,1,0:T(1,128)}) custom-call(bf16[2048,128]{1,0:T(8,128)(2,1)S(1)} %collective-permute-done.20.output_other_ref, ...), custom_call_target="tpu_custom_call", output_to_operand_aliasing={{0}: (5, {}), {1}: (6, {})} | custom-call | tf_op jit(solution)/shard_map/pallas_call | solution.py:1296
  (48 shorter events, 16.9 us)
Async XLA Ops:
  2.1 16.2 %all-to-all-start = ((bf16[32,24,128]{2,1,0:T(8,128)(2,1)}), bf16[32,24,128]{2,1,0:T(8,128)(2,1)S(1)}, u32[]{:S(2)}, u32[]{:S(2)}) async-start(bf16[32,24,128]{2,1,0:T(8,128)(2,1)} %shard_map.188), calls=%async_computation | async-start | bytes 393216 | tf_op jit(solution)/shard_map/all_to_all | solution.py:1112
  9.4 4.1 %collective-permute-start = (s32[1,8,6]{2,1,0:T(8,128)}, s32[1,8,6]{2,1,0:T(8,128)S(1)}, u32[]{:S(2)}, u32[]{:S(2)}) collective-permute-start(s32[1,8,6]{2,1,0:T(8,128)} %bitcast.13), channel_id=1, source_target_pairs={{0,2},{1,3},{2,0},{3,1},{4,6},{5,7},{6,4},{7,5},{8,10},{9,11},{10,... | collective-permute-start | bytes 584 | tf_op jit(solution)/shard_map/ppermute | solution.py:916
  14.1 2.3 %collective-permute-start.1 = (s32[2,8,6]{2,1,0:T(8,128)S(1)}, s32[2,8,6]{2,1,0:T(8,128)S(1)}, u32[]{:S(2)}, u32[]{:S(2)}) collective-permute-start(s32[2,8,6]{2,1,0:T(8,128)S(1)} %pad_add_fusion), channel_id=1, source_target_pairs={{0,1},{1,0},{2,3},{3,2},{4,5},{5,4},{6,7},{7,6},{8,9},{9,8},{10,11... | collective-permute-start | bytes 1160 | tf_op jit(solution)/shard_map/ppermute | solution.py:916
  16.5 0.7 copy-start
  22.8 4.7 %collective-permute-start.2 = (f32[1,1,24,128]{3,2,1,0:T(8,128)S(1)}, f32[1,1,24,128]{3,2,1,0:T(8,128)S(1)}, u32[]{:S(2)}, u32[]{:S(2)}) collective-permute-start(f32[1,1,24,128]{3,2,1,0:T(8,128)S(1)} %get-tuple-element.83.refs_10_), channel_id=1, source_target_pairs={{0,16},{1,17},{2,18},{3,19},{4,20},{5,21},{6,22},{7,23},{8,24},{9,... | collective-permute-start | bytes 36872 | tf_op jit(solution)/shard_map/ppermute | solution.py:916
  27.4 4.0 %collective-permute-start.3 = (f32[2,1,24,128]{3,2,1,0:T(8,128)S(1)}, f32[2,1,24,128]{3,2,1,0:T(8,128)S(1)}, u32[]{:S(2)}, u32[]{:S(2)}) collective-permute-start(f32[2,1,24,128]{3,2,1,0:T(8,128)S(1)} %pad_maximum_fusion.1), channel_id=1, source_target_pairs={{0,8},{1,9},{2,10},{3,11},{4,12},{5,13},{6,14},{7,15},{8,0},{9,1},... | collective-permute-start | bytes 73736 | tf_op jit(solution)/shard_map/ppermute | solution.py:916
  31.4 4.1 %collective-permute-start.4 = (f32[4,1,24,128]{3,2,1,0:T(8,128)S(1)}, f32[4,1,24,128]{3,2,1,0:T(8,128)S(1)}, u32[]{:S(2)}, u32[]{:S(2)}) collective-permute-start(f32[4,1,24,128]{3,2,1,0:T(8,128)S(1)} %pad_maximum_fusion), channel_id=1, source_target_pairs={{0,4},{1,5},{2,6},{3,7},{4,0},{5,1},{6,2},{7,3},{8,12},{9,13},{10,... | collective-permute-start | bytes 147464 | tf_op jit(solution)/shard_map/ppermute | solution.py:916
  40.9 4.5 %collective-permute-start.5 = (f32[2048,128]{1,0:T(8,128)S(1)}, f32[2048,128]{1,0:T(8,128)S(1)}, u32[]{:S(2)}, u32[]{:S(2)}) collective-permute-start(f32[2048,128]{1,0:T(8,128)S(1)} %get-tuple-element.85), channel_id=1, source_target_pairs={{0,1},{1,0},{2,3},{3,2},{4,5},{5,4},{6,7},{7,6},{8,9},{9,8},{10,11... | collective-permute-start | bytes 3145736 | tf_op jit(solution)/shard_map/ppermute | solution.py:916
  44.1 3.1 %collective-permute-start.8 = (f32[1424,128]{1,0:T(8,128)S(1)}, f32[1424,128]{1,0:T(8,128)S(1)}, u32[]{:S(2)}, u32[]{:S(2)}) collective-permute-start(f32[1424,128]{1,0:T(8,128)S(1)} %get-tuple-element.95), channel_id=1, source_target_pairs={{0,1},{1,0},{2,3},{3,2},{4,5},{5,4},{6,7},{7,6},{8,9},{9,8},{10,11... | collective-permute-start | bytes 2187272 | tf_op jit(solution)/shard_map/ppermute | solution.py:916
  45.4 6.4 %collective-permute-start.6 = (bf16[1024,128]{1,0:T(8,128)(2,1)S(1)}, bf16[1024,128]{1,0:T(8,128)(2,1)S(1)}, u32[]{:S(2)}, u32[]{:S(2)}) collective-permute-start(bf16[1024,128]{1,0:T(8,128)(2,1)S(1)} %get-tuple-element.87), channel_id=1, source_target_pairs={{0,4},{1,3},{2,6},{3,1},{4,0},{5,7},{6,2},{7,5},{8,12},{9,11},{10,... | collective-permute-start | bytes 786440 | tf_op jit(solution)/shard_map/ppermute | solution.py:916
  47.3 9.6 %collective-permute-start.9 = (bf16[752,128]{1,0:T(8,128)(2,1)S(1)}, bf16[752,128]{1,0:T(8,128)(2,1)S(1)}, u32[]{:S(2)}, u32[]{:S(2)}) collective-permute-start(bf16[752,128]{1,0:T(8,128)(2,1)S(1)} %get-tuple-element.98), channel_id=1, source_target_pairs={{0,8},{1,3},{2,10},{3,1},{4,12},{5,7},{6,14},{7,5},{8,0},{9,11},{1... | collective-permute-start | bytes 577544 | tf_op jit(solution)/shard_map/ppermute | solution.py:916
  51.9 9.7 %collective-permute-start.7 = (bf16[512,128]{1,0:T(8,128)(2,1)S(1)}, bf16[512,128]{1,0:T(8,128)(2,1)S(1)}, u32[]{:S(2)}, u32[]{:S(2)}) collective-permute-start(bf16[512,128]{1,0:T(8,128)(2,1)S(1)} %get-tuple-element.89), channel_id=1, source_target_pairs={{0,2},{1,9},{2,0},{3,11},{4,6},{5,13},{6,4},{7,15},{8,10},{9,1},{1... | collective-permute-start | bytes 393224 | tf_op jit(solution)/shard_map/ppermute | solution.py:916
  56.9 4.7 %collective-permute-start.10 = (bf16[400,128]{1,0:T(8,128)(2,1)S(1)}, bf16[400,128]{1,0:T(8,128)(2,1)S(1)}, u32[]{:S(2)}, u32[]{:S(2)}) collective-permute-start(bf16[400,128]{1,0:T(8,128)(2,1)S(1)} %get-tuple-element.101), channel_id=1, source_target_pairs={{0,4},{1,9},{2,6},{3,11},{4,0},{5,13},{6,2},{7,15},{8,12},{9,1},{1... | collective-permute-start | bytes 307208 | tf_op jit(solution)/shard_map/ppermute | solution.py:916
  61.7 5.5 %collective-permute-start.11 = (f32[256,128]{1,0:T(8,128)S(1)}, f32[256,128]{1,0:T(8,128)S(1)}, u32[]{:S(2)}, u32[]{:S(2)}) collective-permute-start(f32[256,128]{1,0:T(8,128)S(1)} %get-tuple-element.104), channel_id=1, source_target_pairs={{0,8},{1,5},{2,10},{3,7},{4,12},{5,1},{6,14},{7,3},{8,0},{9,13},{1... | collective-permute-start | bytes 393224 | tf_op jit(solution)/shard_map/ppermute | solution.py:916
  62.6 4.6 %collective-permute-start.12 = (f32[192,128]{1,0:T(8,128)S(1)}, f32[192,128]{1,0:T(8,128)S(1)}, u32[]{:S(2)}, u32[]{:S(2)}) collective-permute-start(f32[192,128]{1,0:T(8,128)S(1)} %get-tuple-element.106), channel_id=1, source_target_pairs={{0,2},{1,5},{2,0},{3,7},{4,6},{5,1},{6,4},{7,3},{8,10},{9,13},{10,... | collective-permute-start | bytes 294920 | tf_op jit(solution)/shard_map/ppermute | solution.py:916
  67.3 8.4 %collective-permute-start.13 = (bf16[656,128]{1,0:T(8,128)(2,1)S(1)}, bf16[656,128]{1,0:T(8,128)(2,1)S(1)}, u32[]{:S(2)}, u32[]{:S(2)}) collective-permute-start(bf16[656,128]{1,0:T(8,128)(2,1)S(1)} %get-tuple-element.108.own_ref), channel_id=1, source_target_pairs={{0,16},{1,17},{2,18},{3,19},{4,20},{5,21},{6,22},{7,23},{8,24},{9,... | collective-permute-start | bytes 503816 | tf_op jit(solution)/shard_map/ppermute | solution.py:916
  75.7 5.0 %collective-permute-start.14 = (bf16[256,128]{1,0:T(8,128)(2,1)S(1)}, bf16[256,128]{1,0:T(8,128)(2,1)S(1)}, u32[]{:S(2)}, u32[]{:S(2)}) collective-permute-start(bf16[256,128]{1,0:T(8,128)(2,1)S(1)} %get-tuple-element.112.refs_0_), channel_id=1, source_target_pairs={{0,8},{1,5},{2,10},{3,7},{4,12},{5,1},{6,14},{7,3},{8,0},{9,13},{1... | collective-permute-start | bytes 196616 | tf_op jit(solution)/shard_map/ppermute | solution.py:916
  75.8 4.4 %collective-permute-start.15 = (bf16[176,128]{1,0:T(8,128)(2,1)S(1)}, bf16[176,128]{1,0:T(8,128)(2,1)S(1)}, u32[]{:S(2)}, u32[]{:S(2)}) collective-permute-start(bf16[176,128]{1,0:T(8,128)(2,1)S(1)} %get-tuple-element.113.refs_2_), channel_id=1, source_target_pairs={{0,2},{1,5},{2,0},{3,7},{4,6},{5,1},{6,4},{7,3},{8,10},{9,13},{10,... | collective-permute-start | bytes 135176 | tf_op jit(solution)/shard_map/ppermute | solution.py:916
  80.7 6.3 %collective-permute-start.16 = (bf16[512,128]{1,0:T(8,128)(2,1)S(1)}, bf16[512,128]{1,0:T(8,128)(2,1)S(1)}, u32[]{:S(2)}, u32[]{:S(2)}) collective-permute-start(bf16[512,128]{1,0:T(8,128)(2,1)S(1)} %get-tuple-element.114.refs_0_), channel_id=1, source_target_pairs={{0,2},{1,9},{2,0},{3,11},{4,6},{5,13},{6,4},{7,15},{8,10},{9,1},{1... | collective-permute-start | bytes 393224 | tf_op jit(solution)/shard_map/ppermute | solution.py:916
  82.4 4.5 %collective-permute-start.17 = (bf16[352,128]{1,0:T(8,128)(2,1)S(1)}, bf16[352,128]{1,0:T(8,128)(2,1)S(1)}, u32[]{:S(2)}, u32[]{:S(2)}) collective-permute-start(bf16[352,128]{1,0:T(8,128)(2,1)S(1)} %get-tuple-element.115.refs_2_), channel_id=1, source_target_pairs={{0,4},{1,9},{2,6},{3,11},{4,0},{5,13},{6,2},{7,15},{8,12},{9,1},{1... | collective-permute-start | bytes 270344 | tf_op jit(solution)/shard_map/ppermute | solution.py:916
  87.0 6.4 %collective-permute-start.18 = (bf16[1024,128]{1,0:T(8,128)(2,1)S(1)}, bf16[1024,128]{1,0:T(8,128)(2,1)S(1)}, u32[]{:S(2)}, u32[]{:S(2)}) collective-permute-start(bf16[1024,128]{1,0:T(8,128)(2,1)S(1)} %get-tuple-element.116.refs_0_), channel_id=1, source_target_pairs={{0,4},{1,3},{2,6},{3,1},{4,0},{5,7},{6,2},{7,5},{8,12},{9,11},{10,... | collective-permute-start | bytes 786440 | tf_op jit(solution)/shard_map/ppermute | solution.py:916
  88.1 5.5 %collective-permute-start.19 = (bf16[704,128]{1,0:T(8,128)(2,1)S(1)}, bf16[704,128]{1,0:T(8,128)(2,1)S(1)}, u32[]{:S(2)}, u32[]{:S(2)}) collective-permute-start(bf16[704,128]{1,0:T(8,128)(2,1)S(1)} %get-tuple-element.117.refs_0_), channel_id=1, source_target_pairs={{0,8},{1,3},{2,10},{3,1},{4,12},{5,7},{6,14},{7,5},{8,0},{9,11},{1... | collective-permute-start | bytes 540680 | tf_op jit(solution)/shard_map/ppermute | solution.py:916
  93.5 2.5 %collective-permute-start.20 = (bf16[2048,128]{1,0:T(8,128)(2,1)S(1)}, bf16[2048,128]{1,0:T(8,128)(2,1)S(1)}, u32[]{:S(2)}, u32[]{:S(2)}) collective-permute-start(bf16[2048,128]{1,0:T(8,128)(2,1)S(1)} %shard_map.204.refs_0_), channel_id=1, source_target_pairs={{0,1},{1,0},{2,3},{3,2},{4,5},{5,4},{6,7},{7,6},{8,9},{9,8},{10,11... | collective-permute-start | bytes 1572872 | tf_op jit(solution)/shard_map/ppermute | solution.py:916
  93.7 2.4 %collective-permute-start.21 = (bf16[1408,128]{1,0:T(8,128)(2,1)S(1)}, bf16[1408,128]{1,0:T(8,128)(2,1)S(1)}, u32[]{:S(2)}, u32[]{:S(2)}) collective-permute-start(bf16[1408,128]{1,0:T(8,128)(2,1)S(1)} %shard_map.205.refs_1_.rest_own_ref), channel_id=1, source_target_pairs={{0,1},{1,0},{2,3},{3,2},{4,5},{5,4},{6,7},{7,6},{8,9},{9,8},{10,11... | collective-permute-start | bytes 1081352 | tf_op jit(solution)/shard_map/ppermute | solution.py:916

commit v2 on v1

--- a/solution.py
+++ b/solution.py
@@ -130,6 +130,46 @@
     packet = packet_ref[...].astype(BF16)
     for d in range(packets_ref.shape[0]):
         packets_ref[d] = packet
+
+
+def label_packet_kernel(predictor_hbm, labels_hbm, packet_ref, predictor_ref, labels_ref, sems):
+    loads = [
+        pltpu.make_async_copy(predictor_hbm, predictor_ref, sems.at[0]),
+        pltpu.make_async_copy(labels_hbm, labels_ref, sems.at[1]),
+    ]
+    for load in loads:
+        load.start()
+    for load in loads:
+        load.wait()
+    seqs, units = labels_ref.shape
+    width = packet_ref.shape[2]
+    flat = jnp.zeros((1, width), F32)
+    for s in range(seqs):
+        row = labels_ref[s : s + 1, :].astype(F32)
+        row = jnp.concatenate([row, jnp.zeros((1, width - units), F32)], axis=1)
+        flat = flat + (pltpu.roll(row, s * units, 1) if s else row)
+    high = jnp.floor(flat * (1.0 / 32.0))
+    packet_ref[0] = jnp.concatenate(
+        [predictor_ref[...].astype(F32), high, flat - high * 32.0], axis=0
+    ).astype(BF16)
+
+
+def packet_table_kernel(places, *refs):
+    *packet_refs, table_ref = refs
+    first_seq = first_of(None, None)
+    held_units, width = packet_refs[0].shape[1] - 2, packet_refs[0].shape[2]
+    units = held_units * lax.axis_size("tokens")
+    lanes = lane_ids(1)
+    table = jnp.zeros((1, 128), F32)
+    for ref, n, f, k in sources_of(places, packet_refs):
+        halves = ref[n].astype(F32)[held_units:]
+        row = halves[:1] * 32.0 + halves[1:2]
+        for s in range(2):
+            start = s * units + k * held_units
+            shift = start - (first_seq + s) * held_units
+            shifted = pltpu.roll(row, jnp.where(shift < 0, shift + width, shift), 1)[:, :128]
+            table = jnp.where((lanes >= start) & (lanes < start + held_units), shifted, table)
+    table_ref[...] = table.astype(jnp.int32)
 
 
 def unpack_rows(packet, rows_ref, place):
@@ -163,17 +203,18 @@
 
 
 def load_kernel(*refs):
-    count = (len(refs) - 2) // 2
-    *loaded_refs, frame_ref, sems = refs[count:]
+    count = (len(refs) - 1) // 2
     loads = [
-        pltpu.make_async_copy(source, target, sems.at[n])
-        for n, (source, target) in enumerate(zip(refs[:count], loaded_refs))
+        pltpu.make_async_copy(source, target, refs[-1].at[n])
+        for n, (source, target) in enumerate(zip(refs[:count], refs[count:-1]))
     ]
     for load in loads:
         load.start()
     for load in loads:
         load.wait()
-    encoder_ref, weight_ref, bias_ref = loaded_refs[:3]
+
+
+def project_kernel(encoder_ref, weight_ref, bias_ref, frame_ref):
     frame_ref[...] = (
         (
             jnp.dot(
@@ -189,6 +230,35 @@
     )
 
 
+def stack_kernel(*refs):
+    at = 0
+    for ref in refs[:-1]:
+        refs[-1][at : at + ref.shape[0]] = ref[...]
+        at += ref.shape[0]
+
+
+def sources_of(places, refs):
+    f, k = lax.axis_index("frames"), lax.axis_index("tokens")
+    entries = [(ref, n) for ref in refs for n in range(ref.shape[0])]
+    return [(ref, n, f ^ (place >> 8), k ^ (place & 255)) for place, (ref, n) in zip(places, entries)]
+
+
+def predictor_kernel(places, *refs):
+    *packet_refs, predictor_ref, rows_ref = refs
+    if places is None:
+        held_rows = rows_ref.shape[0] // packet_refs[0].shape[0]
+        for d in range(packet_refs[0].shape[0]):
+            unpack_rows(packet_refs[0][d], rows_ref, d * held_rows)
+    else:
+        for ref, n, f, k in sources_of(places, packet_refs):
+            rows = ref[n].astype(F32)
+            count = rows.shape[0] - 2
+            start = (f * lax.axis_size("tokens") + k) * count
+            for r in range(count):
+                rows_ref[pl.ds(start + r, 1), :] = rows[r : r + 1]
+    predictor_ref[...] = rows_ref[...].astype(BF16)
+
+
 def entry(row_ref, place):
     row = row_ref[...].astype(F32)
     ids = lax.broadcasted_iota(jnp.int32, row.shape, 1)
@@ -200,8 +270,15 @@
 
 
 def first_of(seqs_here, offset_ref):
+    if seqs_here is None:
+        return lax.axis_index("frames") // 2 * 2
     first_seq = lax.axis_index("tokens") * seqs_here
     return first_seq if offset_ref is None else first_seq + whole_number(offset_ref, 0)
+
+
+def chunk_of(seqs_here):
+    f, k = lax.axis_index("frames"), lax.axis_index("tokens")
+    return f if seqs_here is not None else 2 * k + (f & 1)
 
 
 def block_counts(lens_ref, tokens_ref, first_seq, first_frame):
@@ -215,8 +292,8 @@
 
 def score_kernel(
     seqs_here,
+    packet_places,
     offset_ref,
-    packets_ref,
     lens_ref,
     tokens_ref,
     frame_ref,
@@ -225,19 +302,10 @@
     weight_ref,
     bias_ref,
     label_table_ref,
-    softmax_ref,
-    token_ref,
-    blank_ref,
-    label_ref,
-    hidden_ref,
-    inverse_ref,
-    parts_ref,
-    matrix_ref,
-    even_ref,
-    odd_ref,
-    labels_smem,
-    label_sem,
+    *refs,
 ):
+    *packet_refs, softmax_ref, token_ref, blank_ref, label_ref, hidden_ref, inverse_ref = refs[:-6]
+    parts_ref, matrix_ref, even_ref, odd_ref, labels_smem, label_sem = refs[-6:]
     label_copy = pltpu.make_async_copy(label_table_ref, labels_smem, label_sem)
     label_copy.start()
     seqs, frame_count, width = frame_ref.shape
@@ -246,15 +314,22 @@
     shard_units = units // shards
     part = frame_count // 2
     steps = part + units - 1
-    first_frame = lax.axis_index("frames") * frame_count
+    first_frame = chunk_of(seqs_here) * frame_count
     first_seq = first_of(seqs_here, offset_ref)
     vocab = weight_ref.shape[1]
     blank_ref[...] = jnp.zeros_like(blank_ref)
     label_ref[...] = jnp.full(label_ref.shape, NEG, F32)
-    for s in range(seqs):
-        for k in range(shards):
-            packet = packets_ref[(first_seq + s) * shards + k]
-            unpack_rows(packet, token_ref, s * units + k * shard_units)
+    if packet_places is None:
+        for s in range(seqs):
+            for k in range(shards):
+                packet = packet_refs[0][(first_seq + s) * shards + k]
+                unpack_rows(packet, token_ref, s * units + k * shard_units)
+    else:
+        for ref, n, f, k in sources_of(packet_places, packet_refs):
+            rows = ref[n].astype(F32)
+            start = (f & 1) * units + k * shard_units
+            for r in range(shard_units):
+                token_ref[pl.ds(start + r, 1), :] = rows[r : r + 1]
     token_ref[...] = (
         jnp.dot(token_ref[...].astype(BF16), predictor_weight_ref[...], preferred_element_type=F32)
         + predictor_bias_ref[...]
@@ -349,7 +424,7 @@
 
 def turn_kernel(layout, offset_ref, lens_ref, tokens_ref, hidden_ref, turned_ref):
     width = hidden_ref.shape[2]
-    first_frame = lax.axis_index("frames") * layout["frame_count"]
+    first_frame = chunk_of(layout["seqs_here"]) * layout["frame_count"]
     first_seq = first_of(layout["seqs_here"], offset_ref)
     counts = block_counts(lens_ref, tokens_ref, first_seq, first_frame)
 
@@ -404,7 +479,7 @@
     units = layout["units"]
     part = frame_count // 2
     steps = part + units - 1
-    here = lax.axis_index("frames")
+    here = chunk_of(layout["seqs_here"])
     first_frame = here * frame_count
     first_seq = first_of(layout["seqs_here"], offset_ref)
     chunks = matrices_ref.shape[0]
@@ -568,7 +643,7 @@
     seqs, frame_count, width = encoder_ref.shape
     units = token_sum_ref.shape[0] // seqs
     vocab = weight_ref.shape[1]
-    first_frame = lax.axis_index("frames") * frame_count
+    first_frame = chunk_of(layout["seqs_here"]) * frame_count
     first_seq = first_of(layout["seqs_here"], offset_ref)
     frame_sum_ref[...] = jnp.zeros_like(frame_sum_ref)
     token_sum_ref[...] = jnp.zeros_like(token_sum_ref)
@@ -644,7 +719,8 @@
     write_exact(sent_ref, kept_ref.shape[0], exact_ref[...])
 
 
-def encoder_kernel(frame_tangent_ref, encoder_weight_ref, encoder_gradient_ref):
+def encoder_kernel(frame_tangent_ref, encoder_weight_ref, encoder_gradient_ref, mark_ref):
+    mark_ref[...] = jnp.zeros_like(mark_ref)
     encoder_gradient_ref[...] = lax.dot_general(
         frame_tangent_ref[...],
         encoder_weight_ref[...],
@@ -704,7 +780,7 @@
 
 
 def add_kernel(count, *refs):
-    sum_ref, exact_sum_ref = refs[2 * count + 1 :]
+    sum_ref, exact_sum_ref = refs[-2:]
     at = 0
     for n in range(count):
         kept_ref, received_ref = refs[2 * n : 2 * n + 2]
@@ -719,7 +795,7 @@
     write_exact(sum_ref, at + rows, exact)
 
 
-def last_kernel(own_ref, other_ref, exact_ref, beside_ref, *sum_refs):
+def last_kernel(own_ref, other_ref, exact_ref, *sum_refs):
     *sum_refs, exact_sum_ref = sum_refs
     at = 0
     for n, sum_ref in enumerate(sum_refs):
@@ -737,7 +813,7 @@
 
 def join_kernel(stages, merged, *refs):
     count, at = len(stages), 0
-    joined_refs = refs[2:] if merged else refs[2 * count :]
+    joined_refs = refs[-count:]
     for n, (stage, joined_ref) in enumerate(zip(stages, joined_refs)):
         half = joined_ref.shape[0] // 2
         own, other = two_halves(stage, half)
@@ -823,7 +899,7 @@
     output_other_ref,
     rest_own_ref,
     rest_other_ref,
-    packets_ref,
+    predictor_ref,
     predictor_weight_ref,
     output_weight_begun,
     encoder_weight_begun,
@@ -838,7 +914,6 @@
     bias_gradient_ref,
     predictor_gradient_ref,
     tokens_ref,
-    predictor_ref,
     sems,
 ):
     width = encoder_buffer.shape[0]
@@ -866,16 +941,15 @@
     pl.when(place == 0)(lambda: gather_tokens(rest_own_ref, rest_other_ref))
     pl.when(place == 1)(lambda: gather_tokens(rest_other_ref, rest_own_ref))
     tokens = tokens_ref[...]
-    held_rows = packets_ref.shape[1] // (width // 128)
-    for d in range(packets_ref.shape[0]):
-        unpack_rows(packets_ref[d], predictor_ref, d * held_rows)
+    held_rows = predictor_gradient_ref.shape[0]
+
     def send(source, target):
         copy = pltpu.make_async_copy(source, target, sems.at[len(copies)])
         copy.start()
         copies.append(copy)
 
     weight_gradient_ref[...] = lax.dot_general(
-        predictor_ref[...].astype(BF16),
+        predictor_ref[...],
         tokens.astype(BF16),
         (((0,), (0,)), ((), ())),
         preferred_element_type=F32,
@@ -916,16 +990,27 @@
     return lax.ppermute(array, AXES, pairs)
 
 
-def doubled(array, axis):
-    blocks, places = [array], [[0]]
-    bit = lax.axis_size(axis) // 2
+def axis_flips(axis):
+    flips, bit = [], lax.axis_size(axis) // 2
     while bit:
-        joined = jnp.concatenate(blocks, axis=0) if len(blocks) > 1 else blocks[0]
-        flip = ((bit, 0), (bit, 0)) if axis == "frames" else ((0, bit), (0, bit))
-        blocks.append(permuted(joined, across(flip)))
-        places.append([place ^ bit for held in places for place in held])
+        flips.append(((bit, 0) if axis == "frames" else (0, bit), bit))
         bit //= 2
-    return blocks, [place for held in places for place in held]
+    return flips
+
+
+def stacked(blocks):
+    if len(blocks) == 1:
+        return blocks[0]
+    shape = (sum(block.shape[0] for block in blocks),) + blocks[0].shape[1:]
+    return call(stack_kernel, blocks, [(shape, blocks[0].dtype, True)])[0]
+
+
+def doubled(blocks, places, flips):
+    blocks, places = list(blocks), list(places)
+    for bits, mark in flips:
+        blocks.append(permuted(stacked(blocks), across((bits, bits))))
+        places += [place ^ mark for place in places]
+    return blocks, places
 
 
 def stages(even, odd):
@@ -973,7 +1058,7 @@
     )(*(in_vmem(array) for array in ins if array is not None))
 
 
-def reduced_and_gathered(pieces, exact, beside):
+def reduced_and_gathered(pieces, exact, beside, held):
     plans = list(zip(*(stages(*shifts) for shifts in ORDERS)))
     flat = [a for kept, sent in pieces for a in (kept, permuted(sent, neighbour))]
     way_back = []
@@ -1016,18 +1101,18 @@
     rows = sum(shape[0] for shape in shapes) + shapes[-1][0] + exact_rows(BF16)
     own, exact = call(
         functools.partial(add_kernel, len(shapes)),
-        [*flat, exact],
+        [*flat, exact, *beside],
         [((rows, 128), BF16, True), ((EXACT, 128), F32, True)],
     )
     other = permuted(own, across(last_plan[0]))
     vmem = pl.BlockSpec(memory_space=pltpu.VMEM)
     *arrays, exact = pl.pallas_call(
         last_kernel,
-        in_specs=[vmem, vmem, vmem, pl.BlockSpec(memory_space=pl.ANY)],
+        in_specs=[vmem, vmem, vmem],
         out_specs=[vmem] * (len(shapes) + 1),
         out_shape=[pltpu.VMEM(shape, BF16) for shape in shapes] + [pltpu.VMEM((EXACT, 128), F32)],
         compiler_params=pltpu.CompilerParams(vmem_limit_bytes=4 * 2**20),
-    )(in_vmem(own), in_vmem(other), in_vmem(exact), in_hbm(beside))
+    )(in_vmem(own), in_vmem(other), in_vmem(exact))
     for number, (plan, merged, sizes) in reversed(list(enumerate(way_back))):
         flat = [a for array, stage in zip(arrays, plan) for a in (array, permuted(array, across(stage)))]
         outs = [((size, 128), BF16, True) for size in sizes]
@@ -1041,7 +1126,8 @@
                 for n, stage in enumerate(plan)
             ]
         else:
-            arrays = call(functools.partial(join_kernel, plan, merged), flat, outs)
+            given = [*flat, *held] if number == 1 else flat
+            arrays = call(functools.partial(join_kernel, plan, merged), given, outs)
     return [(array, permuted(array, neighbour)) for array in arrays], exact
 
 
@@ -1072,8 +1158,12 @@
     vmem = pl.BlockSpec(memory_space=pltpu.VMEM)
     anywhere = pl.BlockSpec(memory_space=pl.ANY)
 
+    in_plane = seq_count == 2 and token_axis == 4 and frame_axis == 8
+
+    def turned_over(f, k):
+        return 2 * k + (f & 1), f >> 1
+
     weights = (
-        encoder_out,
         encoder_weight,
         encoder_bias.reshape(1, width),
         predictor_weight,
@@ -1084,32 +1174,54 @@
         token_lens.reshape(1, all_seqs),
         loss_scale.reshape(1, all_seqs),
     )
-    packet_rows = held_units * width // 128
-    packets = pl.pallas_call(
-        packet_kernel,
-        in_specs=[anywhere],
-        out_specs=vmem,
-        out_shape=jax.ShapeDtypeStruct((device_count, packet_rows, 128), BF16),
-        scratch_shapes=[
-            pltpu.VMEM((held_units, width), BF16),
-            pltpu.VMEM((packet_rows, 128), F32),
-            pltpu.SemaphoreType.DMA,
-        ],
-        compiler_params=pltpu.CompilerParams(vmem_limit_bytes=4 * 2**20),
-    )(in_hbm(predictor_out.reshape(held_units, width)))
-    label_blocks, label_places = doubled(labels[None], "tokens")
-    *weights, frames = pl.pallas_call(
+    if in_plane:
+        plane = [((0, 1), 1), ((1, 0), 256), ((0, 2), 2)]
+        encoder = permuted(encoder_out, turned_over)
+        packet = pl.pallas_call(
+            label_packet_kernel,
+            in_specs=[anywhere] * 2,
+            out_specs=vmem,
+            out_shape=pltpu.VMEM((1, held_units + 2, width), BF16),
+            scratch_shapes=[
+                pltpu.VMEM((held_units, width), BF16),
+                pltpu.VMEM(labels.shape, jnp.int32),
+                pltpu.SemaphoreType.DMA((2,)),
+            ],
+            compiler_params=pltpu.CompilerParams(vmem_limit_bytes=4 * 2**20),
+        )(in_hbm(predictor_out.reshape(held_units, width)), in_hbm(labels))
+        packets, packet_places = doubled([packet], [0], plane)
+        own_seqs = None
+    else:
+        packet_rows = held_units * width // 128
+        packets = pl.pallas_call(
+            packet_kernel,
+            in_specs=[anywhere],
+            out_specs=vmem,
+            out_shape=jax.ShapeDtypeStruct((device_count, packet_rows, 128), BF16),
+            scratch_shapes=[
+                pltpu.VMEM((held_units, width), BF16),
+                pltpu.VMEM((packet_rows, 128), F32),
+                pltpu.SemaphoreType.DMA,
+            ],
+            compiler_params=pltpu.CompilerParams(vmem_limit_bytes=4 * 2**20),
+        )(in_hbm(predictor_out.reshape(held_units, width)))
+        packets, packet_places = [lax.all_to_all(packets, AXES, 0, 0, tiled=True)], None
+        encoder, own_seqs = encoder_out, seq_count
+    if not in_plane:
+        label_blocks, label_places = doubled([labels[None]], [0], axis_flips("tokens"))
+    weights = pl.pallas_call(
         load_kernel,
         in_specs=[anywhere] * len(weights),
-        out_specs=[vmem] * (1 + len(weights)),
-        out_shape=[pltpu.VMEM(w.shape, w.dtype) for w in weights]
-        + [pltpu.VMEM(encoder_out.shape, F32)],
+        out_specs=[vmem] * len(weights),
+        out_shape=[pltpu.VMEM(w.shape, w.dtype) for w in weights],
         scratch_shapes=[pltpu.SemaphoreType.DMA((len(weights),))],
         compiler_params=pltpu.CompilerParams(vmem_limit_bytes=4 * 2**20),
     )(*map(in_hbm, weights))
     *weights, frame_lens, token_lens, loss_scale = weights
     lens = frame_lens, token_lens
-    packets = lax.all_to_all(packets, AXES, 0, 0, tiled=True)
+    (frames,) = call(
+        project_kernel, (encoder, weights[0], weights[1]), [(encoder_out.shape, F32, True)]
+    )
 
     score_shapes = [
         ((2 * units // SUB_UNITS, SUB_UNITS * frame_count, vocab), F32),
@@ -1123,14 +1235,15 @@
     ]
 
     def scores(offset, frames):
-        (table,) = call(
-            functools.partial(table_kernel, label_places, seq_count),
-            (offset, *label_blocks),
-            [((1, 128), jnp.int32, True)],
-        )
+        if in_plane:
+            body, given = functools.partial(packet_table_kernel, packet_places), packets
+        else:
+            body = functools.partial(table_kernel, label_places, own_seqs)
+            given = (offset, *label_blocks)
+        (table,) = call(body, given, [((1, 128), jnp.int32, True)])
         scored = call(
-            functools.partial(score_kernel, seq_count),
-            (offset, packets, *lens, frames, *weights[3:], table),
+            functools.partial(score_kernel, own_seqs, packet_places),
+            (offset, *lens, frames, *weights[2:], table, *packets),
             [(shape, kind, True) for shape, kind in score_shapes],
             scratch=[
                 pltpu.VMEM((SUB_UNITS * frame_count, vocab), F32),
@@ -1143,7 +1256,7 @@
         return [table, *scored]
 
     offsets = 2 * jnp.arange(calls, dtype=jnp.int32).reshape(calls, 1, 1)
-    encoders = weights[0].reshape(calls, 2, frame_count, width)
+    encoders = encoder.reshape(calls, 2, frame_count, width)
     if calls == 1:
         scored = scores(None, frames)
         matrix = scored[-1]
@@ -1154,8 +1267,20 @@
         )
         matrix = scored[-1].reshape(1, calls, units, 128)
 
-    matrices, matrix_places = doubled(matrix, "frames")
-    layout = {"matrix_places": matrix_places, "seqs_here": seq_count, "frame_count": frame_count, "units": units}
+    chunk_flips = [((0, 2), 4), ((1, 0), 1), ((0, 1), 2)] if in_plane else axis_flips("frames")
+    matrices, matrix_places = doubled([matrix], [0], chunk_flips)
+    if in_plane:
+        packets, packet_places = doubled(
+            [stacked(packets)], packet_places, [((4, 0), 1024), ((2, 0), 512)]
+        )
+    (predictor_all,) = call(
+        functools.partial(predictor_kernel, packet_places),
+        packets,
+        [((all_seqs * units, width), BF16, True)],
+        scratch=[pltpu.VMEM((all_seqs * units, width), F32)],
+        limit=8,
+    )
+    layout = {"matrix_places": matrix_places, "seqs_here": own_seqs, "frame_count": frame_count, "units": units}
     align = 16 * device_count // 4
     blocks_each = width // 128 // 2
     layout["token"], layout["token_rows"] = blocks_each * width, all_seqs * units
@@ -1210,7 +1335,10 @@
     def inners(offset, encoder, scored, tangent, output_bias_sum, loss):
         return call(
             functools.partial(inner_kernel, layout),
-            (offset, *lens, tangent, scored[5], weights[5], encoder, output_bias_sum, loss),
+            (
+                *(offset, *lens, tangent, scored[5], weights[4], encoder),
+                *(output_bias_sum, loss),
+            ),
             [
                 ((2 * frame_count, width), BF16, True),
                 ((EXACT, 128), F32, True),
@@ -1230,9 +1358,9 @@
     def encoder_gradient_of(frame_tangent):
         return call(
             encoder_kernel,
-            (frame_tangent, weights[1]),
-            [((2, frame_count, width), F32, False)],
-        )[0]
+            (frame_tangent, weights[0]),
+            [((2, frame_count, width), F32, False), ((8, 128), F32, True)],
+        )
 
     if calls == 1:
         scored = scored[:-1]
@@ -1240,10 +1368,13 @@
         tangent, output_bias_sum, loss, *output_sums = tangents(None, scored, turned, matrices)
 
         frame_tangent, exact, *rest = inners(
-            None, weights[0], scored, tangent, output_bias_sum, loss
+            None, encoder, scored, tangent, output_bias_sum, loss
         )
         sums = [*output_sums, *rest, exact]
-        encoder_gradient = encoder_gradient_of(frame_tangent)
+        if in_plane:
+            frame_tangent = permuted(frame_tangent, turned_over)
+        encoder_gradient, mark = encoder_gradient_of(frame_tangent)
+        beside, held = [frame_tangent], [predictor_all, mark]
     else:
 
         def add_call(sums, given):
@@ -1255,7 +1386,7 @@
                 offset, encoder, scored, tangent, output_bias_sum, loss
             )
             sums = [a + b for a, b in zip(sums, [*more, *rest, exact])]
-            return sums, encoder_gradient_of(frame_tangent)
+            return sums, encoder_gradient_of(frame_tangent)[0]
 
         sizes = (output_rows // 2,) * 2 + (rest_rows // 2, rest_rows // 2 + EXACT, EXACT)
         sums, encoder_gradient = lax.scan(
@@ -1264,9 +1395,10 @@
             (offsets, encoders, scored[:-1], jnp.arange(calls)),
         )
         encoder_gradient = encoder_gradient.reshape(encoder_out.shape)
+        beside, held = [], [predictor_all]
 
     halves, exact = reduced_and_gathered(
-        [sums[:2], sums[2:4]], sums[4], encoder_gradient
+        [sums[:2], sums[2:4]], sums[4], beside, held
     )
     (output_own, output_other), (rest_own, rest_other) = halves
     buffers = [
@@ -1303,12 +1435,11 @@
             *buffers,
             *(pltpu.VMEM(shape, F32) for shape in shapes[2:]),
             pltpu.VMEM((all_seqs * units, width), F32),
-            pltpu.VMEM((all_seqs * units, width), F32),
             pltpu.SemaphoreType.DMA((5,)),
         ],
         compiler_params=pltpu.CompilerParams(vmem_limit_bytes=20 * 2**20),
     )(
-        *map(in_vmem, (output_other, rest_own, rest_other, packets, weights[3])),
+        *map(in_vmem, (output_other, rest_own, rest_other, predictor_all, weights[2])),
         *map(in_hbm, begun),
     )
     return (

time: 97.8 us -> 95.6 us (0.978); the launches traced: 97.8 us -> 94.5 us
  waiting for transfers between devices: 43.6 us -> 37.2 us
  Pallas kernels: 21.6 us -> 25.5 us
    ppermute x22 -> x27, starting transfers between devices: 23 us -> 30.8 us  [permuted(): return lax.ppermute(array, AXES, pairs)]
    all_to_all x1 -> x0, starting transfers between devices: 7.3 us -> none  [per_device(): packets = lax.all_to_all(packets, AXES, 0, 0, tiled=True)]
    ppermute x22 -> x27, waiting for transfers between devices: 42.6 us -> 37.2 us  [permuted(): return lax.ppermute(array, AXES, pairs)]
    pallas_call x17 -> x25, Pallas kernels: 16.1 us -> 21.3 us  [call(): pl.pallas_call(kernel, in_specs=[vmem] * sum(there), out_specs=[pl.BlockS...]
    all_to_all x1 -> x0, waiting for transfers between devices: 1.01 us -> none  [per_device(): packets = lax.all_to_all(packets, AXES, 0, 0, tiled=True)]
  transfers between devices with their start and end apart: 23 -> 27, of which waited for: 15 -> 19; matrix products, arithmetic and copies ran while one was open for 1% -> 0% of each run, Pallas kernels for 9% -> 11%
where the time goes in v2:
time: 95.6 us; the launch traced here: 94.5 us
  waiting for transfers between devices  37.2 us (39%)
  starting transfers between devices  30.8 us (32%)
  Pallas kernels  25.5 us (27%)
  between operations  1.03 us (1%)
    ppermute x27, waiting for transfers between devices, permuted(): return lax.ppermute(array, AXES, pairs)  37.2 us
    ppermute x27, starting transfers between devices, permuted(): return lax.ppermute(array, AXES, pairs)  30.8 us
    pallas_call x25, Pallas kernels, call(): pl.pallas_call(kernel, in_specs=[vmem] * sum(there), out_specs=[pl.BlockS...  21.3 us
  transfers between devices with their start and end apart: 27, of which 19 were waited for; matrix products, arithmetic and copies ran while one was open for 0% of the time, Pallas kernels for 11%

profile of v2, /device:TPU:0, one launch (start us, length us, event | category | flops | bytes accessed | tf_op | source)
XLA Modules:
  0.0 94.5 jit_solution(1387593567721087152)
XLA Ops:
  0.6 1.6 %collective-permute-start = (bf16[2,64,512]{2,1,0:T(8,128)(2,1)}, bf16[2,64,512]{2,1,0:T(8,128)(2,1)S(1)}, u32[]{:S(2)}, u32[]{:S(2)}) collective-permute-start(bf16[2,64,512]{2,1,0:T(8,128)(2,1)} %param.12), channel_id=1, source_target_pairs={{0,0},{1,8},{2,16},{3,24},{4,4},{5,12},{6,20},{7,28},{8,1},{9,9},{... | collective-permute-start | bytes 393224 | tf_op jit(solution)/shard_map/ppermute | solution.py:990
  3.0 3.6 %collective-permute-start.1 = (bf16[1,8,512]{2,1,0:T(8,128)(2,1)S(1)}, bf16[1,8,512]{2,1,0:T(8,128)(2,1)S(1)}, u32[]{:S(2)}, u32[]{:S(2)}) collective-permute-start(bf16[1,8,512]{2,1,0:T(8,128)(2,1)S(1)} %shard_map.189.refs_0_.refs_8_), channel_id=1, source_target_pairs={{0,1},{1,0},{2,3},{3,2},{4,5},{5,4},{6,7},{7,6},{8,9},{9,8},{10,11... | collective-permute-start | bytes 24584 | tf_op jit(solution)/shard_map/ppermute | solution.py:990
  8.9 2.2 %collective-permute-done.2.refs_2_.refs_10_ = bf16[2,8,512]{2,1,0:T(8,128)(2,1)S(1)} collective-permute-done((bf16[2,8,512]{2,1,0:T(8,128)(2,1)S(1)}, bf16[2,8,512]{2,1,0:T(8,128)(2,1)S(1)}, u32[]{:S(2)}, u32[]{:S(2)}) %collective-permute-start.2) | collective-permute-done | bytes 16416 | tf_op jit(solution)/shard_map/ppermute | solution.py:990
  11.2 3.5 %collective-permute-start.3 = (bf16[4,8,512]{2,1,0:T(8,128)(2,1)S(1)}, bf16[4,8,512]{2,1,0:T(8,128)(2,1)S(1)}, u32[]{:S(2)}, u32[]{:S(2)}) collective-permute-start(bf16[4,8,512]{2,1,0:T(8,128)(2,1)S(1)} %shard_map.191), channel_id=1, source_target_pairs={{0,2},{1,3},{2,0},{3,1},{4,6},{5,7},{6,4},{7,5},{8,10},{9,11},{10,... | collective-permute-start | bytes 98312 | tf_op jit(solution)/shard_map/ppermute | solution.py:990
  14.6 1.7 %shard_map.187 = (bf16[512,512]{1,0:T(8,128)(2,1)S(1)}, f32[1,512]{1,0:T(1,128)S(1)}, bf16[512,512]{1,0:T(8,128)(2,1)S(1)}, f32[1,512]{1,0:T(1,128)S(1)}, bf16[5...) custom-call(bf16[512,512]{1,0:T(8,128)(2,1)} %refs_0_.1, ...), custom_call_target="tpu_custom_call" | custom-call | tf_op jit(solution)/shard_map/pallas_call | solution.py:1212
  16.9 6.1 %shard_map.193 = (f32[12,256,1024]{2,1,0:T(8,128)S(1)}, f32[48,512]{1,0:T(8,128)}, f32[1344,128]{1,0:T(8,128)S(1)}, f32[1344,128]{1,0:T(8,128)S(1)}, f32[12,256,...) custom-call(s32[1,8]{1,0:T(1,128)S(1)} %get-tuple-element.70.refs_0_, ...), custom_call_target="tpu_custom_call" | custom-call | tf_op jit(solution)/shard_map/pallas_call | solution.py:1046
  24.2 2.7 %collective-permute-done.4.refs_1_.refs_11_ = f32[1,1,24,128]{3,2,1,0:T(8,128)S(1)} collective-permute-done((f32[1,1,24,128]{3,2,1,0:T(8,128)S(1)}, f32[1,1,24,128]{3,2,1,0:T(8,128)S(1)}, u32[]{:S(2)}, u32[]{:S(2)}) %collective-permute-start.4) | collective-permute-done | bytes 12320 | tf_op jit(solution)/shard_map/ppermute | solution.py:990
  26.9 1.5 %collective-permute-start.5 = (f32[2,1,24,128]{3,2,1,0:T(8,128)S(1)}, f32[2,1,24,128]{3,2,1,0:T(8,128)S(1)}, u32[]{:S(2)}, u32[]{:S(2)}) collective-permute-start(f32[2,1,24,128]{3,2,1,0:T(8,128)S(1)} %shard_map.195), channel_id=1, source_target_pairs={{0,4},{1,5},{2,6},{3,7},{4,0},{5,1},{6,2},{7,3},{8,12},{9,13},{10,... | collective-permute-start | bytes 73736 | tf_op jit(solution)/shard_map/ppermute | solution.py:990
  28.4 2.3 %collective-permute-done.5.refs_2_.refs_12_ = f32[2,1,24,128]{3,2,1,0:T(8,128)S(1)} collective-permute-done((f32[2,1,24,128]{3,2,1,0:T(8,128)S(1)}, f32[2,1,24,128]{3,2,1,0:T(8,128)S(1)}, u32[]{:S(2)}, u32[]{:S(2)}) %collective-permute-start.5) | collective-permute-done | bytes 24608 | tf_op jit(solution)/shard_map/ppermute | solution.py:990
  31.9 6.9 %shard_map.197 = (bf16[12,256,1024]{2,1,0:T(8,128)(2,1)S(1)}, f32[1,1024]{1,0:T(1,128)S(1)}, f32[1,128]{1,0:T(1,128)S(1)}, f32[2048,128]{1,0:T(8,128)S(1)}, f32[2048,128]{1,0:T(8,128)S(1)}) custom-call(s32[1,8]{1,0:T(1,128)S(1)} %get-tuple-element.70.refs_0_, s32[1,8]{1,0:T(1,128)S(1)} %get-tuple-element.71.refs_1_, f32[1,8]{1,0:T(1,128)S(1)} %get-tuple-element.72.refs_2_, ...), custom_call_target="tpu_custom_call" | custom-call | tf_op jit(solution)/shard_map/pallas_call | solution.py:1046
  38.9 3.6 %shard_map.200 = (bf16[128,512]{1,0:T(8,128)(2,1)S(1)}, f32[16,128]{1,0:T(8,128)S(1)}, f32[1408,128]{1,0:T(8,128)S(1)}, f32[1424,128]{1,0:T(8,128)S(1)}) custom-call(s32[1,8]{1,0:T(1,128)S(1)} %get-tuple-element.70.refs_0_, s32[1,8]{1,0:T(1,128)S(1)} %get-tuple-element.71.refs_1_, bf16[12,256,1024]{2,1,0:T(8,128)(2,1)S(1)} %get-tuple-element.92.refs_2_, ...), custom_call_target="tpu_custom_call" | custom-call | tf_op jit(solution)/shard_map/pallas_call | solution.py:1046
  42.7 1.6 %collective-permute-start.8 = (bf16[1024,128]{1,0:T(8,128)(2,1)S(1)}, bf16[1024,128]{1,0:T(8,128)(2,1)S(1)}, u32[]{:S(2)}, u32[]{:S(2)}) collective-permute-start(bf16[1024,128]{1,0:T(8,128)(2,1)S(1)} %get-tuple-element.89), channel_id=1, source_target_pairs={{0,4},{1,3},{2,6},{3,1},{4,0},{5,7},{6,2},{7,5},{8,12},{9,11},{10,... | collective-permute-start | bytes 786440 | tf_op jit(solution)/shard_map/ppermute | solution.py:990
  45.0 4.2 %collective-permute-done.8.refs_1_ = bf16[1024,128]{1,0:T(8,128)(2,1)S(1)} collective-permute-done((bf16[1024,128]{1,0:T(8,128)(2,1)S(1)}, bf16[1024,128]{1,0:T(8,128)(2,1)S(1)}, u32[]{:S(2)}, u32[]{:S(2)}) %collective-permute-start.8) | collective-permute-done | bytes 262176 | tf_op jit(solution)/shard_map/ppermute | solution.py:990
  50.6 1.6 %collective-permute-start.12 = (bf16[400,128]{1,0:T(8,128)(2,1)S(1)}, bf16[400,128]{1,0:T(8,128)(2,1)S(1)}, u32[]{:S(2)}, u32[]{:S(2)}) collective-permute-start(bf16[400,128]{1,0:T(8,128)(2,1)S(1)} %get-tuple-element.102), channel_id=1, source_target_pairs={{0,4},{1,9},{2,6},{3,11},{4,0},{5,13},{6,2},{7,15},{8,12},{9,1},{1... | collective-permute-start | bytes 307208 | tf_op jit(solution)/shard_map/ppermute | solution.py:990
  53.0 2.3 %collective-permute-done.12.refs_3_ = bf16[400,128]{1,0:T(8,128)(2,1)S(1)} collective-permute-done((bf16[400,128]{1,0:T(8,128)(2,1)S(1)}, bf16[400,128]{1,0:T(8,128)(2,1)S(1)}, u32[]{:S(2)}, u32[]{:S(2)}) %collective-permute-start.12) | collective-permute-done | bytes 102432 | tf_op jit(solution)/shard_map/ppermute | solution.py:990
  55.5 1.6 %collective-permute-start.14 = (f32[192,128]{1,0:T(8,128)S(1)}, f32[192,128]{1,0:T(8,128)S(1)}, u32[]{:S(2)}, u32[]{:S(2)}) collective-permute-start(f32[192,128]{1,0:T(8,128)S(1)} %get-tuple-element.107), channel_id=1, source_target_pairs={{0,2},{1,5},{2,0},{3,7},{4,6},{5,1},{6,4},{7,3},{8,10},{9,13},{10,... | collective-permute-start | bytes 294920 | tf_op jit(solution)/shard_map/ppermute | solution.py:990
  57.1 4.0 %collective-permute-done.14.refs_3_ = f32[192,128]{1,0:T(8,128)S(1)} collective-permute-done((f32[192,128]{1,0:T(8,128)S(1)}, f32[192,128]{1,0:T(8,128)S(1)}, u32[]{:S(2)}, u32[]{:S(2)}) %collective-permute-start.14) | collective-permute-done | bytes 98336 | tf_op jit(solution)/shard_map/ppermute | solution.py:990
  63.8 1.6 %collective-permute-start.21 = (bf16[8,8,512]{2,1,0:T(8,128)(2,1)S(1)}, bf16[8,8,512]{2,1,0:T(8,128)(2,1)S(1)}, u32[]{:S(2)}, u32[]{:S(2)}) collective-permute-start(bf16[8,8,512]{2,1,0:T(8,128)(2,1)S(1)} %shard_map.207.refs_0_), channel_id=1, source_target_pairs={{0,16},{1,17},{2,18},{3,19},{4,20},{5,21},{6,22},{7,23},{8,24},{9,... | collective-permute-start | bytes 196616 | tf_op jit(solution)/shard_map/ppermute | solution.py:990
  65.4 7.7 %collective-permute-done.16.other_ref = bf16[656,128]{1,0:T(8,128)(2,1)S(1)} collective-permute-done((bf16[656,128]{1,0:T(8,128)(2,1)S(1)}, bf16[656,128]{1,0:T(8,128)(2,1)S(1)}, u32[]{:S(2)}, u32[]{:S(2)}) %collective-permute-start.16) | collective-permute-done | bytes 167968 | tf_op jit(solution)/shard_map/ppermute | solution.py:990
  74.3 2.0 %collective-permute-start.22 = (bf16[16,8,512]{2,1,0:T(8,128)(2,1)S(1)}, bf16[16,8,512]{2,1,0:T(8,128)(2,1)S(1)}, u32[]{:S(2)}, u32[]{:S(2)}) collective-permute-start(bf16[16,8,512]{2,1,0:T(8,128)(2,1)S(1)} %shard_map.208), channel_id=1, source_target_pairs={{0,8},{1,9},{2,10},{3,11},{4,12},{5,13},{6,14},{7,15},{8,0},{9,1},... | collective-permute-start | bytes 393224 | tf_op jit(solution)/shard_map/ppermute | solution.py:990
  78.9 1.9 %collective-permute-start.20 = (bf16[352,128]{1,0:T(8,128)(2,1)S(1)}, bf16[352,128]{1,0:T(8,128)(2,1)S(1)}, u32[]{:S(2)}, u32[]{:S(2)}) collective-permute-start(bf16[352,128]{1,0:T(8,128)(2,1)S(1)} %get-tuple-element.115.refs_2_), channel_id=1, source_target_pairs={{0,4},{1,9},{2,6},{3,11},{4,0},{5,13},{6,2},{7,15},{8,12},{9,1},{1... | collective-permute-start | bytes 270344 | tf_op jit(solution)/shard_map/ppermute | solution.py:990
  83.5 1.9 %collective-permute-start.23 = (bf16[1024,128]{1,0:T(8,128)(2,1)S(1)}, bf16[1024,128]{1,0:T(8,128)(2,1)S(1)}, u32[]{:S(2)}, u32[]{:S(2)}) collective-permute-start(bf16[1024,128]{1,0:T(8,128)(2,1)S(1)} %get-tuple-element.117.refs_0_), channel_id=1, source_target_pairs={{0,4},{1,3},{2,6},{3,1},{4,0},{5,7},{6,2},{7,5},{8,12},{9,11},{10,... | collective-permute-start | bytes 786440 | tf_op jit(solution)/shard_map/ppermute | solution.py:990
  86.5 3.4 %collective-permute-done.23.refs_1_ = bf16[1024,128]{1,0:T(8,128)(2,1)S(1)} collective-permute-done((bf16[1024,128]{1,0:T(8,128)(2,1)S(1)}, bf16[1024,128]{1,0:T(8,128)(2,1)S(1)}, u32[]{:S(2)}, u32[]{:S(2)}) %collective-permute-start.23) | collective-permute-done | bytes 262176 | tf_op jit(solution)/shard_map/ppermute | solution.py:990
  92.7 1.7 %shard_map.215 = (f32[512,1024]{1,0:T(8,128)}, f32[512,512]{1,0:T(8,128)}, f32[512,512]{1,0:T(8,128)}, f32[1,512]{1,0:T(1,128)}, f32[6,1,512]{2,1,0:T(1,128)}) custom-call(bf16[2048,128]{1,0:T(8,128)(2,1)S(1)} %collective-permute-done.25.output_other_ref, ...), custom_call_target="tpu_custom_call", output_to_operand_aliasing={{0}: (5, {}), {1}: (6, {})} | custom-call | tf_op jit(solution)/shard_map/pallas_call | solution.py:1428
  (59 shorter events, 22.5 us)
Async XLA Ops:
  0.6 16.1 %collective-permute-start = (bf16[2,64,512]{2,1,0:T(8,128)(2,1)}, bf16[2,64,512]{2,1,0:T(8,128)(2,1)S(1)}, u32[]{:S(2)}, u32[]{:S(2)}) collective-permute-start(bf16[2,64,512]{2,1,0:T(8,128)(2,1)} %param.12), channel_id=1, source_target_pairs={{0,0},{1,8},{2,16},{3,24},{4,4},{5,12},{6,20},{7,28},{8,1},{9,9},{... | collective-permute-start | bytes 393224 | tf_op jit(solution)/shard_map/ppermute | solution.py:990
  3.0 4.4 %collective-permute-start.1 = (bf16[1,8,512]{2,1,0:T(8,128)(2,1)S(1)}, bf16[1,8,512]{2,1,0:T(8,128)(2,1)S(1)}, u32[]{:S(2)}, u32[]{:S(2)}) collective-permute-start(bf16[1,8,512]{2,1,0:T(8,128)(2,1)S(1)} %shard_map.189.refs_0_.refs_8_), channel_id=1, source_target_pairs={{0,1},{1,0},{2,3},{3,2},{4,5},{5,4},{6,7},{7,6},{8,9},{9,8},{10,11... | collective-permute-start | bytes 24584 | tf_op jit(solution)/shard_map/ppermute | solution.py:990
  7.4 3.7 %collective-permute-start.2 = (bf16[2,8,512]{2,1,0:T(8,128)(2,1)S(1)}, bf16[2,8,512]{2,1,0:T(8,128)(2,1)S(1)}, u32[]{:S(2)}, u32[]{:S(2)}) collective-permute-start(bf16[2,8,512]{2,1,0:T(8,128)(2,1)S(1)} %shard_map.190), channel_id=1, source_target_pairs={{0,4},{1,5},{2,6},{3,7},{4,0},{5,1},{6,2},{7,3},{8,12},{9,13},{10,... | collective-permute-start | bytes 49160 | tf_op jit(solution)/shard_map/ppermute | solution.py:990
  11.2 5.4 %collective-permute-start.3 = (bf16[4,8,512]{2,1,0:T(8,128)(2,1)S(1)}, bf16[4,8,512]{2,1,0:T(8,128)(2,1)S(1)}, u32[]{:S(2)}, u32[]{:S(2)}) collective-permute-start(bf16[4,8,512]{2,1,0:T(8,128)(2,1)S(1)} %shard_map.191), channel_id=1, source_target_pairs={{0,2},{1,3},{2,0},{3,1},{4,6},{5,7},{6,4},{7,5},{8,10},{9,11},{10,... | collective-permute-start | bytes 98312 | tf_op jit(solution)/shard_map/ppermute | solution.py:990
  23.1 3.8 %collective-permute-start.4 = (f32[1,1,24,128]{3,2,1,0:T(8,128)S(1)}, f32[1,1,24,128]{3,2,1,0:T(8,128)S(1)}, u32[]{:S(2)}, u32[]{:S(2)}) collective-permute-start(f32[1,1,24,128]{3,2,1,0:T(8,128)S(1)} %get-tuple-element.85.refs_0_.refs_10_), channel_id=1, source_target_pairs={{0,2},{1,3},{2,0},{3,1},{4,6},{5,7},{6,4},{7,5},{8,10},{9,11},{10,... | collective-permute-start | bytes 36872 | tf_op jit(solution)/shard_map/ppermute | solution.py:990
  26.9 3.8 %collective-permute-start.5 = (f32[2,1,24,128]{3,2,1,0:T(8,128)S(1)}, f32[2,1,24,128]{3,2,1,0:T(8,128)S(1)}, u32[]{:S(2)}, u32[]{:S(2)}) collective-permute-start(f32[2,1,24,128]{3,2,1,0:T(8,128)S(1)} %shard_map.195), channel_id=1, source_target_pairs={{0,4},{1,5},{2,6},{3,7},{4,0},{5,1},{6,2},{7,3},{8,12},{9,13},{10,... | collective-permute-start | bytes 73736 | tf_op jit(solution)/shard_map/ppermute | solution.py:990
  38.8 3.8 %collective-permute-start.7 = (f32[2048,128]{1,0:T(8,128)S(1)}, f32[2048,128]{1,0:T(8,128)S(1)}, u32[]{:S(2)}, u32[]{:S(2)}) collective-permute-start(f32[2048,128]{1,0:T(8,128)S(1)} %get-tuple-element.87), channel_id=1, source_target_pairs={{0,1},{1,0},{2,3},{3,2},{4,5},{5,4},{6,7},{7,6},{8,9},{9,8},{10,11... | collective-permute-start | bytes 3145736 | tf_op jit(solution)/shard_map/ppermute | solution.py:990
  42.7 6.4 %collective-permute-start.8 = (bf16[1024,128]{1,0:T(8,128)(2,1)S(1)}, bf16[1024,128]{1,0:T(8,128)(2,1)S(1)}, u32[]{:S(2)}, u32[]{:S(2)}) collective-permute-start(bf16[1024,128]{1,0:T(8,128)(2,1)S(1)} %get-tuple-element.89), channel_id=1, source_target_pairs={{0,4},{1,3},{2,6},{3,1},{4,0},{5,7},{6,2},{7,5},{8,12},{9,11},{10,... | collective-permute-start | bytes 786440 | tf_op jit(solution)/shard_map/ppermute | solution.py:990
  44.9 5.7 %collective-permute-start.11 = (bf16[752,128]{1,0:T(8,128)(2,1)S(1)}, bf16[752,128]{1,0:T(8,128)(2,1)S(1)}, u32[]{:S(2)}, u32[]{:S(2)}) collective-permute-start(bf16[752,128]{1,0:T(8,128)(2,1)S(1)} %get-tuple-element.99), channel_id=1, source_target_pairs={{0,8},{1,3},{2,10},{3,1},{4,12},{5,7},{6,14},{7,5},{8,0},{9,11},{1... | collective-permute-start | bytes 577544 | tf_op jit(solution)/shard_map/ppermute | solution.py:990
  49.2 6.2 %collective-permute-start.9 = (bf16[512,128]{1,0:T(8,128)(2,1)S(1)}, bf16[512,128]{1,0:T(8,128)(2,1)S(1)}, u32[]{:S(2)}, u32[]{:S(2)}) collective-permute-start(bf16[512,128]{1,0:T(8,128)(2,1)S(1)} %get-tuple-element.91), channel_id=1, source_target_pairs={{0,2},{1,9},{2,0},{3,11},{4,6},{5,13},{6,4},{7,15},{8,10},{9,1},{1... | collective-permute-start | bytes 393224 | tf_op jit(solution)/shard_map/ppermute | solution.py:990
  50.6 4.7 %collective-permute-start.12 = (bf16[400,128]{1,0:T(8,128)(2,1)S(1)}, bf16[400,128]{1,0:T(8,128)(2,1)S(1)}, u32[]{:S(2)}, u32[]{:S(2)}) collective-permute-start(bf16[400,128]{1,0:T(8,128)(2,1)S(1)} %get-tuple-element.102), channel_id=1, source_target_pairs={{0,4},{1,9},{2,6},{3,11},{4,0},{5,13},{6,2},{7,15},{8,12},{9,1},{1... | collective-permute-start | bytes 307208 | tf_op jit(solution)/shard_map/ppermute | solution.py:990
  52.2 4.9 %collective-permute-start.15 = (bf16[128,512]{1,0:T(8,128)(2,1)S(1)}, bf16[128,512]{1,0:T(8,128)(2,1)S(1)}, u32[]{:S(2)}, u32[]{:S(2)}) collective-permute-start(bf16[128,512]{1,0:T(8,128)(2,1)S(1)} %get-tuple-element.109), channel_id=1, source_target_pairs={{0,0},{1,8},{2,16},{3,24},{4,4},{5,12},{6,20},{7,28},{8,1},{9,9},{... | collective-permute-start | bytes 393224 | tf_op jit(solution)/shard_map/ppermute | solution.py:990
  55.4 6.9 %collective-permute-start.13 = (f32[256,128]{1,0:T(8,128)S(1)}, f32[256,128]{1,0:T(8,128)S(1)}, u32[]{:S(2)}, u32[]{:S(2)}) collective-permute-start(f32[256,128]{1,0:T(8,128)S(1)} %get-tuple-element.105), channel_id=1, source_target_pairs={{0,8},{1,5},{2,10},{3,7},{4,12},{5,1},{6,14},{7,3},{8,0},{9,13},{1... | collective-permute-start | bytes 393224 | tf_op jit(solution)/shard_map/ppermute | solution.py:990
  55.5 5.6 %collective-permute-start.14 = (f32[192,128]{1,0:T(8,128)S(1)}, f32[192,128]{1,0:T(8,128)S(1)}, u32[]{:S(2)}, u32[]{:S(2)}) collective-permute-start(f32[192,128]{1,0:T(8,128)S(1)} %get-tuple-element.107), channel_id=1, source_target_pairs={{0,2},{1,5},{2,0},{3,7},{4,6},{5,1},{6,4},{7,3},{8,10},{9,13},{10,... | collective-permute-start | bytes 294920 | tf_op jit(solution)/shard_map/ppermute | solution.py:990
  62.4 10.7 %collective-permute-start.16 = (bf16[656,128]{1,0:T(8,128)(2,1)S(1)}, bf16[656,128]{1,0:T(8,128)(2,1)S(1)}, u32[]{:S(2)}, u32[]{:S(2)}) collective-permute-start(bf16[656,128]{1,0:T(8,128)(2,1)S(1)} %get-tuple-element.110.own_ref), channel_id=1, source_target_pairs={{0,16},{1,17},{2,18},{3,19},{4,20},{5,21},{6,22},{7,23},{8,24},{9,... | collective-permute-start | bytes 503816 | tf_op jit(solution)/shard_map/ppermute | solution.py:990
  63.8 10.5 %collective-permute-start.21 = (bf16[8,8,512]{2,1,0:T(8,128)(2,1)S(1)}, bf16[8,8,512]{2,1,0:T(8,128)(2,1)S(1)}, u32[]{:S(2)}, u32[]{:S(2)}) collective-permute-start(bf16[8,8,512]{2,1,0:T(8,128)(2,1)S(1)} %shard_map.207.refs_0_), channel_id=1, source_target_pairs={{0,16},{1,17},{2,18},{3,19},{4,20},{5,21},{6,22},{7,23},{8,24},{9,... | collective-permute-start | bytes 196616 | tf_op jit(solution)/shard_map/ppermute | solution.py:990
  73.2 4.6 %collective-permute-start.17 = (bf16[256,128]{1,0:T(8,128)(2,1)S(1)}, bf16[256,128]{1,0:T(8,128)(2,1)S(1)}, u32[]{:S(2)}, u32[]{:S(2)}) collective-permute-start(bf16[256,128]{1,0:T(8,128)(2,1)S(1)} %get-tuple-element.112.refs_0_), channel_id=1, source_target_pairs={{0,8},{1,5},{2,10},{3,7},{4,12},{5,1},{6,14},{7,3},{8,0},{9,13},{1... | collective-permute-start | bytes 196616 | tf_op jit(solution)/shard_map/ppermute | solution.py:990
  73.3 4.1 %collective-permute-start.18 = (bf16[176,128]{1,0:T(8,128)(2,1)S(1)}, bf16[176,128]{1,0:T(8,128)(2,1)S(1)}, u32[]{:S(2)}, u32[]{:S(2)}) collective-permute-start(bf16[176,128]{1,0:T(8,128)(2,1)S(1)} %get-tuple-element.113.refs_2_), channel_id=1, source_target_pairs={{0,2},{1,5},{2,0},{3,7},{4,6},{5,1},{6,4},{7,3},{8,10},{9,13},{10,... | collective-permute-start | bytes 135176 | tf_op jit(solution)/shard_map/ppermute | solution.py:990
  74.3 6.5 %collective-permute-start.22 = (bf16[16,8,512]{2,1,0:T(8,128)(2,1)S(1)}, bf16[16,8,512]{2,1,0:T(8,128)(2,1)S(1)}, u32[]{:S(2)}, u32[]{:S(2)}) collective-permute-start(bf16[16,8,512]{2,1,0:T(8,128)(2,1)S(1)} %shard_map.208), channel_id=1, source_target_pairs={{0,8},{1,9},{2,10},{3,11},{4,12},{5,13},{6,14},{7,15},{8,0},{9,1},... | collective-permute-start | bytes 393224 | tf_op jit(solution)/shard_map/ppermute | solution.py:990
  77.8 5.6 %collective-permute-start.19 = (bf16[512,128]{1,0:T(8,128)(2,1)S(1)}, bf16[512,128]{1,0:T(8,128)(2,1)S(1)}, u32[]{:S(2)}, u32[]{:S(2)}) collective-permute-start(bf16[512,128]{1,0:T(8,128)(2,1)S(1)} %get-tuple-element.114.refs_0_), channel_id=1, source_target_pairs={{0,2},{1,9},{2,0},{3,11},{4,6},{5,13},{6,4},{7,15},{8,10},{9,1},{1... | collective-permute-start | bytes 393224 | tf_op jit(solution)/shard_map/ppermute | solution.py:990
  78.9 4.5 %collective-permute-start.20 = (bf16[352,128]{1,0:T(8,128)(2,1)S(1)}, bf16[352,128]{1,0:T(8,128)(2,1)S(1)}, u32[]{:S(2)}, u32[]{:S(2)}) collective-permute-start(bf16[352,128]{1,0:T(8,128)(2,1)S(1)} %get-tuple-element.115.refs_2_), channel_id=1, source_target_pairs={{0,4},{1,9},{2,6},{3,11},{4,0},{5,13},{6,2},{7,15},{8,12},{9,1},{1... | collective-permute-start | bytes 270344 | tf_op jit(solution)/shard_map/ppermute | solution.py:990
  83.5 6.4 %collective-permute-start.23 = (bf16[1024,128]{1,0:T(8,128)(2,1)S(1)}, bf16[1024,128]{1,0:T(8,128)(2,1)S(1)}, u32[]{:S(2)}, u32[]{:S(2)}) collective-permute-start(bf16[1024,128]{1,0:T(8,128)(2,1)S(1)} %get-tuple-element.117.refs_0_), channel_id=1, source_target_pairs={{0,4},{1,3},{2,6},{3,1},{4,0},{5,7},{6,2},{7,5},{8,12},{9,11},{10,... | collective-permute-start | bytes 786440 | tf_op jit(solution)/shard_map/ppermute | solution.py:990
  85.4 5.5 %collective-permute-start.24 = (bf16[704,128]{1,0:T(8,128)(2,1)S(1)}, bf16[704,128]{1,0:T(8,128)(2,1)S(1)}, u32[]{:S(2)}, u32[]{:S(2)}) collective-permute-start(bf16[704,128]{1,0:T(8,128)(2,1)S(1)} %get-tuple-element.118.refs_0_), channel_id=1, source_target_pairs={{0,8},{1,3},{2,10},{3,1},{4,12},{5,7},{6,14},{7,5},{8,0},{9,11},{1... | collective-permute-start | bytes 540680 | tf_op jit(solution)/shard_map/ppermute | solution.py:990
  90.0 2.7 %collective-permute-start.25 = (bf16[2048,128]{1,0:T(8,128)(2,1)S(1)}, bf16[2048,128]{1,0:T(8,128)(2,1)S(1)}, u32[]{:S(2)}, u32[]{:S(2)}) collective-permute-start(bf16[2048,128]{1,0:T(8,128)(2,1)S(1)} %shard_map.212.refs_0_), channel_id=1, source_target_pairs={{0,1},{1,0},{2,3},{3,2},{4,5},{5,4},{6,7},{7,6},{8,9},{9,8},{10,11... | collective-permute-start | bytes 1572872 | tf_op jit(solution)/shard_map/ppermute | solution.py:990
  (3 other events, 5.2 us)

commit v3 on v2

--- a/solution.py
+++ b/solution.py
@@ -1175,7 +1175,7 @@
         loss_scale.reshape(1, all_seqs),
     )
     if in_plane:
-        plane = [((0, 1), 1), ((1, 0), 256), ((0, 2), 2)]
+        plane = [((0, 2), 2), ((0, 1), 1), ((1, 0), 256)]
         encoder = permuted(encoder_out, turned_over)
         packet = pl.pallas_call(
             label_packet_kernel,

time: 95.6 us -> 97.2 us (1.017); the launches traced: 94.5 us -> 97.4 us
  starting transfers between devices: 30.8 us -> 40.4 us
  waiting for transfers between devices: 37.2 us -> 30.4 us
    ppermute x27, starting transfers between devices: 30.8 us -> 40.4 us  [permuted(): return lax.ppermute(array, AXES, pairs)]
    ppermute x27, waiting for transfers between devices: 37.2 us -> 30.4 us  [permuted(): return lax.ppermute(array, AXES, pairs)]
  transfers between devices with their start and end apart: 27 -> 27, of which waited for: 19 -> 16; matrix products, arithmetic and copies ran while one was open for 0% -> 0% of each run, Pallas kernels for 11% -> 11%
where the time goes in v3:
time: 97.2 us; the launch traced here: 97.4 us
  starting transfers between devices  40.4 us (42%)
  waiting for transfers between devices  30.4 us (31%)
  Pallas kernels  25.6 us (26%)
  between operations  1.02 us (1%)
    ppermute x27, starting transfers between devices, permuted(): return lax.ppermute(array, AXES, pairs)  40.4 us
    ppermute x27, waiting for transfers between devices, permuted(): return lax.ppermute(array, AXES, pairs)  30.4 us
    pallas_call x25, Pallas kernels, call(): pl.pallas_call(kernel, in_specs=[vmem] * sum(there), out_specs=[pl.BlockS...  21.4 us
  transfers between devices with their start and end apart: 27, of which 16 were waited for; matrix products, arithmetic and copies ran while one was open for 0% of the time, Pallas kernels for 11%

profile of v3, /device:TPU:0, one launch (start us, length us, event | category | flops | bytes accessed | tf_op | source)
XLA Modules:
  0.0 97.4 jit_solution(11371257714049008746)
XLA Ops:
  3.0 5.9 %collective-permute-start.1 = (bf16[1,8,512]{2,1,0:T(8,128)(2,1)S(1)}, bf16[1,8,512]{2,1,0:T(8,128)(2,1)S(1)}, u32[]{:S(2)}, u32[]{:S(2)}) collective-permute-start(bf16[1,8,512]{2,1,0:T(8,128)(2,1)S(1)} %shard_map.189.refs_0_.refs_8_), channel_id=1, source_target_pairs={{0,2},{1,3},{2,0},{3,1},{4,6},{5,7},{6,4},{7,5},{8,10},{9,11},{10,... | collective-permute-start | bytes 24584 | tf_op jit(solution)/shard_map/ppermute | solution.py:990
  8.9 1.6 %collective-permute-done.1.refs_1_.refs_9_ = bf16[1,8,512]{2,1,0:T(8,128)(2,1)S(1)} collective-permute-done((bf16[1,8,512]{2,1,0:T(8,128)(2,1)S(1)}, bf16[1,8,512]{2,1,0:T(8,128)(2,1)S(1)}, u32[]{:S(2)}, u32[]{:S(2)}) %collective-permute-start.1) | collective-permute-done | bytes 8224 | tf_op jit(solution)/shard_map/ppermute | solution.py:990
  13.3 1.7 %shard_map.187 = (bf16[512,512]{1,0:T(8,128)(2,1)S(1)}, f32[1,512]{1,0:T(1,128)S(1)}, bf16[512,512]{1,0:T(8,128)(2,1)S(1)}, f32[1,512]{1,0:T(1,128)S(1)}, bf16[5...) custom-call(bf16[512,512]{1,0:T(8,128)(2,1)} %refs_0_.1, ...), custom_call_target="tpu_custom_call" | custom-call | tf_op jit(solution)/shard_map/pallas_call | solution.py:1212
  16.1 6.2 %shard_map.193 = (f32[12,256,1024]{2,1,0:T(8,128)S(1)}, f32[48,512]{1,0:T(8,128)}, f32[1344,128]{1,0:T(8,128)S(1)}, f32[1344,128]{1,0:T(8,128)S(1)}, f32[12,256,...) custom-call(s32[1,8]{1,0:T(1,128)S(1)} %get-tuple-element.70.refs_0_, ...), custom_call_target="tpu_custom_call" | custom-call | tf_op jit(solution)/shard_map/pallas_call | solution.py:1046
  23.4 2.7 %collective-permute-done.4.refs_1_.refs_11_ = f32[1,1,24,128]{3,2,1,0:T(8,128)S(1)} collective-permute-done((f32[1,1,24,128]{3,2,1,0:T(8,128)S(1)}, f32[1,1,24,128]{3,2,1,0:T(8,128)S(1)}, u32[]{:S(2)}, u32[]{:S(2)}) %collective-permute-start.4) | collective-permute-done | bytes 12320 | tf_op jit(solution)/shard_map/ppermute | solution.py:990
  27.5 2.3 %collective-permute-done.5.refs_2_.refs_12_ = f32[2,1,24,128]{3,2,1,0:T(8,128)S(1)} collective-permute-done((f32[2,1,24,128]{3,2,1,0:T(8,128)S(1)}, f32[2,1,24,128]{3,2,1,0:T(8,128)S(1)}, u32[]{:S(2)}, u32[]{:S(2)}) %collective-permute-start.5) | collective-permute-done | bytes 24608 | tf_op jit(solution)/shard_map/ppermute | solution.py:990
  31.1 6.9 %shard_map.197 = (bf16[12,256,1024]{2,1,0:T(8,128)(2,1)S(1)}, f32[1,1024]{1,0:T(1,128)S(1)}, f32[1,128]{1,0:T(1,128)S(1)}, f32[2048,128]{1,0:T(8,128)S(1)}, f32[2048,128]{1,0:T(8,128)S(1)}) custom-call(s32[1,8]{1,0:T(1,128)S(1)} %get-tuple-element.70.refs_0_, s32[1,8]{1,0:T(1,128)S(1)} %get-tuple-element.71.refs_1_, f32[1,8]{1,0:T(1,128)S(1)} %get-tuple-element.72.refs_2_, ...), custom_call_target="tpu_custom_call" | custom-call | tf_op jit(solution)/shard_map/pallas_call | solution.py:1046
  38.1 3.6 %shard_map.200 = (bf16[128,512]{1,0:T(8,128)(2,1)S(1)}, f32[16,128]{1,0:T(8,128)S(1)}, f32[1408,128]{1,0:T(8,128)S(1)}, f32[1424,128]{1,0:T(8,128)S(1)}) custom-call(s32[1,8]{1,0:T(1,128)S(1)} %get-tuple-element.70.refs_0_, s32[1,8]{1,0:T(1,128)S(1)} %get-tuple-element.71.refs_1_, bf16[12,256,1024]{2,1,0:T(8,128)(2,1)S(1)} %get-tuple-element.92.refs_2_, ...), custom_call_target="tpu_custom_call" | custom-call | tf_op jit(solution)/shard_map/pallas_call | solution.py:1046
  44.1 4.6 %collective-permute-start.11 = (bf16[752,128]{1,0:T(8,128)(2,1)S(1)}, bf16[752,128]{1,0:T(8,128)(2,1)S(1)}, u32[]{:S(2)}, u32[]{:S(2)}) collective-permute-start(bf16[752,128]{1,0:T(8,128)(2,1)S(1)} %get-tuple-element.99), channel_id=1, source_target_pairs={{0,8},{1,3},{2,10},{3,1},{4,12},{5,7},{6,14},{7,5},{8,0},{9,11},{1... | collective-permute-start | bytes 577544 | tf_op jit(solution)/shard_map/ppermute | solution.py:990
  48.7 1.6 %collective-permute-start.9 = (bf16[512,128]{1,0:T(8,128)(2,1)S(1)}, bf16[512,128]{1,0:T(8,128)(2,1)S(1)}, u32[]{:S(2)}, u32[]{:S(2)}) collective-permute-start(bf16[512,128]{1,0:T(8,128)(2,1)S(1)} %get-tuple-element.91), channel_id=1, source_target_pairs={{0,2},{1,9},{2,0},{3,11},{4,6},{5,13},{6,4},{7,15},{8,10},{9,1},{1... | collective-permute-start | bytes 393224 | tf_op jit(solution)/shard_map/ppermute | solution.py:990
  50.3 1.9 %collective-permute-done.11.refs_1_ = bf16[752,128]{1,0:T(8,128)(2,1)S(1)} collective-permute-done((bf16[752,128]{1,0:T(8,128)(2,1)S(1)}, bf16[752,128]{1,0:T(8,128)(2,1)S(1)}, u32[]{:S(2)}, u32[]{:S(2)}) %collective-permute-start.11) | collective-permute-done | bytes 192544 | tf_op jit(solution)/shard_map/ppermute | solution.py:990
  54.7 2.3 %collective-permute-done.12.refs_3_ = bf16[400,128]{1,0:T(8,128)(2,1)S(1)} collective-permute-done((bf16[400,128]{1,0:T(8,128)(2,1)S(1)}, bf16[400,128]{1,0:T(8,128)(2,1)S(1)}, u32[]{:S(2)}, u32[]{:S(2)}) %collective-permute-start.12) | collective-permute-done | bytes 102432 | tf_op jit(solution)/shard_map/ppermute | solution.py:990
  57.1 2.3 %collective-permute-start.13 = (f32[256,128]{1,0:T(8,128)S(1)}, f32[256,128]{1,0:T(8,128)S(1)}, u32[]{:S(2)}, u32[]{:S(2)}) collective-permute-start(f32[256,128]{1,0:T(8,128)S(1)} %get-tuple-element.105), channel_id=1, source_target_pairs={{0,8},{1,5},{2,10},{3,7},{4,12},{5,1},{6,14},{7,3},{8,0},{9,13},{1... | collective-permute-start | bytes 393224 | tf_op jit(solution)/shard_map/ppermute | solution.py:990
  60.7 3.8 %collective-permute-done.14.refs_3_ = f32[192,128]{1,0:T(8,128)S(1)} collective-permute-done((f32[192,128]{1,0:T(8,128)S(1)}, f32[192,128]{1,0:T(8,128)S(1)}, u32[]{:S(2)}, u32[]{:S(2)}) %collective-permute-start.14) | collective-permute-done | bytes 98336 | tf_op jit(solution)/shard_map/ppermute | solution.py:990
  64.6 2.0 %collective-permute-start.16 = (bf16[656,128]{1,0:T(8,128)(2,1)S(1)}, bf16[656,128]{1,0:T(8,128)(2,1)S(1)}, u32[]{:S(2)}, u32[]{:S(2)}) collective-permute-start(bf16[656,128]{1,0:T(8,128)(2,1)S(1)} %get-tuple-element.110.own_ref), channel_id=1, source_target_pairs={{0,16},{1,17},{2,18},{3,19},{4,20},{5,21},{6,22},{7,23},{8,24},{9,... | collective-permute-start | bytes 503816 | tf_op jit(solution)/shard_map/ppermute | solution.py:990
  67.6 7.5 %collective-permute-done.16.other_ref = bf16[656,128]{1,0:T(8,128)(2,1)S(1)} collective-permute-done((bf16[656,128]{1,0:T(8,128)(2,1)S(1)}, bf16[656,128]{1,0:T(8,128)(2,1)S(1)}, u32[]{:S(2)}, u32[]{:S(2)}) %collective-permute-start.16) | collective-permute-done | bytes 167968 | tf_op jit(solution)/shard_map/ppermute | solution.py:990
  75.3 2.4 %collective-permute-start.18 = (bf16[176,128]{1,0:T(8,128)(2,1)S(1)}, bf16[176,128]{1,0:T(8,128)(2,1)S(1)}, u32[]{:S(2)}, u32[]{:S(2)}) collective-permute-start(bf16[176,128]{1,0:T(8,128)(2,1)S(1)} %get-tuple-element.113.refs_2_), channel_id=1, source_target_pairs={{0,2},{1,5},{2,0},{3,7},{4,6},{5,1},{6,4},{7,3},{8,10},{9,13},{10,... | collective-permute-start | bytes 135176 | tf_op jit(solution)/shard_map/ppermute | solution.py:990
  77.7 2.0 %collective-permute-start.22 = (bf16[16,8,512]{2,1,0:T(8,128)(2,1)S(1)}, bf16[16,8,512]{2,1,0:T(8,128)(2,1)S(1)}, u32[]{:S(2)}, u32[]{:S(2)}) collective-permute-start(bf16[16,8,512]{2,1,0:T(8,128)(2,1)S(1)} %shard_map.208), channel_id=1, source_target_pairs={{0,8},{1,9},{2,10},{3,11},{4,12},{5,13},{6,14},{7,15},{8,0},{9,1},... | collective-permute-start | bytes 393224 | tf_op jit(solution)/shard_map/ppermute | solution.py:990
  80.0 2.0 %collective-permute-start.19 = (bf16[512,128]{1,0:T(8,128)(2,1)S(1)}, bf16[512,128]{1,0:T(8,128)(2,1)S(1)}, u32[]{:S(2)}, u32[]{:S(2)}) collective-permute-start(bf16[512,128]{1,0:T(8,128)(2,1)S(1)} %get-tuple-element.114.refs_0_), channel_id=1, source_target_pairs={{0,2},{1,9},{2,0},{3,11},{4,6},{5,13},{6,4},{7,15},{8,10},{9,1},{1... | collective-permute-start | bytes 393224 | tf_op jit(solution)/shard_map/ppermute | solution.py:990
  82.0 1.6 %collective-permute-start.20 = (bf16[352,128]{1,0:T(8,128)(2,1)S(1)}, bf16[352,128]{1,0:T(8,128)(2,1)S(1)}, u32[]{:S(2)}, u32[]{:S(2)}) collective-permute-start(bf16[352,128]{1,0:T(8,128)(2,1)S(1)} %get-tuple-element.115.refs_2_), channel_id=1, source_target_pairs={{0,4},{1,9},{2,6},{3,11},{4,0},{5,13},{6,2},{7,15},{8,12},{9,1},{1... | collective-permute-start | bytes 270344 | tf_op jit(solution)/shard_map/ppermute | solution.py:990
  86.6 1.7 %collective-permute-start.23 = (bf16[1024,128]{1,0:T(8,128)(2,1)S(1)}, bf16[1024,128]{1,0:T(8,128)(2,1)S(1)}, u32[]{:S(2)}, u32[]{:S(2)}) collective-permute-start(bf16[1024,128]{1,0:T(8,128)(2,1)S(1)} %get-tuple-element.117.refs_0_), channel_id=1, source_target_pairs={{0,4},{1,3},{2,6},{3,1},{4,0},{5,7},{6,2},{7,5},{8,12},{9,11},{10,... | collective-permute-start | bytes 786440 | tf_op jit(solution)/shard_map/ppermute | solution.py:990
  88.3 1.7 %collective-permute-start.24 = (bf16[704,128]{1,0:T(8,128)(2,1)S(1)}, bf16[704,128]{1,0:T(8,128)(2,1)S(1)}, u32[]{:S(2)}, u32[]{:S(2)}) collective-permute-start(bf16[704,128]{1,0:T(8,128)(2,1)S(1)} %get-tuple-element.118.refs_0_), channel_id=1, source_target_pairs={{0,8},{1,3},{2,10},{3,1},{4,12},{5,7},{6,14},{7,5},{8,0},{9,11},{1... | collective-permute-start | bytes 540680 | tf_op jit(solution)/shard_map/ppermute | solution.py:990
  90.0 3.1 %collective-permute-done.23.refs_1_ = bf16[1024,128]{1,0:T(8,128)(2,1)S(1)} collective-permute-done((bf16[1024,128]{1,0:T(8,128)(2,1)S(1)}, bf16[1024,128]{1,0:T(8,128)(2,1)S(1)}, u32[]{:S(2)}, u32[]{:S(2)}) %collective-permute-start.23) | collective-permute-done | bytes 262176 | tf_op jit(solution)/shard_map/ppermute | solution.py:990
  95.6 1.7 %shard_map.215 = (f32[512,1024]{1,0:T(8,128)}, f32[512,512]{1,0:T(8,128)}, f32[512,512]{1,0:T(8,128)}, f32[1,512]{1,0:T(1,128)}, f32[6,1,512]{2,1,0:T(1,128)}) custom-call(bf16[2048,128]{1,0:T(8,128)(2,1)S(1)} %collective-permute-done.25.output_other_ref, ...), custom_call_target="tpu_custom_call", output_to_operand_aliasing={{0}: (5, {}), {1}: (6, {})} | custom-call | tf_op jit(solution)/shard_map/pallas_call | solution.py:1428
  (59 shorter events, 23.2 us)
Async XLA Ops:
  0.6 15.2 %collective-permute-start = (bf16[2,64,512]{2,1,0:T(8,128)(2,1)}, bf16[2,64,512]{2,1,0:T(8,128)(2,1)S(1)}, u32[]{:S(2)}, u32[]{:S(2)}) collective-permute-start(bf16[2,64,512]{2,1,0:T(8,128)(2,1)} %param.12), channel_id=1, source_target_pairs={{0,0},{1,8},{2,16},{3,24},{4,4},{5,12},{6,20},{7,28},{8,1},{9,9},{... | collective-permute-start | bytes 393224 | tf_op jit(solution)/shard_map/ppermute | solution.py:990
  3.0 7.6 %collective-permute-start.1 = (bf16[1,8,512]{2,1,0:T(8,128)(2,1)S(1)}, bf16[1,8,512]{2,1,0:T(8,128)(2,1)S(1)}, u32[]{:S(2)}, u32[]{:S(2)}) collective-permute-start(bf16[1,8,512]{2,1,0:T(8,128)(2,1)S(1)} %shard_map.189.refs_0_.refs_8_), channel_id=1, source_target_pairs={{0,2},{1,3},{2,0},{3,1},{4,6},{5,7},{6,4},{7,5},{8,10},{9,11},{10,... | collective-permute-start | bytes 24584 | tf_op jit(solution)/shard_map/ppermute | solution.py:990
  11.8 3.9 %collective-permute-start.3 = (bf16[4,8,512]{2,1,0:T(8,128)(2,1)S(1)}, bf16[4,8,512]{2,1,0:T(8,128)(2,1)S(1)}, u32[]{:S(2)}, u32[]{:S(2)}) collective-permute-start(bf16[4,8,512]{2,1,0:T(8,128)(2,1)S(1)} %shard_map.191), channel_id=1, source_target_pairs={{0,4},{1,5},{2,6},{3,7},{4,0},{5,1},{6,2},{7,3},{8,12},{9,13},{10,... | collective-permute-start | bytes 98312 | tf_op jit(solution)/shard_map/ppermute | solution.py:990
  22.3 3.8 %collective-permute-start.4 = (f32[1,1,24,128]{3,2,1,0:T(8,128)S(1)}, f32[1,1,24,128]{3,2,1,0:T(8,128)S(1)}, u32[]{:S(2)}, u32[]{:S(2)}) collective-permute-start(f32[1,1,24,128]{3,2,1,0:T(8,128)S(1)} %get-tuple-element.85.refs_0_.refs_10_), channel_id=1, source_target_pairs={{0,2},{1,3},{2,0},{3,1},{4,6},{5,7},{6,4},{7,5},{8,10},{9,11},{10,... | collective-permute-start | bytes 36872 | tf_op jit(solution)/shard_map/ppermute | solution.py:990
  26.1 3.8 %collective-permute-start.5 = (f32[2,1,24,128]{3,2,1,0:T(8,128)S(1)}, f32[2,1,24,128]{3,2,1,0:T(8,128)S(1)}, u32[]{:S(2)}, u32[]{:S(2)}) collective-permute-start(f32[2,1,24,128]{3,2,1,0:T(8,128)S(1)} %shard_map.195), channel_id=1, source_target_pairs={{0,4},{1,5},{2,6},{3,7},{4,0},{5,1},{6,2},{7,3},{8,12},{9,13},{10,... | collective-permute-start | bytes 73736 | tf_op jit(solution)/shard_map/ppermute | solution.py:990
  38.0 3.8 %collective-permute-start.7 = (f32[2048,128]{1,0:T(8,128)S(1)}, f32[2048,128]{1,0:T(8,128)S(1)}, u32[]{:S(2)}, u32[]{:S(2)}) collective-permute-start(f32[2048,128]{1,0:T(8,128)S(1)} %get-tuple-element.87), channel_id=1, source_target_pairs={{0,1},{1,0},{2,3},{3,2},{4,5},{5,4},{6,7},{7,6},{8,9},{9,8},{10,11... | collective-permute-start | bytes 3145736 | tf_op jit(solution)/shard_map/ppermute | solution.py:990
  41.7 2.3 %collective-permute-start.10 = (f32[1424,128]{1,0:T(8,128)S(1)}, f32[1424,128]{1,0:T(8,128)S(1)}, u32[]{:S(2)}, u32[]{:S(2)}) collective-permute-start(f32[1424,128]{1,0:T(8,128)S(1)} %get-tuple-element.96), channel_id=1, source_target_pairs={{0,1},{1,0},{2,3},{3,2},{4,5},{5,4},{6,7},{7,6},{8,9},{9,8},{10,11... | collective-permute-start | bytes 2187272 | tf_op jit(solution)/shard_map/ppermute | solution.py:990
  41.9 6.7 %collective-permute-start.8 = (bf16[1024,128]{1,0:T(8,128)(2,1)S(1)}, bf16[1024,128]{1,0:T(8,128)(2,1)S(1)}, u32[]{:S(2)}, u32[]{:S(2)}) collective-permute-start(bf16[1024,128]{1,0:T(8,128)(2,1)S(1)} %get-tuple-element.89), channel_id=1, source_target_pairs={{0,4},{1,3},{2,6},{3,1},{4,0},{5,7},{6,2},{7,5},{8,12},{9,11},{10,... | collective-permute-start | bytes 786440 | tf_op jit(solution)/shard_map/ppermute | solution.py:990
  44.1 8.2 %collective-permute-start.11 = (bf16[752,128]{1,0:T(8,128)(2,1)S(1)}, bf16[752,128]{1,0:T(8,128)(2,1)S(1)}, u32[]{:S(2)}, u32[]{:S(2)}) collective-permute-start(bf16[752,128]{1,0:T(8,128)(2,1)S(1)} %get-tuple-element.99), channel_id=1, source_target_pairs={{0,8},{1,3},{2,10},{3,1},{4,12},{5,7},{6,14},{7,5},{8,0},{9,11},{1... | collective-permute-start | bytes 577544 | tf_op jit(solution)/shard_map/ppermute | solution.py:990
  48.7 8.3 %collective-permute-start.9 = (bf16[512,128]{1,0:T(8,128)(2,1)S(1)}, bf16[512,128]{1,0:T(8,128)(2,1)S(1)}, u32[]{:S(2)}, u32[]{:S(2)}) collective-permute-start(bf16[512,128]{1,0:T(8,128)(2,1)S(1)} %get-tuple-element.91), channel_id=1, source_target_pairs={{0,2},{1,9},{2,0},{3,11},{4,6},{5,13},{6,4},{7,15},{8,10},{9,1},{1... | collective-permute-start | bytes 393224 | tf_op jit(solution)/shard_map/ppermute | solution.py:990
  52.3 4.7 %collective-permute-start.12 = (bf16[400,128]{1,0:T(8,128)(2,1)S(1)}, bf16[400,128]{1,0:T(8,128)(2,1)S(1)}, u32[]{:S(2)}, u32[]{:S(2)}) collective-permute-start(bf16[400,128]{1,0:T(8,128)(2,1)S(1)} %get-tuple-element.102), channel_id=1, source_target_pairs={{0,4},{1,9},{2,6},{3,11},{4,0},{5,13},{6,2},{7,15},{8,12},{9,1},{1... | collective-permute-start | bytes 307208 | tf_op jit(solution)/shard_map/ppermute | solution.py:990
  53.9 6.9 %collective-permute-start.15 = (bf16[128,512]{1,0:T(8,128)(2,1)S(1)}, bf16[128,512]{1,0:T(8,128)(2,1)S(1)}, u32[]{:S(2)}, u32[]{:S(2)}) collective-permute-start(bf16[128,512]{1,0:T(8,128)(2,1)S(1)} %get-tuple-element.109), channel_id=1, source_target_pairs={{0,0},{1,8},{2,16},{3,24},{4,4},{5,12},{6,20},{7,28},{8,1},{9,9},{... | collective-permute-start | bytes 393224 | tf_op jit(solution)/shard_map/ppermute | solution.py:990
  57.1 7.5 %collective-permute-start.13 = (f32[256,128]{1,0:T(8,128)S(1)}, f32[256,128]{1,0:T(8,128)S(1)}, u32[]{:S(2)}, u32[]{:S(2)}) collective-permute-start(f32[256,128]{1,0:T(8,128)S(1)} %get-tuple-element.105), channel_id=1, source_target_pairs={{0,8},{1,5},{2,10},{3,7},{4,12},{5,1},{6,14},{7,3},{8,0},{9,13},{1... | collective-permute-start | bytes 393224 | tf_op jit(solution)/shard_map/ppermute | solution.py:990
  59.4 5.1 %collective-permute-start.14 = (f32[192,128]{1,0:T(8,128)S(1)}, f32[192,128]{1,0:T(8,128)S(1)}, u32[]{:S(2)}, u32[]{:S(2)}) collective-permute-start(f32[192,128]{1,0:T(8,128)S(1)} %get-tuple-element.107), channel_id=1, source_target_pairs={{0,2},{1,5},{2,0},{3,7},{4,6},{5,1},{6,4},{7,3},{8,10},{9,13},{10,... | collective-permute-start | bytes 294920 | tf_op jit(solution)/shard_map/ppermute | solution.py:990
  64.6 10.5 %collective-permute-start.16 = (bf16[656,128]{1,0:T(8,128)(2,1)S(1)}, bf16[656,128]{1,0:T(8,128)(2,1)S(1)}, u32[]{:S(2)}, u32[]{:S(2)}) collective-permute-start(bf16[656,128]{1,0:T(8,128)(2,1)S(1)} %get-tuple-element.110.own_ref), channel_id=1, source_target_pairs={{0,16},{1,17},{2,18},{3,19},{4,20},{5,21},{6,22},{7,23},{8,24},{9,... | collective-permute-start | bytes 503816 | tf_op jit(solution)/shard_map/ppermute | solution.py:990
  66.6 11.1 %collective-permute-start.21 = (bf16[8,8,512]{2,1,0:T(8,128)(2,1)S(1)}, bf16[8,8,512]{2,1,0:T(8,128)(2,1)S(1)}, u32[]{:S(2)}, u32[]{:S(2)}) collective-permute-start(bf16[8,8,512]{2,1,0:T(8,128)(2,1)S(1)} %shard_map.207.refs_0_), channel_id=1, source_target_pairs={{0,16},{1,17},{2,18},{3,19},{4,20},{5,21},{6,22},{7,23},{8,24},{9,... | collective-permute-start | bytes 196616 | tf_op jit(solution)/shard_map/ppermute | solution.py:990
  75.2 4.7 %collective-permute-start.17 = (bf16[256,128]{1,0:T(8,128)(2,1)S(1)}, bf16[256,128]{1,0:T(8,128)(2,1)S(1)}, u32[]{:S(2)}, u32[]{:S(2)}) collective-permute-start(bf16[256,128]{1,0:T(8,128)(2,1)S(1)} %get-tuple-element.112.refs_0_), channel_id=1, source_target_pairs={{0,8},{1,5},{2,10},{3,7},{4,12},{5,1},{6,14},{7,3},{8,0},{9,13},{1... | collective-permute-start | bytes 196616 | tf_op jit(solution)/shard_map/ppermute | solution.py:990
  75.3 4.5 %collective-permute-start.18 = (bf16[176,128]{1,0:T(8,128)(2,1)S(1)}, bf16[176,128]{1,0:T(8,128)(2,1)S(1)}, u32[]{:S(2)}, u32[]{:S(2)}) collective-permute-start(bf16[176,128]{1,0:T(8,128)(2,1)S(1)} %get-tuple-element.113.refs_2_), channel_id=1, source_target_pairs={{0,2},{1,5},{2,0},{3,7},{4,6},{5,1},{6,4},{7,3},{8,10},{9,13},{10,... | collective-permute-start | bytes 135176 | tf_op jit(solution)/shard_map/ppermute | solution.py:990
  77.7 5.9 %collective-permute-start.22 = (bf16[16,8,512]{2,1,0:T(8,128)(2,1)S(1)}, bf16[16,8,512]{2,1,0:T(8,128)(2,1)S(1)}, u32[]{:S(2)}, u32[]{:S(2)}) collective-permute-start(bf16[16,8,512]{2,1,0:T(8,128)(2,1)S(1)} %shard_map.208), channel_id=1, source_target_pairs={{0,8},{1,9},{2,10},{3,11},{4,12},{5,13},{6,14},{7,15},{8,0},{9,1},... | collective-permute-start | bytes 393224 | tf_op jit(solution)/shard_map/ppermute | solution.py:990
  80.0 6.6 %collective-permute-start.19 = (bf16[512,128]{1,0:T(8,128)(2,1)S(1)}, bf16[512,128]{1,0:T(8,128)(2,1)S(1)}, u32[]{:S(2)}, u32[]{:S(2)}) collective-permute-start(bf16[512,128]{1,0:T(8,128)(2,1)S(1)} %get-tuple-element.114.refs_0_), channel_id=1, source_target_pairs={{0,2},{1,9},{2,0},{3,11},{4,6},{5,13},{6,4},{7,15},{8,10},{9,1},{1... | collective-permute-start | bytes 393224 | tf_op jit(solution)/shard_map/ppermute | solution.py:990
  82.0 4.5 %collective-permute-start.20 = (bf16[352,128]{1,0:T(8,128)(2,1)S(1)}, bf16[352,128]{1,0:T(8,128)(2,1)S(1)}, u32[]{:S(2)}, u32[]{:S(2)}) collective-permute-start(bf16[352,128]{1,0:T(8,128)(2,1)S(1)} %get-tuple-element.115.refs_2_), channel_id=1, source_target_pairs={{0,4},{1,9},{2,6},{3,11},{4,0},{5,13},{6,2},{7,15},{8,12},{9,1},{1... | collective-permute-start | bytes 270344 | tf_op jit(solution)/shard_map/ppermute | solution.py:990
  86.6 6.4 %collective-permute-start.23 = (bf16[1024,128]{1,0:T(8,128)(2,1)S(1)}, bf16[1024,128]{1,0:T(8,128)(2,1)S(1)}, u32[]{:S(2)}, u32[]{:S(2)}) collective-permute-start(bf16[1024,128]{1,0:T(8,128)(2,1)S(1)} %get-tuple-element.117.refs_0_), channel_id=1, source_target_pairs={{0,4},{1,3},{2,6},{3,1},{4,0},{5,7},{6,2},{7,5},{8,12},{9,11},{10,... | collective-permute-start | bytes 786440 | tf_op jit(solution)/shard_map/ppermute | solution.py:990
  88.3 5.5 %collective-permute-start.24 = (bf16[704,128]{1,0:T(8,128)(2,1)S(1)}, bf16[704,128]{1,0:T(8,128)(2,1)S(1)}, u32[]{:S(2)}, u32[]{:S(2)}) collective-permute-start(bf16[704,128]{1,0:T(8,128)(2,1)S(1)} %get-tuple-element.118.refs_0_), channel_id=1, source_target_pairs={{0,8},{1,3},{2,10},{3,1},{4,12},{5,7},{6,14},{7,5},{8,0},{9,11},{1... | collective-permute-start | bytes 540680 | tf_op jit(solution)/shard_map/ppermute | solution.py:990
  93.1 2.5 %collective-permute-start.25 = (bf16[2048,128]{1,0:T(8,128)(2,1)S(1)}, bf16[2048,128]{1,0:T(8,128)(2,1)S(1)}, u32[]{:S(2)}, u32[]{:S(2)}) collective-permute-start(bf16[2048,128]{1,0:T(8,128)(2,1)S(1)} %shard_map.212.refs_0_), channel_id=1, source_target_pairs={{0,1},{1,0},{2,3},{3,2},{4,5},{5,4},{6,7},{7,6},{8,9},{9,8},{10,11... | collective-permute-start | bytes 1572872 | tf_op jit(solution)/shard_map/ppermute | solution.py:990
  (3 other events, 4.2 us)
